TPU v7x, 32 devices: a whole 2x2x4 slice. The times are simulated.
32 devices in a mesh: grp: 4 (over z), dev: 8 (over y, x, core).
Axes of the slice: x: 2, y: 2, z: 4, core: 2. Of those that a mesh axis runs over, the one named last changes fastest.
Arguments:
- fields: float32 [128, 6, 16, 256], P(('grp', 'dev')), may hold values from 0 to 1
- swap_dev: int32 [32], P(('grp', 'dev')), may hold values from 0 to 1, as said below
- swap_grp: int32 [32], P(('grp', 'dev')), may hold values from 0 to 1, as said below
- neighbors: int32 [128, 6], P(('grp', 'dev')), may hold values from -1 to 127, as said below
- orient: int32 [128], P(('grp', 'dev')), may hold values from 0 to 7
Outputs:
- advanced: float32 [128, 6, 16, 256], P(('grp', 'dev'))
Inputs may be any that keep to these rules, and one draw needn't show every extreme that they name: `swap_dev`: equal on devices 2i and 2i+1 of each group. `swap_grp`: equal on the devices of one dev index in groups 2j and 2j+1. `neighbors`: adjacency is mutual: b names n across a face exactly when n names b across the opposite face. Neighbours across -x and -y lie on the same device or the previous dev index of the same group, across +x and +y on the same device or the next dev index of the same group; across -z and +z on the same dev index of the previous and the next group.
All inputs are finite; a program needn't handle non-finite values.
Results may differ from a plain program's by a relative error of at most 0.0001.
Values sent between devices are 32-bit elements; how exact they have to be, the bound alone decides.
No kernel may reach another device: no remote copies, remote signals or barrier semaphores. Data moves between devices by JAX's collectives and lax.ppermute only.
A program may use at most 64 MiB of HBM per device.

v0:
```python
import math

import jax
import jax.numpy as jnp
from jax import lax
from jax.experimental import pallas as pl
from jax.experimental.pallas import tpu as pltpu
from jax.sharding import PartitionSpec as P

NPHASE = 4
NCONC = 2
NFIELD = NPHASE + NCONC
EDGE = 16
PLANE = EDGE * EDGE
HALF = PLANE // 2
GROUPS = HALF // EDGE
SLOTS = 4
ROWS = NFIELD * SLOTS

phase_rate = 0.05
closure = 0.1
coupling = (0.5, -0.5, 1.0, -1.0)
conc_rates = (0.08, 0.04)

STATE = (2, EDGE * ROWS, HALF)
SPARE = (2, (EDGE + 1) * ROWS, HALF)
FACE = (ROWS, PLANE)
SIDE = (3, ROWS, PLANE)
SOURCES = 4
PARTS = 2
SELECT = (3, 2 * ROWS, PARTS * SOURCES * ROWS)


def partners(axis, offset):
    sizes = (lax.axis_size("grp"), lax.axis_size("dev"))
    along = ("grp", "dev").index(axis)
    route = []
    for grp in range(sizes[0]):
        for dev in range(sizes[1]):
            own = (grp, dev)
            step = 1 if (own[along] - offset) % 2 == 0 else -1
            partner = list(own)
            partner[along] += step
            if not 0 <= partner[along] < sizes[along]:
                partner = list(own)
                partner[1 - along] ^= 1
                if partner[1 - along] >= sizes[1 - along]:
                    partner = list(own)
            route.append((grp * sizes[1] + dev, partner[0] * sizes[1] + partner[1]))
    return route


def exchange(block, axis, offset):
    return lax.ppermute(block, ("grp", "dev"), partners(axis, offset))


def iota(shape, dim):
    return lax.broadcasted_iota(jnp.int32, shape, dim)


def plane_at(ref, x):
    rows = pl.ds(x * ROWS, ROWS)
    return ref[0, rows, :], ref[1, rows, :]


def turned(value, shift):
    shift %= HALF
    return pltpu.roll(value, shift, 1) if shift else value


class Packer:
    def __init__(self):
        lane = iota((ROWS, HALF), 1)
        self.lane, self.group, self.place = lane, lane // EDGE, lane % EDGE
        self.y = [[None, None], [None, None]]
        self.z = [[None, None], [None, None]]

    def add(self, x, left, right):
        odd, half, at = x % 2, x // GROUPS, x % GROUPS
        ends = turned(jnp.where(self.lane < EDGE, left, right), EDGE * at)
        taken = (self.group == at) | (self.group == (at + GROUPS - 1) % GROUPS)
        before = self.y[half][odd]
        self.y[half][odd] = ends if before is None else jnp.where(taken, ends, before)
        at = EDGE - 1 - x
        odd = at % 2
        taken = (self.place == at) | (self.place == (at + EDGE - 1) % EDGE)
        for h, value in enumerate((left, right)):
            moved = turned(value, at)
            before = self.z[h][odd]
            self.z[h][odd] = moved if before is None else jnp.where(taken, moved, before)

    def tables(self, h):
        even_group, even_place = self.group % 2 == 0, self.place % 2 == 0
        (y_even, y_odd), (z_even, z_odd) = self.y[h], self.z[h]
        low = (jnp.where(even_group, y_even, y_odd), jnp.where(even_place, z_even, z_odd))
        y_high, z_high = jnp.where(even_group, y_odd, y_even), jnp.where(even_place, z_odd, z_even)
        return low, (turned(y_high, EDGE), turned(z_high, 1 - EDGE))


def write_tables(packer, state, own):
    low, high = own
    for h in range(2):
        lanes = pl.ds(h * HALF, HALF)
        for ref, x in ((low, 0), (high, EDGE - 1)):
            ref[0, :, lanes] = state[h, pl.ds(x * ROWS, ROWS), :]
        for ref, (y_table, z_table) in zip(own, packer.tables(h)):
            ref[1, :, lanes] = y_table
            ref[2, :, lanes] = z_table


def emit_faces(packer, state, own, sends):
    write_tables(packer, state, own)
    low, high = own
    flat_a, flat_b, deep_a, deep_b = sends
    even = even_place("dev")
    for face in range(2):
        flat_a[face] = jnp.where(even, high[face], low[face])
        flat_b[face] = jnp.where(even, low[face], high[face])
    even = even_place("grp")
    deep_a[...] = jnp.where(even, high[2], low[2])
    deep_b[...] = jnp.where(even, low[2], high[2])


def fill_slot(state, slot, block, first=0, count=EDGE):
    for f in range(NFIELD):
        value = block(f)
        for h in range(2):
            rows = pl.ds(first * ROWS + f * SLOTS + slot, count, stride=ROWS)
            state[h, rows, :] = value[:, h * HALF : (h + 1) * HALF]


def slot_rows():
    return iota(FACE, 0) % SLOTS


def shifted(value, rows):
    rows %= ROWS
    return pltpu.roll(value, rows, 0) if rows else value


def gathered(tables, slot):
    rows = slot_rows()
    out = shifted(tables[0], -slot)
    for number in range(1, len(tables)):
        out = jnp.where(rows == number, shifted(tables[number], number - slot), out)
    return out


def squeezed(table):
    tile = 2 * SLOTS
    rows = iota((tile, PLANE), 0) % SLOTS
    first, second, third = (table[number * tile : (number + 1) * tile] for number in range(3))
    between = jnp.where(rows == 1, pltpu.roll(second, 1, 0), pltpu.roll(second, tile - 1, 0))
    return jnp.concatenate([jnp.where((rows == 1) | (rows == 2), between, first), third], axis=0)


def stretched(value):
    tile = 2 * SLOTS
    rows = iota((tile, PLANE), 0) % SLOTS
    first, third = value[:tile], value[tile:]
    second = jnp.where(rows == 0, pltpu.roll(first, tile - 1, 0), pltpu.roll(first, 1, 0))
    return jnp.concatenate([first, second, third], axis=0)


def scattered(table, number, slot):
    return shifted(table, slot - number)


def even_place(axis):
    return lax.rem(lax.axis_index(axis), 2) == 0


def block_kernel(mask_dev, fields, low, high, to_dev, to_grp):
    last, size = SLOTS - 1, NFIELD * EDGE
    for f in range(NFIELD):
        to_dev[f * EDGE : (f + 1) * EDGE] = fields[last, f]
        to_grp[f * EDGE : (f + 1) * EDGE] = fields[0, f]
    rows, even = slot_rows(), even_place("grp")
    table = jnp.where(rows == 0, jnp.where(even, low[2], high[2]), jnp.where(even, high[2], low[2]))
    to_grp[size : size + ROWS] = jnp.where(rows == SLOTS - 1, mask_dev[...], table)


def faces_kernel(mask_dev, mask_grp, low, high, faces, faces_dev, *outs):
    new_low, new_high, flat_a, flat_b, deep_b = outs
    rows, last = slot_rows(), SLOTS - 1
    first_rows = (rows == 0) & (mask_grp[...] > 0.5)
    last_rows = (rows == last) & (mask_dev[...] > 0.5)
    even = even_place("grp")
    got_first, got_last = faces[:ROWS], faces_dev[:ROWS]
    got_z, got_last_z = stretched(faces[ROWS:]), stretched(faces_dev[ROWS:])
    for side, (raw, new) in enumerate(((low, new_low), (high, new_high))):
        for axis in range(2):
            number = 2 * axis + side
            table = jnp.where(first_rows, scattered(got_first, number, 0), raw[axis])
            new[axis] = jnp.where(last_rows, scattered(got_last, number, last), table)
        table = jnp.where(first_rows & (even if side == 0 else ~even), got_z, raw[2])
        new[2] = jnp.where(last_rows, scattered(got_last_z, side * last, last), table)
    even_dev = even_place("dev")
    for axis in range(2):
        flat_a[axis] = jnp.where(even_dev, new_high[axis], new_low[axis])
        flat_b[axis] = jnp.where(even_dev, new_low[axis], new_high[axis])
    flat_a[2] = got_z
    deep_b[...] = jnp.where(even, new_low[2], new_high[2])


def cos_quarter(number):
    turn = number & 7
    size = jnp.where((turn & 3) == 0, 1.0, jnp.where((turn & 3) == 2, 0.0, math.sqrt(0.5)))
    return jnp.where((turn > 2) & (turn < 6), -size, size)


def plan_kernel(neighbors, orient, scale, select):
    shape = (ROWS, HALF)
    slot, field, column = iota(shape, 0) % SLOTS, iota(shape, 0) // SLOTS, iota(shape, 1)
    grp, dev = lax.axis_index("grp"), lax.axis_index("dev")
    rank = grp * lax.axis_size("dev") + dev

    def by_slot(values):
        rows = values[0]
        for number in range(1, SLOTS):
            rows = jnp.where(slot == number, values[number], rows)
        return rows

    spread = []
    for number in range(SLOTS):
        turn = 0.5 * cos_quarter(orient[number])
        lift = 0.5 * cos_quarter(orient[number] + 6)
        spread.append((1.0 + turn, 1.0 - turn, 1.0 + lift))
    conc = jnp.where(field == NPHASE, conc_rates[0], conc_rates[1])
    weights = [jnp.where(field < NPHASE, phase_rate * by_slot([own[axis] for own in spread]), conc) for axis in range(3)]
    for axis in range(3):
        scale[axis] = weights[axis]
    scale[3] = 1.0 - 2.0 * (weights[0] + weights[1] + weights[2])
    for face in range(6):
        first = []
        came = 2 + lax.rem(lax.rem(dev if face < 4 else grp, 2) + face % 2 + 1, 2)
        for number in range(SLOTS):
            target = neighbors[number, face]
            source = jnp.where(target < 0, face % 2, jnp.where(target // SLOTS == rank, 1 - face % 2, came))
            first.append(source * ROWS + jnp.where(target < 0, number, target & (SLOTS - 1)))
        chosen = jnp.where(column == by_slot(first) + field * SLOTS, 1.0, 0.0)[:, : SOURCES * ROWS]
        rows = pl.ds(face % 2 * ROWS, ROWS)
        for part in range(PARTS):
            select[face // 2, rows, pl.ds(part * SOURCES * ROWS, SOURCES * ROWS)] = chosen


def start_kernel(fields, neighbors, orient, *refs):
    fetched, low, high, faces_grp, faces_dev, scale, select = refs[:7]
    state, near, turn, arrived = refs[7:]
    scalars = ((neighbors, near), (orient, turn))
    parts = [pl.ds(first, EDGE // 2) for first in (0, EDGE // 2)]
    blocks = tuple((fields.at[:, :, part], fetched.at[:, :, part]) for part in parts)
    copies = [pltpu.make_async_copy(*pair, arrived.at[number]) for number, pair in enumerate((*scalars, *blocks))]
    for copy in copies:
        copy.start()
    for copy in copies[: len(scalars)]:
        copy.wait()
    plan_kernel(near, turn, scale, select)
    packer = Packer()
    for number, part in enumerate(parts):
        copies[len(scalars) + number].wait()
        first = number * (EDGE // 2)
        for slot in range(SLOTS):
            fill_slot(state, slot, lambda f: fetched[slot, f, part], first, EDGE // 2)
        for x in range(first, first + EDGE // 2):
            packer.add(x, *plane_at(state, x))
    write_tables(packer, state, (low, high))
    faces_grp[:ROWS] = gathered([low[0], high[0], low[1], high[1]], 0)
    faces_grp[ROWS:] = squeezed(jnp.where(even_place("grp"), high[2], low[2]))
    faces_dev[:ROWS] = gathered([low[0], high[0], low[1], high[1]], SLOTS - 1)
    faces_dev[ROWS:] = squeezed(gathered([low[2], low[2], low[2], high[2]], SLOTS - 1))


def first_inner_kernel(mask_dev, mask_grp, scale, fields, block_dev, block_grp, faces, low, high, new_low, new_high, *refs):
    partial, got_deep, relayed, z_low, z_high, state = refs
    size = NFIELD * EDGE
    swap_dev, swap_grp = mask_dev[...] > 0.5, mask_grp[...] > 0.5

    def block(slot):
        def of(f):
            value = fields[slot, f]
            if slot == 0:
                value = jnp.where(swap_grp[:EDGE], block_grp[f * EDGE : (f + 1) * EDGE], value)
            if slot == SLOTS - 1:
                value = jnp.where(swap_dev[:EDGE], block_dev[f * EDGE : (f + 1) * EDGE], value)
            return value

        return of

    for slot in range(SLOTS):
        fill_slot(state, slot, block(slot))
    rows, even = slot_rows(), even_place("grp")
    first_rows = (rows == 0) & swap_grp
    other = block_grp[size : size + ROWS]
    got = jnp.where((rows == 0) | (rows == SLOTS - 1), stretched(faces[ROWS:]), other)
    got_deep[...] = jnp.where(first_rows, jnp.where(even, low[2], high[2]), got)
    relayed[...] = jnp.where(rows == SLOTS - 1, jnp.broadcast_to(other[SLOTS - 1 : SLOTS], FACE), 0.0)
    z_low[...] = jnp.where(first_rows & ~even, other, new_low[2])
    z_high[...] = jnp.where(first_rows & even, other, new_high[2])
    inner_kernel(state, scale, partial)


def inner_kernel(state, scale, partial):
    lane = iota((ROWS, HALF), 1)
    start_y, end_y = lane < EDGE, lane >= HALF - EDGE
    start_z, end_z = lane % EDGE == 0, lane % EDGE == EDGE - 1
    weight_x, weight_y, weight_z, weight = (scale[number] for number in range(4))
    tile = 2 * SLOTS
    planes = {0: plane_at(state, 0)}
    for x in range(EDGE):
        if x + 1 < EDGE:
            planes[x + 1] = plane_at(state, x + 1)
        left, right = planes[x]
        up = [turned(half, EDGE) for half in (left, right)]
        down = [turned(half, -EDGE) for half in (left, right)]
        sum_y = (
            jnp.where(start_y, 0.0, up[0]) + jnp.where(end_y, down[1], down[0]),
            jnp.where(start_y, up[0], up[1]) + jnp.where(end_y, 0.0, down[1]),
        )
        for h, half in enumerate((left, right)):
            sum_z = jnp.where(start_z, 0.0, turned(half, 1)) + jnp.where(end_z, 0.0, turned(half, -1))
            if x == 0:
                sum_x = planes[1][h]
            elif x == EDGE - 1:
                sum_x = planes[x - 1][h]
            else:
                sum_x = planes[x - 1][h] + planes[x + 1][h]
            flow = weight * half + weight_x * sum_x + weight_y * sum_y[h] + weight_z * sum_z
            phases, conc = (half[:tile], half[tile : 2 * tile]), half[2 * tile :]
            drive = conc - pltpu.roll(conc, SLOTS, 0)
            total = phases[0] + phases[1]
            total = total + pltpu.roll(total, SLOTS, 0)
            tail = (phase_rate * closure) * (1.0 - total)
            rows = x * ROWS
            for number, value in enumerate(phases):
                gain = value * (1.0 - value) * (coupling[2 * number] * drive + (2.0 * value - 1.0))
                part = flow[number * tile : (number + 1) * tile]
                partial[h, pl.ds(rows + number * tile, tile), :] = part + (phase_rate * gain + tail)
            partial[h, pl.ds(rows + 2 * tile, tile), :] = flow[2 * tile :]


def ghosts_of(axis, scale, select, tables):
    tables = jnp.concatenate(tables, axis=0)
    near = tables.astype(jnp.bfloat16)
    rest = (tables - near.astype(jnp.float32)).astype(jnp.bfloat16)
    both = jnp.concatenate([near, rest], axis=0)
    pair = jnp.dot(select[axis].astype(jnp.bfloat16), both, preferred_element_type=jnp.float32)
    weight = jnp.concatenate([scale[axis]] * 2, axis=1)
    return weight * pair[:ROWS], weight * pair[ROWS:]


def side_by_side(low, high, even):
    return jnp.where(even, low, high), jnp.where(even, high, low)


def sides_kernel(scale, select, partial, low, high, flat_a, flat_b, *refs):
    done, blocks = refs[-1], refs[0] if len(refs) > 1 else None
    sources = (low, high, flat_a, flat_b)
    x_low, x_high = ghosts_of(0, scale, select, [ref[0] for ref in sources])
    y_low, y_high = ghosts_of(1, scale, select, [ref[1] for ref in sources])
    lane = iota((ROWS, HALF), 1)
    inside = (lane < EDGE, lane >= HALF - EDGE)
    even = (lane // EDGE) % 2 == 0
    pairs = []
    for h in range(2):
        lanes = slice(h * HALF, (h + 1) * HALF)
        pairs.append(side_by_side(y_low[:, lanes], turned(y_high[:, lanes], -EDGE), even))
    for x in range(EDGE):
        ends = turned(pairs[x // GROUPS][x % 2], -EDGE * (x % GROUPS))
        for h, value in enumerate(plane_at(partial, x)):
            value = value + jnp.where(inside[h], ends, 0.0)
            if x == 0:
                value = value + x_low[:, h * HALF : (h + 1) * HALF]
            if x == EDGE - 1:
                value = value + x_high[:, h * HALF : (h + 1) * HALF]
            done[h, pl.ds(x * ROWS, ROWS), :] = value
    if blocks is not None:
        for slot in range(SLOTS):
            for f in range(NFIELD):
                for h in range(2):
                    rows = pl.ds(f * SLOTS + slot, EDGE, stride=ROWS)
                    blocks[slot, f, :, h * HALF : (h + 1) * HALF] = done[h, rows, :]


def z_pairs(scale, select, tables):
    z_low, z_high = ghosts_of(2, scale, select, tables)
    even = iota((ROWS, HALF), 1) % 2 == 0
    halves = [slice(h * HALF, (h + 1) * HALF) for h in range(2)]
    return [side_by_side(z_low[:, lanes], turned(z_high[:, lanes], EDGE - 1), even) for lanes in halves]


def ends_of(shape):
    place = iota(shape, 1) % EDGE
    return (place == 0) | (place == EDGE - 1)


def finish_kernel(scale, select, partial, known, deep_b, flat_a, relayed, z_low, z_high, done, *outs):
    deep_a = jnp.where(relayed[...] > 0.5, flat_a[2], known[...])
    pairs = z_pairs(scale, select, [z_low[...], z_high[...], deep_a, deep_b[...]])
    ends = ends_of((ROWS, HALF))
    packer = Packer()
    for x in range(EDGE):
        halves, at = [], EDGE - 1 - x
        for h, value in enumerate(plane_at(partial, x)):
            value = value + jnp.where(ends, turned(pairs[h][at % 2], -at), 0.0)
            done[h, pl.ds(x * ROWS, ROWS), :] = value
            halves.append(value)
        packer.add(x, *halves)
    emit_faces(packer, done, outs[0:2], outs[2:6])


def last_kernel(scale, select, partial, low, high, deep_a, deep_b, result, rows_of, blocks, sent):
    for h, pair in enumerate(z_pairs(scale, select, [low[2], high[2], deep_a[...], deep_b[...]])):
        for odd in range(2):
            rows_of[h, odd] = pair[odd]
    shape = (EDGE, HALF)
    ends, even = ends_of(shape), iota(shape, 0) % 2 == 0
    copies = []
    for slot in range(SLOTS):
        for f in range(NFIELD):
            row = pl.ds(f * SLOTS + slot, 1)
            for h in range(2):
                both = [jnp.broadcast_to(rows_of[h, odd, row, :], shape) for odd in (1, 0)]
                ghost = pltpu.roll(jnp.where(even, *both), HALF - EDGE + 1, 1, stride=1, stride_axis=0)
                lanes = pl.ds(h * HALF, HALF)
                blocks[slot, f, :, lanes] = partial[slot, f, :, lanes] + jnp.where(ends, ghost, 0.0)
        copy = pltpu.make_async_copy(blocks.at[slot], result.at[slot], sent.at[slot])
        copy.start()
        copies.append(copy)
    for copy in copies:
        copy.wait()


def spec(space):
    return pl.BlockSpec(memory_space=space)


VECTOR = pltpu.VMEM
SMALL = pltpu.CompilerParams(vmem_limit_bytes=8 << 20)
FLAT = (2, ROWS, PLANE)
TABLES = (STATE, SIDE, SIDE, FLAT, FLAT, FACE, FACE)
EARLY = (ROWS + 4 * SLOTS, PLANE)
TO_DEV = (NFIELD * EDGE, PLANE)
TO_GRP = (NFIELD * EDGE + ROWS, PLANE)


def shaped(shape):
    return jax.ShapeDtypeStruct(shape, jnp.float32)


def cost(flops):
    return pl.CostEstimate(flops=flops, bytes_accessed=min(flops, 2 << 20), transcendentals=0)


def call(kernel, name, shapes, vectors, flops=1 << 20, scratch=()):
    return pl.pallas_call(
        kernel,
        name=name,
        compiler_params=SMALL,
        out_shape=[shaped(shape) for shape in shapes],
        in_specs=[spec(VECTOR)] * len(vectors),
        out_specs=[spec(VECTOR)] * len(shapes),
        scratch_shapes=list(scratch),
        cost_estimate=cost(flops),
    )(*vectors)


def start(arguments):
    shapes = (arguments[0].shape, SIDE, SIDE, EARLY, EARLY, (4, ROWS, HALF), SELECT)
    return pl.pallas_call(
        start_kernel,
        name="start",
        compiler_params=SMALL,
        out_shape=[shaped(shape) for shape in shapes],
        in_specs=[spec(pl.ANY)] * len(arguments),
        out_specs=[spec(VECTOR)] * len(shapes),
        scratch_shapes=[
            pltpu.VMEM(SPARE, jnp.float32),
            *(pltpu.SMEM(array.shape, jnp.int32) for array in arguments[1:]),
            pltpu.SemaphoreType.DMA((len(arguments) + 1,)),
        ],
    )(*(pltpu.with_memory_space_constraint(array, pltpu.HBM) for array in arguments))


def mask(flag):
    return jnp.broadcast_to(jnp.where(flag == 1, 1.0, 0.0).reshape(1, 1), FACE)


def body(fields, swap_dev, swap_grp, neighbors, orient):
    fields, low, high, faces, faces_dev, scale, select = start((fields, neighbors, orient))
    swap_dev, faces = lax.optimization_barrier((swap_dev, faces))
    faces = exchange(faces, "grp", 0)
    faces_dev = exchange(faces_dev, "dev", 0)
    mask_dev = mask(swap_dev)
    to_dev, to_grp = call(block_kernel, "blocks", [TO_DEV, TO_GRP], [mask_dev, fields, low, high], 1 << 28)
    swap_grp, to_grp = lax.optimization_barrier((swap_grp, to_grp))
    mask_grp = mask(swap_grp)
    block_grp = exchange(to_grp, "grp", 0)
    block_dev = exchange(to_dev, "dev", 0)
    new_low, new_high, *sends = call(
        faces_kernel,
        "faces",
        [SIDE, SIDE, SIDE, FLAT, FACE],
        [mask_dev, mask_grp, low, high, faces, faces_dev],
        1 << 28,
    )
    flat_a = exchange(sends[0], "dev", 0)
    flat_b = exchange(sends[1], "dev", 1)
    deep_b = exchange(sends[2], "grp", 1)
    partial, deep_a, relayed, z_low, z_high = call(
        first_inner_kernel,
        "inner_0",
        [STATE, FACE, FACE, FACE, FACE],
        [mask_dev, mask_grp, scale, fields, block_dev, block_grp, faces, low, high, new_low, new_high],
        4 << 20,
        [pltpu.VMEM(SPARE, jnp.float32)],
    )
    (partial,) = call(sides_kernel, "sides_0", [STATE], [scale, select, partial, new_low, new_high, flat_a, flat_b])
    state, *tables = call(
        finish_kernel,
        "finish_0",
        TABLES,
        [scale, select, partial, deep_a, deep_b, flat_a, relayed, z_low, z_high],
    )
    own, sends = tables[:2], tables[2:]
    flat_a = exchange(sends[0], "dev", 0)
    flat_b = exchange(sends[1], "dev", 1)
    deep_a = exchange(sends[2], "grp", 0)
    deep_b = exchange(sends[3], "grp", 1)
    (partial,) = call(inner_kernel, "inner_1", [STATE], [state, scale], 4 << 20)
    (blocks,) = call(
        sides_kernel,
        "sides_1",
        [fields.shape],
        [scale, select, partial, *own, flat_a, flat_b],
        scratch=[pltpu.VMEM(SPARE, jnp.float32)],
    )
    return pl.pallas_call(
        last_kernel,
        name="finish_1",
        compiler_params=SMALL,
        out_shape=shaped(fields.shape),
        in_specs=[spec(VECTOR)] * 7,
        out_specs=spec(pl.ANY),
        scratch_shapes=[
            pltpu.VMEM((2, 2, ROWS, HALF), jnp.float32),
            pltpu.VMEM(fields.shape, jnp.float32),
            pltpu.SemaphoreType.DMA((SLOTS,)),
        ],
    )(scale, select, blocks, *own, deep_a, deep_b)


def solution(mesh):
    in_specs = (
        P(("grp", "dev"), None, None, None),
        P(("grp", "dev")),
        P(("grp", "dev")),
        P(("grp", "dev"), None),
        P(("grp", "dev")),
    )
    out_specs = P(("grp", "dev"), None, None, None)
    return jax.shard_map(body, mesh=mesh, in_specs=in_specs, out_specs=out_specs, check_vma=False)
```

profile of v0, /device:TPU:0, one launch (start us, length us, event | category | flops | bytes accessed | tf_op | source)
XLA Modules:
  0.0 19.4 jit_solution(2113577925223074560)
XLA Ops:
  0.0 1.4 %start.1 = (f32[4,6,16,256]{3,2,1,0:T(8,128)S(1)}, f32[3,24,256]{2,1,0:T(8,128)S(1)}, f32[3,24,256]{2,1,0:T(8,128)S(1)}, f32[40,256]{1,0:T(8,128)S(1)}, f32[40,2...) custom-call(f32[4,6,16,256]{3,2,1,0:T(8,128)} %fields.1, s32[4,6]{1,0:T(4,128)} %neighbors.1, ...), custom_call_target="tpu_custom_call" | custom-call | tf_op jit(solution)/shard_map/start/pallas_call | solution.py:470
  1.4 3.1 %collective-permute-start.2 = (f32[40,256]{1,0:T(8,128)S(1)}, f32[40,256]{1,0:T(8,128)S(1)}, u32[]{:S(2)}, u32[]{:S(2)}) collective-permute-start(f32[40,256]{1,0:T(8,128)S(1)} %get-tuple-element.46), channel_id=1, source_target_pairs={{0,8},{1,9},{2,10},{3,11},{4,12},{5,13},{6,14},{7,15},{8,0},{9,1},... | collective-permute-start | bytes 122888 | tf_op jit(solution)/shard_map/ppermute | solution.py:54
  4.5 0.0 collective-permute-start.3
  5.2 0.1 collective-permute-start.1
  5.4 0.5 %collective-permute-start = (f32[96,256]{1,0:T(8,128)S(1)}, f32[96,256]{1,0:T(8,128)S(1)}, u32[]{:S(2)}, u32[]{:S(2)}) collective-permute-start(f32[96,256]{1,0:T(8,128)S(1)} %get-tuple-element.44), channel_id=1, source_target_pairs={{0,1},{1,0},{2,3},{3,2},{4,5},{5,4},{6,7},{7,6},{8,9},{9,8},{10,11... | collective-permute-start | bytes 294920 | tf_op jit(solution)/shard_map/ppermute | solution.py:54
  6.5 0.0 collective-permute-done.2.faces
  6.5 0.0 collective-permute-done.3.faces_dev
  6.6 0.1 faces.1
  6.6 0.1 collective-permute-start.4
  6.7 2.0 %collective-permute-start.5 = (f32[2,24,256]{2,1,0:T(8,128)S(1)}, f32[2,24,256]{2,1,0:T(8,128)S(1)}, u32[]{:S(2)}, u32[]{:S(2)}) collective-permute-start(f32[2,24,256]{2,1,0:T(8,128)S(1)} %get-tuple-element.52), channel_id=1, source_target_pairs={{0,8},{1,2},{2,1},{3,4},{4,3},{5,6},{6,5},{7,15},{8,0},{9,10},{10,... | collective-permute-start | bytes 147464 | tf_op jit(solution)/shard_map/ppermute | solution.py:54
  8.7 0.0 collective-permute-start.6
  8.8 0.0 collective-permute-done.block_dev
  8.8 2.3 %collective-permute-done.1.block_grp = f32[120,256]{1,0:T(8,128)S(1)} collective-permute-done((f32[120,256]{1,0:T(8,128)S(1)}, f32[120,256]{1,0:T(8,128)S(1)}, u32[]{:S(2)}, u32[]{:S(2)}) %collective-permute-start.1) | collective-permute-done | bytes 122912 | tf_op jit(solution)/shard_map/ppermute | solution.py:54
  11.0 0.5 %inner_0.1 = (f32[2,384,128]{2,1,0:T(8,128)S(1)}, f32[24,256]{1,0:T(8,128)S(1)}, f32[24,256]{1,0:T(8,128)S(1)}, f32[24,256]{1,0:T(8,128)S(1)}, f32[24,256]{1,0:T(8,128)S(1)}) custom-call(f32[24,256]{1,0:T(8,128)S(1)} %broadcast_in_dim.21.mask_dev, f32[24,256]{1,0:T(8,128)S(1)} %broadcast_in_dim.23.mask_grp, f32[4,24,128]{2,1,0:T(8,128)S(1)} %get-tuple-element.35.scale, ...), custom_call_target="tpu_custom_call" | custom-call | flops 4194304 | bytes 2097152 | tf_op jit(solution)/shard_map/inner_0/pallas_call | solution.py:456
  11.6 0.0 collective-permute-done.5.flat_b
  11.6 0.0 collective-permute-done.4.flat_a
  11.6 0.3 %sides_0.1.partial = f32[2,384,128]{2,1,0:T(8,128)S(1)} custom-call(f32[4,24,128]{2,1,0:T(8,128)S(1)} %get-tuple-element.35.scale, f32[3,48,192]{2,1,0:T(8,128)S(1)} %get-tuple-element.36.select, f32[2,384,128]{2,1,0:T(8,128)S(1)} %get-tuple-element.50.partial, f32[3,24,256]{2,1,0:T(8,128)S(1)} %get-tuple-element.48.new_low.low, ...), custom_call_target="tpu_custom_call" | custom-call | flops 1048576 | bytes 1048576 | tf_op jit(solution)/shard_map/sides_0/pallas_call | solution.py:456
  11.9 0.0 collective-permute-done.6.deep_b
  11.9 0.6 %finish_0.1 = (f32[2,384,128]{2,1,0:T(8,128)S(1)}, f32[3,24,256]{2,1,0:T(8,128)S(1)}, f32[3,24,256]{2,1,0:T(8,128)S(1)}, f32[2,24,256]{2,1,0:T(8,128)S(1)}, f32[...) custom-call(f32[4,24,128]{2,1,0:T(8,128)S(1)} %get-tuple-element.35.scale, ...), custom_call_target="tpu_custom_call" | custom-call | flops 1048576 | bytes 1048576 | tf_op jit(solution)/shard_map/finish_0/pallas_call | solution.py:456
  12.5 0.1 collective-permute-start.7
  12.6 1.8 %collective-permute-start.8 = (f32[2,24,256]{2,1,0:T(8,128)S(1)}, f32[2,24,256]{2,1,0:T(8,128)S(1)}, u32[]{:S(2)}, u32[]{:S(2)}) collective-permute-start(f32[2,24,256]{2,1,0:T(8,128)S(1)} %get-tuple-element.62), channel_id=1, source_target_pairs={{0,8},{1,2},{2,1},{3,4},{4,3},{5,6},{6,5},{7,15},{8,0},{9,10},{10,... | collective-permute-start | bytes 147464 | tf_op jit(solution)/shard_map/ppermute | solution.py:54
  14.4 0.3 %collective-permute-start.9 = (f32[24,256]{1,0:T(8,128)S(1)}, f32[24,256]{1,0:T(8,128)S(1)}, u32[]{:S(2)}, u32[]{:S(2)}) collective-permute-start(f32[24,256]{1,0:T(8,128)S(1)} %get-tuple-element.63), channel_id=1, source_target_pairs={{0,8},{1,9},{2,10},{3,11},{4,12},{5,13},{6,14},{7,15},{8,0},{9,1},... | collective-permute-start | bytes 73736 | tf_op jit(solution)/shard_map/ppermute | solution.py:54
  14.7 1.2 %collective-permute-start.10 = (f32[24,256]{1,0:T(8,128)S(1)}, f32[24,256]{1,0:T(8,128)S(1)}, u32[]{:S(2)}, u32[]{:S(2)}) collective-permute-start(f32[24,256]{1,0:T(8,128)S(1)} %get-tuple-element.64), channel_id=1, source_target_pairs={{0,1},{1,0},{2,3},{3,2},{4,5},{5,4},{6,7},{7,6},{8,16},{9,17},{10,... | collective-permute-start | bytes 73736 | tf_op jit(solution)/shard_map/ppermute | solution.py:54
  15.9 0.5 %inner_1.1.partial = f32[2,384,128]{2,1,0:T(8,128)S(1)} custom-call(f32[2,384,128]{2,1,0:T(8,128)S(1)} %get-tuple-element.58.state, f32[4,24,128]{2,1,0:T(8,128)S(1)} %get-tuple-element.35.scale), custom_call_target="tpu_custom_call" | custom-call | flops 4194304 | bytes 2097152 | tf_op jit(solution)/shard_map/inner_1/pallas_call | solution.py:456
  16.4 0.0 collective-permute-done.7.flat_a
  16.4 0.4 %collective-permute-done.8.flat_b = f32[2,24,256]{2,1,0:T(8,128)S(1)} collective-permute-done((f32[2,24,256]{2,1,0:T(8,128)S(1)}, f32[2,24,256]{2,1,0:T(8,128)S(1)}, u32[]{:S(2)}, u32[]{:S(2)}) %collective-permute-start.8) | collective-permute-done | bytes 49184 | tf_op jit(solution)/shard_map/ppermute | solution.py:54
  16.8 0.4 %sides_1.1.partial = f32[4,6,16,256]{3,2,1,0:T(8,128)S(1)} custom-call(f32[4,24,128]{2,1,0:T(8,128)S(1)} %get-tuple-element.35.scale, f32[3,48,192]{2,1,0:T(8,128)S(1)} %get-tuple-element.36.select, f32[2,384,128]{2,1,0:T(8,128)S(1)} %inner_1.1.partial, f32[3,24,256]{2,1,0:T(8,128)S(1)} %get-tuple-element.59.low, f32[3,24,256]{2,1,0:T(8,128)S(1)} %get-tuple-element.60.high, ...), custom_call_target="tpu_custom_call" | custom-call | flops 1048576 | bytes 1048576 | tf_op jit(solution)/shard_map/sides_1/pallas_call | solution.py:456
  17.1 1.1 %collective-permute-done.9.deep_a = f32[24,256]{1,0:T(8,128)S(1)} collective-permute-done((f32[24,256]{1,0:T(8,128)S(1)}, f32[24,256]{1,0:T(8,128)S(1)}, u32[]{:S(2)}, u32[]{:S(2)}) %collective-permute-start.9) | collective-permute-done | bytes 24608 | tf_op jit(solution)/shard_map/ppermute | solution.py:54
  18.2 0.0 collective-permute-done.10.deep_b
  18.2 1.1 %finish_1.1 = f32[4,6,16,256]{3,2,1,0:T(8,128)} custom-call(f32[4,24,128]{2,1,0:T(8,128)S(1)} %get-tuple-element.35.scale, f32[3,48,192]{2,1,0:T(8,128)S(1)} %get-tuple-element.36.select, f32[4,6,16,256]{3,2,1,0:T(8,128)S(1)} %sides_1.1.partial, f32[3,24,256]{2,1,0:T(8,128)S(1)} %get-tuple-element.59.low, f32[3,24,256]{2,1,0:T(8,128)S(1)} %get-tuple-element.60.high, ...), custom_call_target="tpu_custom_call" | custom-call | tf_op jit(solution)/shard_map/finish_1/pallas_call | solution.py:538
  (3 shorter events, 0.0 us)
Async XLA Ops:
  1.4 5.1 %collective-permute-start.2 = (f32[40,256]{1,0:T(8,128)S(1)}, f32[40,256]{1,0:T(8,128)S(1)}, u32[]{:S(2)}, u32[]{:S(2)}) collective-permute-start(f32[40,256]{1,0:T(8,128)S(1)} %get-tuple-element.46), channel_id=1, source_target_pairs={{0,8},{1,9},{2,10},{3,11},{4,12},{5,13},{6,14},{7,15},{8,0},{9,1},... | collective-permute-start | bytes 122888 | tf_op jit(solution)/shard_map/ppermute | solution.py:54
  4.5 2.0 %collective-permute-start.3 = (f32[40,256]{1,0:T(8,128)S(1)}, f32[40,256]{1,0:T(8,128)S(1)}, u32[]{:S(2)}, u32[]{:S(2)}) collective-permute-start(f32[40,256]{1,0:T(8,128)S(1)} %get-tuple-element.47), channel_id=1, source_target_pairs={{0,1},{1,0},{2,3},{3,2},{4,5},{5,4},{6,7},{7,6},{8,9},{9,8},{10,11... | collective-permute-start | bytes 122888 | tf_op jit(solution)/shard_map/ppermute | solution.py:54
  5.2 5.8 %collective-permute-start.1 = (f32[120,256]{1,0:T(8,128)S(1)}, f32[120,256]{1,0:T(8,128)S(1)}, u32[]{:S(2)}, u32[]{:S(2)}) collective-permute-start(f32[120,256]{1,0:T(8,128)S(1)} %get-tuple-element.45), channel_id=1, source_target_pairs={{0,8},{1,9},{2,10},{3,11},{4,12},{5,13},{6,14},{7,15},{8,0},{9,1},... | collective-permute-start | bytes 368648 | tf_op jit(solution)/shard_map/ppermute | solution.py:54
  5.4 3.4 %collective-permute-start = (f32[96,256]{1,0:T(8,128)S(1)}, f32[96,256]{1,0:T(8,128)S(1)}, u32[]{:S(2)}, u32[]{:S(2)}) collective-permute-start(f32[96,256]{1,0:T(8,128)S(1)} %get-tuple-element.44), channel_id=1, source_target_pairs={{0,1},{1,0},{2,3},{3,2},{4,5},{5,4},{6,7},{7,6},{8,9},{9,8},{10,11... | collective-permute-start | bytes 294920 | tf_op jit(solution)/shard_map/ppermute | solution.py:54
  6.6 5.0 %collective-permute-start.4 = (f32[3,24,256]{2,1,0:T(8,128)S(1)}, f32[3,24,256]{2,1,0:T(8,128)S(1)}, u32[]{:S(2)}, u32[]{:S(2)}) collective-permute-start(f32[3,24,256]{2,1,0:T(8,128)S(1)} %get-tuple-element.51), channel_id=1, source_target_pairs={{0,1},{1,0},{2,3},{3,2},{4,5},{5,4},{6,7},{7,6},{8,9},{9,8},{10,11... | collective-permute-start | bytes 221192 | tf_op jit(solution)/shard_map/ppermute | solution.py:54
  6.7 4.9 %collective-permute-start.5 = (f32[2,24,256]{2,1,0:T(8,128)S(1)}, f32[2,24,256]{2,1,0:T(8,128)S(1)}, u32[]{:S(2)}, u32[]{:S(2)}) collective-permute-start(f32[2,24,256]{2,1,0:T(8,128)S(1)} %get-tuple-element.52), channel_id=1, source_target_pairs={{0,8},{1,2},{2,1},{3,4},{4,3},{5,6},{6,5},{7,15},{8,0},{9,10},{10,... | collective-permute-start | bytes 147464 | tf_op jit(solution)/shard_map/ppermute | solution.py:54
  8.7 3.2 %collective-permute-start.6 = (f32[24,256]{1,0:T(8,128)S(1)}, f32[24,256]{1,0:T(8,128)S(1)}, u32[]{:S(2)}, u32[]{:S(2)}) collective-permute-start(f32[24,256]{1,0:T(8,128)S(1)} %get-tuple-element.54), channel_id=1, source_target_pairs={{0,1},{1,0},{2,3},{3,2},{4,5},{5,4},{6,7},{7,6},{8,16},{9,17},{10,... | collective-permute-start | bytes 73736 | tf_op jit(solution)/shard_map/ppermute | solution.py:54
  12.5 3.9 %collective-permute-start.7 = (f32[2,24,256]{2,1,0:T(8,128)S(1)}, f32[2,24,256]{2,1,0:T(8,128)S(1)}, u32[]{:S(2)}, u32[]{:S(2)}) collective-permute-start(f32[2,24,256]{2,1,0:T(8,128)S(1)} %get-tuple-element.61), channel_id=1, source_target_pairs={{0,1},{1,0},{2,3},{3,2},{4,5},{5,4},{6,7},{7,6},{8,9},{9,8},{10,11... | collective-permute-start | bytes 147464 | tf_op jit(solution)/shard_map/ppermute | solution.py:54
  12.6 4.2 %collective-permute-start.8 = (f32[2,24,256]{2,1,0:T(8,128)S(1)}, f32[2,24,256]{2,1,0:T(8,128)S(1)}, u32[]{:S(2)}, u32[]{:S(2)}) collective-permute-start(f32[2,24,256]{2,1,0:T(8,128)S(1)} %get-tuple-element.62), channel_id=1, source_target_pairs={{0,8},{1,2},{2,1},{3,4},{4,3},{5,6},{6,5},{7,15},{8,0},{9,10},{10,... | collective-permute-start | bytes 147464 | tf_op jit(solution)/shard_map/ppermute | solution.py:54
  14.4 3.8 %collective-permute-start.9 = (f32[24,256]{1,0:T(8,128)S(1)}, f32[24,256]{1,0:T(8,128)S(1)}, u32[]{:S(2)}, u32[]{:S(2)}) collective-permute-start(f32[24,256]{1,0:T(8,128)S(1)} %get-tuple-element.63), channel_id=1, source_target_pairs={{0,8},{1,9},{2,10},{3,11},{4,12},{5,13},{6,14},{7,15},{8,0},{9,1},... | collective-permute-start | bytes 73736 | tf_op jit(solution)/shard_map/ppermute | solution.py:54
  14.7 3.5 %collective-permute-start.10 = (f32[24,256]{1,0:T(8,128)S(1)}, f32[24,256]{1,0:T(8,128)S(1)}, u32[]{:S(2)}, u32[]{:S(2)}) collective-permute-start(f32[24,256]{1,0:T(8,128)S(1)} %get-tuple-element.64), channel_id=1, source_target_pairs={{0,1},{1,0},{2,3},{3,2},{4,5},{5,4},{6,7},{7,6},{8,16},{9,17},{10,... | collective-permute-start | bytes 73736 | tf_op jit(solution)/shard_map/ppermute | solution.py:54
where the time goes:
time: 19.6 us; the launch traced here: 19.4 us
  starting transfers between devices  9.23 us (47%)
  Pallas kernels  4.97 us (25%)
  waiting for transfers between devices  3.73 us (19%)
  between operations  1.44 us (7%)
    ppermute x11, starting transfers between devices, exchange(): return lax.ppermute(block, ('grp', 'dev'), partners(axis, offset))  9.23 us
    ppermute x11, waiting for transfers between devices, exchange(): return lax.ppermute(block, ('grp', 'dev'), partners(axis, offset))  3.73 us
    pallas_call x7, Pallas kernels, call(): pl.pallas_call(kernel, name=name, compiler_params=SMALL, out_shape=[shape...  2.39 us
    pallas_call x1, Pallas kernels, start(): pl.pallas_call(start_kernel, name='start', compiler_params=SMALL, out_sha...  1.43 us
    pallas_call x1, Pallas kernels, body(): pl.pallas_call(last_kernel, name='finish_1', compiler_params=SMALL, out_s...  1.15 us
  transfers between devices with their start and end apart: 11, of which 3 were waited for; matrix products, arithmetic and copies ran while one was open for 0% of the time, Pallas kernels for 9%

commit v1 on v0

--- a/solution.py
+++ b/solution.py
@@ -409,7 +409,7 @@
     emit_faces(packer, done, outs[0:2], outs[2:6])
 
 
-def last_kernel(scale, select, partial, low, high, deep_a, deep_b, result, rows_of, blocks, sent):
+def last_kernel(scale, select, partial, low, high, deep_b, deep_a, result, rows_of, blocks, sent):
     for h, pair in enumerate(z_pairs(scale, select, [low[2], high[2], deep_a[...], deep_b[...]])):
         for odd in range(2):
             rows_of[h, odd] = pair[odd]
@@ -547,7 +547,7 @@
             pltpu.VMEM(fields.shape, jnp.float32),
             pltpu.SemaphoreType.DMA((SLOTS,)),
         ],
-    )(scale, select, blocks, *own, deep_a, deep_b)
+    )(scale, select, blocks, *own, deep_b, deep_a)
 
 
 def solution(mesh):

time: 19.6 us -> 20.2 us (1.031)
  starting transfers between devices: 9.23 us -> 10.4 us
  waiting for transfers between devices: 3.73 us -> 3.15 us
    ppermute x11, starting transfers between devices: 9.23 us -> 10.4 us  [exchange(): return lax.ppermute(block, ('grp', 'dev'), partners(axis, offset))]
    ppermute x11, waiting for transfers between devices: 3.73 us -> 3.15 us  [exchange(): return lax.ppermute(block, ('grp', 'dev'), partners(axis, offset))]
  transfers between devices with their start and end apart: 11 -> 11, of which waited for: 3 -> 2; matrix products, arithmetic and copies ran while one was open for 0% -> 0% of each run, Pallas kernels for 9% -> 9%
where the time goes in v1:
time: 20.2 us; the launch traced here: 20 us
  starting transfers between devices  10.4 us (51%)
  Pallas kernels  4.97 us (25%)
  waiting for transfers between devices  3.15 us (16%)
  between operations  1.46 us (7%)
    ppermute x11, starting transfers between devices, exchange(): return lax.ppermute(block, ('grp', 'dev'), partners(axis, offset))  10.4 us
    ppermute x11, waiting for transfers between devices, exchange(): return lax.ppermute(block, ('grp', 'dev'), partners(axis, offset))  3.15 us
    pallas_call x7, Pallas kernels, call(): pl.pallas_call(kernel, name=name, compiler_params=SMALL, out_shape=[shape...  2.39 us
    pallas_call x1, Pallas kernels, start(): pl.pallas_call(start_kernel, name='start', compiler_params=SMALL, out_sha...  1.43 us
    pallas_call x1, Pallas kernels, body(): pl.pallas_call(last_kernel, name='finish_1', compiler_params=SMALL, out_s...  1.14 us
  transfers between devices with their start and end apart: 11, of which 2 were waited for; matrix products, arithmetic and copies ran while one was open for 0% of the time, Pallas kernels for 9%

profile of v1, /device:TPU:0, one launch (start us, length us, event | category | flops | bytes accessed | tf_op | source)
XLA Modules:
  0.0 20.0 jit_solution(8936143138580039332)
XLA Ops:
  0.0 1.4 %start.1 = (f32[4,6,16,256]{3,2,1,0:T(8,128)S(1)}, f32[3,24,256]{2,1,0:T(8,128)S(1)}, f32[3,24,256]{2,1,0:T(8,128)S(1)}, f32[40,256]{1,0:T(8,128)S(1)}, f32[40,2...) custom-call(f32[4,6,16,256]{3,2,1,0:T(8,128)} %fields.1, s32[4,6]{1,0:T(4,128)} %neighbors.1, ...), custom_call_target="tpu_custom_call" | custom-call | tf_op jit(solution)/shard_map/start/pallas_call | solution.py:470
  1.4 3.1 %collective-permute-start.2 = (f32[40,256]{1,0:T(8,128)S(1)}, f32[40,256]{1,0:T(8,128)S(1)}, u32[]{:S(2)}, u32[]{:S(2)}) collective-permute-start(f32[40,256]{1,0:T(8,128)S(1)} %get-tuple-element.46), channel_id=1, source_target_pairs={{0,8},{1,9},{2,10},{3,11},{4,12},{5,13},{6,14},{7,15},{8,0},{9,1},... | collective-permute-start | bytes 122888 | tf_op jit(solution)/shard_map/ppermute | solution.py:54
  4.5 0.0 collective-permute-start.3
  5.2 0.1 collective-permute-start.1
  5.4 0.5 %collective-permute-start = (f32[96,256]{1,0:T(8,128)S(1)}, f32[96,256]{1,0:T(8,128)S(1)}, u32[]{:S(2)}, u32[]{:S(2)}) collective-permute-start(f32[96,256]{1,0:T(8,128)S(1)} %get-tuple-element.44), channel_id=1, source_target_pairs={{0,1},{1,0},{2,3},{3,2},{4,5},{5,4},{6,7},{7,6},{8,9},{9,8},{10,11... | collective-permute-start | bytes 294920 | tf_op jit(solution)/shard_map/ppermute | solution.py:54
  6.5 0.0 collective-permute-done.2.faces
  6.5 0.0 collective-permute-done.3.faces_dev
  6.6 0.1 faces.1
  6.6 0.1 collective-permute-start.4
  6.7 2.0 %collective-permute-start.5 = (f32[2,24,256]{2,1,0:T(8,128)S(1)}, f32[2,24,256]{2,1,0:T(8,128)S(1)}, u32[]{:S(2)}, u32[]{:S(2)}) collective-permute-start(f32[2,24,256]{2,1,0:T(8,128)S(1)} %get-tuple-element.52), channel_id=1, source_target_pairs={{0,8},{1,2},{2,1},{3,4},{4,3},{5,6},{6,5},{7,15},{8,0},{9,10},{10,... | collective-permute-start | bytes 147464 | tf_op jit(solution)/shard_map/ppermute | solution.py:54
  8.7 0.0 collective-permute-start.6
  8.8 0.0 collective-permute-done.block_dev
  8.8 2.3 %collective-permute-done.1.block_grp = f32[120,256]{1,0:T(8,128)S(1)} collective-permute-done((f32[120,256]{1,0:T(8,128)S(1)}, f32[120,256]{1,0:T(8,128)S(1)}, u32[]{:S(2)}, u32[]{:S(2)}) %collective-permute-start.1) | collective-permute-done | bytes 122912 | tf_op jit(solution)/shard_map/ppermute | solution.py:54
  11.0 0.5 %inner_0.1 = (f32[2,384,128]{2,1,0:T(8,128)S(1)}, f32[24,256]{1,0:T(8,128)S(1)}, f32[24,256]{1,0:T(8,128)S(1)}, f32[24,256]{1,0:T(8,128)S(1)}, f32[24,256]{1,0:T(8,128)S(1)}) custom-call(f32[24,256]{1,0:T(8,128)S(1)} %broadcast_in_dim.21.mask_dev, f32[24,256]{1,0:T(8,128)S(1)} %broadcast_in_dim.23.mask_grp, f32[4,24,128]{2,1,0:T(8,128)S(1)} %get-tuple-element.35.scale, ...), custom_call_target="tpu_custom_call" | custom-call | flops 4194304 | bytes 2097152 | tf_op jit(solution)/shard_map/inner_0/pallas_call | solution.py:456
  11.6 0.0 collective-permute-done.5.flat_b
  11.6 0.0 collective-permute-done.4.flat_a
  11.6 0.3 %sides_0.1.partial = f32[2,384,128]{2,1,0:T(8,128)S(1)} custom-call(f32[4,24,128]{2,1,0:T(8,128)S(1)} %get-tuple-element.35.scale, f32[3,48,192]{2,1,0:T(8,128)S(1)} %get-tuple-element.36.select, f32[2,384,128]{2,1,0:T(8,128)S(1)} %get-tuple-element.50.partial, f32[3,24,256]{2,1,0:T(8,128)S(1)} %get-tuple-element.48.new_low.low, ...), custom_call_target="tpu_custom_call" | custom-call | flops 1048576 | bytes 1048576 | tf_op jit(solution)/shard_map/sides_0/pallas_call | solution.py:456
  11.9 0.0 collective-permute-done.6.deep_b
  11.9 0.6 %finish_0.1 = (f32[2,384,128]{2,1,0:T(8,128)S(1)}, f32[3,24,256]{2,1,0:T(8,128)S(1)}, f32[3,24,256]{2,1,0:T(8,128)S(1)}, f32[2,24,256]{2,1,0:T(8,128)S(1)}, f32[...) custom-call(f32[4,24,128]{2,1,0:T(8,128)S(1)} %get-tuple-element.35.scale, ...), custom_call_target="tpu_custom_call" | custom-call | flops 1048576 | bytes 1048576 | tf_op jit(solution)/shard_map/finish_0/pallas_call | solution.py:456
  12.5 0.1 collective-permute-start.7
  12.6 1.8 %collective-permute-start.8 = (f32[2,24,256]{2,1,0:T(8,128)S(1)}, f32[2,24,256]{2,1,0:T(8,128)S(1)}, u32[]{:S(2)}, u32[]{:S(2)}) collective-permute-start(f32[2,24,256]{2,1,0:T(8,128)S(1)} %get-tuple-element.62), channel_id=1, source_target_pairs={{0,8},{1,2},{2,1},{3,4},{4,3},{5,6},{6,5},{7,15},{8,0},{9,10},{10,... | collective-permute-start | bytes 147464 | tf_op jit(solution)/shard_map/ppermute | solution.py:54
  14.4 0.2 collective-permute-start.9
  14.6 2.5 %collective-permute-start.10 = (f32[24,256]{1,0:T(8,128)S(1)}, f32[24,256]{1,0:T(8,128)S(1)}, u32[]{:S(2)}, u32[]{:S(2)}) collective-permute-start(f32[24,256]{1,0:T(8,128)S(1)} %get-tuple-element.64), channel_id=1, source_target_pairs={{0,8},{1,9},{2,10},{3,11},{4,12},{5,13},{6,14},{7,15},{8,0},{9,1},... | collective-permute-start | bytes 73736 | tf_op jit(solution)/shard_map/ppermute | solution.py:54
  17.1 0.5 %inner_1.1.partial = f32[2,384,128]{2,1,0:T(8,128)S(1)} custom-call(f32[2,384,128]{2,1,0:T(8,128)S(1)} %get-tuple-element.58.state, f32[4,24,128]{2,1,0:T(8,128)S(1)} %get-tuple-element.35.scale), custom_call_target="tpu_custom_call" | custom-call | flops 4194304 | bytes 2097152 | tf_op jit(solution)/shard_map/inner_1/pallas_call | solution.py:456
  17.6 0.0 collective-permute-done.7.flat_a
  17.6 0.0 collective-permute-done.8.flat_b
  17.6 0.4 %sides_1.1.partial = f32[4,6,16,256]{3,2,1,0:T(8,128)S(1)} custom-call(f32[4,24,128]{2,1,0:T(8,128)S(1)} %get-tuple-element.35.scale, f32[3,48,192]{2,1,0:T(8,128)S(1)} %get-tuple-element.36.select, f32[2,384,128]{2,1,0:T(8,128)S(1)} %inner_1.1.partial, f32[3,24,256]{2,1,0:T(8,128)S(1)} %get-tuple-element.59.low, f32[3,24,256]{2,1,0:T(8,128)S(1)} %get-tuple-element.60.high, ...), custom_call_target="tpu_custom_call" | custom-call | flops 1048576 | bytes 1048576 | tf_op jit(solution)/shard_map/sides_1/pallas_call | solution.py:456
  18.0 0.0 collective-permute-done.9.deep_b
  18.0 0.9 %collective-permute-done.10.deep_a = f32[24,256]{1,0:T(8,128)S(1)} collective-permute-done((f32[24,256]{1,0:T(8,128)S(1)}, f32[24,256]{1,0:T(8,128)S(1)}, u32[]{:S(2)}, u32[]{:S(2)}) %collective-permute-start.10) | collective-permute-done | bytes 24608 | tf_op jit(solution)/shard_map/ppermute | solution.py:54
  18.9 1.1 %finish_1.1 = f32[4,6,16,256]{3,2,1,0:T(8,128)} custom-call(f32[4,24,128]{2,1,0:T(8,128)S(1)} %get-tuple-element.35.scale, f32[3,48,192]{2,1,0:T(8,128)S(1)} %get-tuple-element.36.select, f32[4,6,16,256]{3,2,1,0:T(8,128)S(1)} %sides_1.1.partial, f32[3,24,256]{2,1,0:T(8,128)S(1)} %get-tuple-element.59.low, f32[3,24,256]{2,1,0:T(8,128)S(1)} %get-tuple-element.60.high, ...), custom_call_target="tpu_custom_call" | custom-call | tf_op jit(solution)/shard_map/finish_1/pallas_call | solution.py:538
  (3 shorter events, 0.0 us)
Async XLA Ops:
  1.4 5.1 %collective-permute-start.2 = (f32[40,256]{1,0:T(8,128)S(1)}, f32[40,256]{1,0:T(8,128)S(1)}, u32[]{:S(2)}, u32[]{:S(2)}) collective-permute-start(f32[40,256]{1,0:T(8,128)S(1)} %get-tuple-element.46), channel_id=1, source_target_pairs={{0,8},{1,9},{2,10},{3,11},{4,12},{5,13},{6,14},{7,15},{8,0},{9,1},... | collective-permute-start | bytes 122888 | tf_op jit(solution)/shard_map/ppermute | solution.py:54
  4.5 2.0 %collective-permute-start.3 = (f32[40,256]{1,0:T(8,128)S(1)}, f32[40,256]{1,0:T(8,128)S(1)}, u32[]{:S(2)}, u32[]{:S(2)}) collective-permute-start(f32[40,256]{1,0:T(8,128)S(1)} %get-tuple-element.47), channel_id=1, source_target_pairs={{0,1},{1,0},{2,3},{3,2},{4,5},{5,4},{6,7},{7,6},{8,9},{9,8},{10,11... | collective-permute-start | bytes 122888 | tf_op jit(solution)/shard_map/ppermute | solution.py:54
  5.2 5.8 %collective-permute-start.1 = (f32[120,256]{1,0:T(8,128)S(1)}, f32[120,256]{1,0:T(8,128)S(1)}, u32[]{:S(2)}, u32[]{:S(2)}) collective-permute-start(f32[120,256]{1,0:T(8,128)S(1)} %get-tuple-element.45), channel_id=1, source_target_pairs={{0,8},{1,9},{2,10},{3,11},{4,12},{5,13},{6,14},{7,15},{8,0},{9,1},... | collective-permute-start | bytes 368648 | tf_op jit(solution)/shard_map/ppermute | solution.py:54
  5.4 3.4 %collective-permute-start = (f32[96,256]{1,0:T(8,128)S(1)}, f32[96,256]{1,0:T(8,128)S(1)}, u32[]{:S(2)}, u32[]{:S(2)}) collective-permute-start(f32[96,256]{1,0:T(8,128)S(1)} %get-tuple-element.44), channel_id=1, source_target_pairs={{0,1},{1,0},{2,3},{3,2},{4,5},{5,4},{6,7},{7,6},{8,9},{9,8},{10,11... | collective-permute-start | bytes 294920 | tf_op jit(solution)/shard_map/ppermute | solution.py:54
  6.6 5.0 %collective-permute-start.4 = (f32[3,24,256]{2,1,0:T(8,128)S(1)}, f32[3,24,256]{2,1,0:T(8,128)S(1)}, u32[]{:S(2)}, u32[]{:S(2)}) collective-permute-start(f32[3,24,256]{2,1,0:T(8,128)S(1)} %get-tuple-element.51), channel_id=1, source_target_pairs={{0,1},{1,0},{2,3},{3,2},{4,5},{5,4},{6,7},{7,6},{8,9},{9,8},{10,11... | collective-permute-start | bytes 221192 | tf_op jit(solution)/shard_map/ppermute | solution.py:54
  6.7 4.9 %collective-permute-start.5 = (f32[2,24,256]{2,1,0:T(8,128)S(1)}, f32[2,24,256]{2,1,0:T(8,128)S(1)}, u32[]{:S(2)}, u32[]{:S(2)}) collective-permute-start(f32[2,24,256]{2,1,0:T(8,128)S(1)} %get-tuple-element.52), channel_id=1, source_target_pairs={{0,8},{1,2},{2,1},{3,4},{4,3},{5,6},{6,5},{7,15},{8,0},{9,10},{10,... | collective-permute-start | bytes 147464 | tf_op jit(solution)/shard_map/ppermute | solution.py:54
  8.7 3.2 %collective-permute-start.6 = (f32[24,256]{1,0:T(8,128)S(1)}, f32[24,256]{1,0:T(8,128)S(1)}, u32[]{:S(2)}, u32[]{:S(2)}) collective-permute-start(f32[24,256]{1,0:T(8,128)S(1)} %get-tuple-element.54), channel_id=1, source_target_pairs={{0,1},{1,0},{2,3},{3,2},{4,5},{5,4},{6,7},{7,6},{8,16},{9,17},{10,... | collective-permute-start | bytes 73736 | tf_op jit(solution)/shard_map/ppermute | solution.py:54
  12.5 5.1 %collective-permute-start.7 = (f32[2,24,256]{2,1,0:T(8,128)S(1)}, f32[2,24,256]{2,1,0:T(8,128)S(1)}, u32[]{:S(2)}, u32[]{:S(2)}) collective-permute-start(f32[2,24,256]{2,1,0:T(8,128)S(1)} %get-tuple-element.61), channel_id=1, source_target_pairs={{0,1},{1,0},{2,3},{3,2},{4,5},{5,4},{6,7},{7,6},{8,9},{9,8},{10,11... | collective-permute-start | bytes 147464 | tf_op jit(solution)/shard_map/ppermute | solution.py:54
  12.6 5.0 %collective-permute-start.8 = (f32[2,24,256]{2,1,0:T(8,128)S(1)}, f32[2,24,256]{2,1,0:T(8,128)S(1)}, u32[]{:S(2)}, u32[]{:S(2)}) collective-permute-start(f32[2,24,256]{2,1,0:T(8,128)S(1)} %get-tuple-element.62), channel_id=1, source_target_pairs={{0,8},{1,2},{2,1},{3,4},{4,3},{5,6},{6,5},{7,15},{8,0},{9,10},{10,... | collective-permute-start | bytes 147464 | tf_op jit(solution)/shard_map/ppermute | solution.py:54
  14.4 3.6 %collective-permute-start.9 = (f32[24,256]{1,0:T(8,128)S(1)}, f32[24,256]{1,0:T(8,128)S(1)}, u32[]{:S(2)}, u32[]{:S(2)}) collective-permute-start(f32[24,256]{1,0:T(8,128)S(1)} %get-tuple-element.63), channel_id=1, source_target_pairs={{0,1},{1,0},{2,3},{3,2},{4,5},{5,4},{6,7},{7,6},{8,16},{9,17},{10,... | collective-permute-start | bytes 73736 | tf_op jit(solution)/shard_map/ppermute | solution.py:54
  14.6 4.3 %collective-permute-start.10 = (f32[24,256]{1,0:T(8,128)S(1)}, f32[24,256]{1,0:T(8,128)S(1)}, u32[]{:S(2)}, u32[]{:S(2)}) collective-permute-start(f32[24,256]{1,0:T(8,128)S(1)} %get-tuple-element.64), channel_id=1, source_target_pairs={{0,8},{1,9},{2,10},{3,11},{4,12},{5,13},{6,14},{7,15},{8,0},{9,1},... | collective-permute-start | bytes 73736 | tf_op jit(solution)/shard_map/ppermute | solution.py:54

commit v2 on v0

--- a/solution.py
+++ b/solution.py
@@ -75,12 +75,14 @@
         self.y = [[None, None], [None, None]]
         self.z = [[None, None], [None, None]]
 
-    def add(self, x, left, right):
+    def add_y(self, x, left, right):
         odd, half, at = x % 2, x // GROUPS, x % GROUPS
         ends = turned(jnp.where(self.lane < EDGE, left, right), EDGE * at)
         taken = (self.group == at) | (self.group == (at + GROUPS - 1) % GROUPS)
         before = self.y[half][odd]
         self.y[half][odd] = ends if before is None else jnp.where(taken, ends, before)
+
+    def add_z(self, x, left, right):
         at = EDGE - 1 - x
         odd = at % 2
         taken = (self.place == at) | (self.place == (at + EDGE - 1) % EDGE)
@@ -89,12 +91,13 @@
             before = self.z[h][odd]
             self.z[h][odd] = moved if before is None else jnp.where(taken, moved, before)
 
-    def tables(self, h):
-        even_group, even_place = self.group % 2 == 0, self.place % 2 == 0
-        (y_even, y_odd), (z_even, z_odd) = self.y[h], self.z[h]
-        low = (jnp.where(even_group, y_even, y_odd), jnp.where(even_place, z_even, z_odd))
-        y_high, z_high = jnp.where(even_group, y_odd, y_even), jnp.where(even_place, z_odd, z_even)
-        return low, (turned(y_high, EDGE), turned(z_high, 1 - EDGE))
+    def y_tables(self, h):
+        even, (first, second) = self.group % 2 == 0, self.y[h]
+        return jnp.where(even, first, second), turned(jnp.where(even, second, first), EDGE)
+
+    def z_tables(self, h):
+        even, (first, second) = self.place % 2 == 0, self.z[h]
+        return jnp.where(even, first, second), turned(jnp.where(even, second, first), 1 - EDGE)
 
 
 def write_tables(packer, state, own):
@@ -103,13 +106,11 @@
         lanes = pl.ds(h * HALF, HALF)
         for ref, x in ((low, 0), (high, EDGE - 1)):
             ref[0, :, lanes] = state[h, pl.ds(x * ROWS, ROWS), :]
-        for ref, (y_table, z_table) in zip(own, packer.tables(h)):
-            ref[1, :, lanes] = y_table
-            ref[2, :, lanes] = z_table
-
-
-def emit_faces(packer, state, own, sends):
-    write_tables(packer, state, own)
+        for ref, table in zip(own, packer.y_tables(h)):
+            ref[1, :, lanes] = table
+
+
+def emit_faces(own, sends):
     low, high = own
     flat_a, flat_b, deep_a, deep_b = sends
     even = even_place("dev")
@@ -263,8 +264,12 @@
         for slot in range(SLOTS):
             fill_slot(state, slot, lambda f: fetched[slot, f, part], first, EDGE // 2)
         for x in range(first, first + EDGE // 2):
-            packer.add(x, *plane_at(state, x))
+            packer.add_y(x, *plane_at(state, x))
+            packer.add_z(x, *plane_at(state, x))
     write_tables(packer, state, (low, high))
+    for h in range(2):
+        for ref, table in zip((low, high), packer.z_tables(h)):
+            ref[2, :, h * HALF : (h + 1) * HALF] = table
     faces_grp[:ROWS] = gathered([low[0], high[0], low[1], high[1]], 0)
     faces_grp[ROWS:] = squeezed(jnp.where(even_place("grp"), high[2], low[2]))
     faces_dev[:ROWS] = gathered([low[0], high[0], low[1], high[1]], SLOTS - 1)
@@ -354,7 +359,9 @@
 
 
 def sides_kernel(scale, select, partial, low, high, flat_a, flat_b, *refs):
-    done, blocks = refs[-1], refs[0] if len(refs) > 1 else None
+    first_step = len(refs) == 3
+    done = refs[0] if first_step else refs[1]
+    packer = Packer()
     sources = (low, high, flat_a, flat_b)
     x_low, x_high = ghosts_of(0, scale, select, [ref[0] for ref in sources])
     y_low, y_high = ghosts_of(1, scale, select, [ref[1] for ref in sources])
@@ -367,6 +374,7 @@
         pairs.append(side_by_side(y_low[:, lanes], turned(y_high[:, lanes], -EDGE), even))
     for x in range(EDGE):
         ends = turned(pairs[x // GROUPS][x % 2], -EDGE * (x % GROUPS))
+        halves = []
         for h, value in enumerate(plane_at(partial, x)):
             value = value + jnp.where(inside[h], ends, 0.0)
             if x == 0:
@@ -374,7 +382,15 @@
             if x == EDGE - 1:
                 value = value + x_high[:, h * HALF : (h + 1) * HALF]
             done[h, pl.ds(x * ROWS, ROWS), :] = value
-    if blocks is not None:
+            halves.append(value)
+        if first_step:
+            packer.add_z(x, *halves)
+    if first_step:
+        for h in range(2):
+            for ref, table in zip(refs[1:], packer.z_tables(h)):
+                ref[:, h * HALF : (h + 1) * HALF] = table
+    else:
+        blocks = refs[0]
         for slot in range(SLOTS):
             for f in range(NFIELD):
                 for h in range(2):
@@ -382,8 +398,7 @@
                     blocks[slot, f, :, h * HALF : (h + 1) * HALF] = done[h, rows, :]
 
 
-def z_pairs(scale, select, tables):
-    z_low, z_high = ghosts_of(2, scale, select, tables)
+def z_pairs(z_low, z_high):
     even = iota((ROWS, HALF), 1) % 2 == 0
     halves = [slice(h * HALF, (h + 1) * HALF) for h in range(2)]
     return [side_by_side(z_low[:, lanes], turned(z_high[:, lanes], EDGE - 1), even) for lanes in halves]
@@ -394,9 +409,12 @@
     return (place == 0) | (place == EDGE - 1)
 
 
-def finish_kernel(scale, select, partial, known, deep_b, flat_a, relayed, z_low, z_high, done, *outs):
+def finish_kernel(
+    scale, select, partial, packed_low, packed_high, known, deep_b, flat_a, relayed, z_low, z_high, done, low, high, *sends
+):
     deep_a = jnp.where(relayed[...] > 0.5, flat_a[2], known[...])
-    pairs = z_pairs(scale, select, [z_low[...], z_high[...], deep_a, deep_b[...]])
+    ghosts = ghosts_of(2, scale, select, [z_low[...], z_high[...], deep_a, deep_b[...]])
+    pairs = z_pairs(*ghosts)
     ends = ends_of((ROWS, HALF))
     packer = Packer()
     for x in range(EDGE):
@@ -405,12 +423,15 @@
             value = value + jnp.where(ends, turned(pairs[h][at % 2], -at), 0.0)
             done[h, pl.ds(x * ROWS, ROWS), :] = value
             halves.append(value)
-        packer.add(x, *halves)
-    emit_faces(packer, done, outs[0:2], outs[2:6])
+        packer.add_y(x, *halves)
+    write_tables(packer, done, (low, high))
+    low[2] = packed_low[...] + ghosts[0]
+    high[2] = packed_high[...] + ghosts[1]
+    emit_faces((low, high), sends)
 
 
 def last_kernel(scale, select, partial, low, high, deep_a, deep_b, result, rows_of, blocks, sent):
-    for h, pair in enumerate(z_pairs(scale, select, [low[2], high[2], deep_a[...], deep_b[...]])):
+    for h, pair in enumerate(z_pairs(*ghosts_of(2, scale, select, [low[2], high[2], deep_a[...], deep_b[...]]))):
         for odd in range(2):
             rows_of[h, odd] = pair[odd]
     shape = (EDGE, HALF)
@@ -515,12 +536,17 @@
         4 << 20,
         [pltpu.VMEM(SPARE, jnp.float32)],
     )
-    (partial,) = call(sides_kernel, "sides_0", [STATE], [scale, select, partial, new_low, new_high, flat_a, flat_b])
+    partial, packed_low, packed_high = call(
+        sides_kernel,
+        "sides_0",
+        [STATE, FACE, FACE],
+        [scale, select, partial, new_low, new_high, flat_a, flat_b],
+    )
     state, *tables = call(
         finish_kernel,
         "finish_0",
         TABLES,
-        [scale, select, partial, deep_a, deep_b, flat_a, relayed, z_low, z_high],
+        [scale, select, partial, packed_low, packed_high, deep_a, deep_b, flat_a, relayed, z_low, z_high],
     )
     own, sends = tables[:2], tables[2:]
     flat_a = exchange(sends[0], "dev", 0)

time: 19.6 us -> 19.5 us (level)
  transfers between devices with their start and end apart: 11 -> 11, of which waited for: 3 -> 3; matrix products, arithmetic and copies ran while one was open for 0% -> 0% of each run, Pallas kernels for 9% -> 10%
where the time goes in v2:
time: 19.5 us; the launch traced here: 19.3 us
  starting transfers between devices  9.2 us (47%)
  Pallas kernels  5.08 us (26%)
  waiting for transfers between devices  3.58 us (18%)
  between operations  1.43 us (7%)
    ppermute x11, starting transfers between devices, exchange(): return lax.ppermute(block, ('grp', 'dev'), partners(axis, offset))  9.2 us
    ppermute x11, waiting for transfers between devices, exchange(): return lax.ppermute(block, ('grp', 'dev'), partners(axis, offset))  3.58 us
    pallas_call x7, Pallas kernels, call(): pl.pallas_call(kernel, name=name, compiler_params=SMALL, out_shape=[shape...  2.51 us
    pallas_call x1, Pallas kernels, start(): pl.pallas_call(start_kernel, name='start', compiler_params=SMALL, out_sha...  1.43 us
    pallas_call x1, Pallas kernels, body(): pl.pallas_call(last_kernel, name='finish_1', compiler_params=SMALL, out_s...  1.15 us
  transfers between devices with their start and end apart: 11, of which 3 were waited for; matrix products, arithmetic and copies ran while one was open for 0% of the time, Pallas kernels for 10%

profile of v2, /device:TPU:0, one launch (start us, length us, event | category | flops | bytes accessed | tf_op | source)
XLA Modules:
  0.0 19.3 jit_solution(10688558242462407390)
XLA Ops:
  0.0 1.4 %start.1 = (f32[4,6,16,256]{3,2,1,0:T(8,128)S(1)}, f32[3,24,256]{2,1,0:T(8,128)S(1)}, f32[3,24,256]{2,1,0:T(8,128)S(1)}, f32[40,256]{1,0:T(8,128)S(1)}, f32[40,2...) custom-call(f32[4,6,16,256]{3,2,1,0:T(8,128)} %fields.1, s32[4,6]{1,0:T(4,128)} %neighbors.1, ...), custom_call_target="tpu_custom_call" | custom-call | tf_op jit(solution)/shard_map/start/pallas_call | solution.py:491
  1.4 3.1 %collective-permute-start.2 = (f32[40,256]{1,0:T(8,128)S(1)}, f32[40,256]{1,0:T(8,128)S(1)}, u32[]{:S(2)}, u32[]{:S(2)}) collective-permute-start(f32[40,256]{1,0:T(8,128)S(1)} %get-tuple-element.49), channel_id=1, source_target_pairs={{0,8},{1,9},{2,10},{3,11},{4,12},{5,13},{6,14},{7,15},{8,0},{9,1},... | collective-permute-start | bytes 122888 | tf_op jit(solution)/shard_map/ppermute | solution.py:54
  4.5 0.0 collective-permute-start.3
  5.2 0.1 collective-permute-start.1
  5.4 0.5 %collective-permute-start = (f32[96,256]{1,0:T(8,128)S(1)}, f32[96,256]{1,0:T(8,128)S(1)}, u32[]{:S(2)}, u32[]{:S(2)}) collective-permute-start(f32[96,256]{1,0:T(8,128)S(1)} %get-tuple-element.47), channel_id=1, source_target_pairs={{0,1},{1,0},{2,3},{3,2},{4,5},{5,4},{6,7},{7,6},{8,9},{9,8},{10,11... | collective-permute-start | bytes 294920 | tf_op jit(solution)/shard_map/ppermute | solution.py:54
  6.5 0.0 collective-permute-done.2.faces
  6.5 0.0 collective-permute-done.3.faces_dev
  6.6 0.1 faces.1
  6.6 0.1 collective-permute-start.4
  6.7 2.0 %collective-permute-start.5 = (f32[2,24,256]{2,1,0:T(8,128)S(1)}, f32[2,24,256]{2,1,0:T(8,128)S(1)}, u32[]{:S(2)}, u32[]{:S(2)}) collective-permute-start(f32[2,24,256]{2,1,0:T(8,128)S(1)} %get-tuple-element.55), channel_id=1, source_target_pairs={{0,8},{1,2},{2,1},{3,4},{4,3},{5,6},{6,5},{7,15},{8,0},{9,10},{10,... | collective-permute-start | bytes 147464 | tf_op jit(solution)/shard_map/ppermute | solution.py:54
  8.7 0.0 collective-permute-start.6
  8.8 0.0 collective-permute-done.block_dev
  8.8 2.3 %collective-permute-done.1.block_grp = f32[120,256]{1,0:T(8,128)S(1)} collective-permute-done((f32[120,256]{1,0:T(8,128)S(1)}, f32[120,256]{1,0:T(8,128)S(1)}, u32[]{:S(2)}, u32[]{:S(2)}) %collective-permute-start.1) | collective-permute-done | bytes 122912 | tf_op jit(solution)/shard_map/ppermute | solution.py:54
  11.0 0.5 %inner_0.1 = (f32[2,384,128]{2,1,0:T(8,128)S(1)}, f32[24,256]{1,0:T(8,128)S(1)}, f32[24,256]{1,0:T(8,128)S(1)}, f32[24,256]{1,0:T(8,128)S(1)}, f32[24,256]{1,0:T(8,128)S(1)}) custom-call(f32[24,256]{1,0:T(8,128)S(1)} %broadcast_in_dim.21.mask_dev, f32[24,256]{1,0:T(8,128)S(1)} %broadcast_in_dim.23.mask_grp, f32[4,24,128]{2,1,0:T(8,128)S(1)} %get-tuple-element.38.scale, ...), custom_call_target="tpu_custom_call" | custom-call | flops 4194304 | bytes 2097152 | tf_op jit(solution)/shard_map/inner_0/pallas_call | solution.py:477
  11.6 0.0 collective-permute-done.5.flat_b
  11.6 0.0 collective-permute-done.4.flat_a
  11.6 0.5 %sides_0.1 = (f32[2,384,128]{2,1,0:T(8,128)S(1)}, f32[24,256]{1,0:T(8,128)S(1)}, f32[24,256]{1,0:T(8,128)S(1)}) custom-call(f32[4,24,128]{2,1,0:T(8,128)S(1)} %get-tuple-element.38.scale, f32[3,48,192]{2,1,0:T(8,128)S(1)} %get-tuple-element.39.select, f32[2,384,128]{2,1,0:T(8,128)S(1)} %get-tuple-element.53.partial, ...), custom_call_target="tpu_custom_call" | custom-call | flops 1048576 | bytes 1048576 | tf_op jit(solution)/shard_map/sides_0/pallas_call | solution.py:477
  12.1 0.0 collective-permute-done.6.deep_b
  12.1 0.5 %finish_0.1 = (f32[2,384,128]{2,1,0:T(8,128)S(1)}, f32[3,24,256]{2,1,0:T(8,128)S(1)}, f32[3,24,256]{2,1,0:T(8,128)S(1)}, f32[2,24,256]{2,1,0:T(8,128)S(1)}, f32[...) custom-call(f32[4,24,128]{2,1,0:T(8,128)S(1)} %get-tuple-element.38.scale, ...), custom_call_target="tpu_custom_call" | custom-call | flops 1048576 | bytes 1048576 | tf_op jit(solution)/shard_map/finish_0/pallas_call | solution.py:477
  12.6 0.0 collective-permute-start.7
  12.7 1.6 %collective-permute-start.8 = (f32[2,24,256]{2,1,0:T(8,128)S(1)}, f32[2,24,256]{2,1,0:T(8,128)S(1)}, u32[]{:S(2)}, u32[]{:S(2)}) collective-permute-start(f32[2,24,256]{2,1,0:T(8,128)S(1)} %get-tuple-element.68), channel_id=1, source_target_pairs={{0,8},{1,2},{2,1},{3,4},{4,3},{5,6},{6,5},{7,15},{8,0},{9,10},{10,... | collective-permute-start | bytes 147464 | tf_op jit(solution)/shard_map/ppermute | solution.py:54
  14.3 0.4 %collective-permute-start.9 = (f32[24,256]{1,0:T(8,128)S(1)}, f32[24,256]{1,0:T(8,128)S(1)}, u32[]{:S(2)}, u32[]{:S(2)}) collective-permute-start(f32[24,256]{1,0:T(8,128)S(1)} %get-tuple-element.69), channel_id=1, source_target_pairs={{0,8},{1,9},{2,10},{3,11},{4,12},{5,13},{6,14},{7,15},{8,0},{9,1},... | collective-permute-start | bytes 73736 | tf_op jit(solution)/shard_map/ppermute | solution.py:54
  14.8 1.2 %collective-permute-start.10 = (f32[24,256]{1,0:T(8,128)S(1)}, f32[24,256]{1,0:T(8,128)S(1)}, u32[]{:S(2)}, u32[]{:S(2)}) collective-permute-start(f32[24,256]{1,0:T(8,128)S(1)} %get-tuple-element.70), channel_id=1, source_target_pairs={{0,1},{1,0},{2,3},{3,2},{4,5},{5,4},{6,7},{7,6},{8,16},{9,17},{10,... | collective-permute-start | bytes 73736 | tf_op jit(solution)/shard_map/ppermute | solution.py:54
  16.0 0.5 %inner_1.1.partial = f32[2,384,128]{2,1,0:T(8,128)S(1)} custom-call(f32[2,384,128]{2,1,0:T(8,128)S(1)} %get-tuple-element.64.state, f32[4,24,128]{2,1,0:T(8,128)S(1)} %get-tuple-element.38.scale), custom_call_target="tpu_custom_call" | custom-call | flops 4194304 | bytes 2097152 | tf_op jit(solution)/shard_map/inner_1/pallas_call | solution.py:477
  16.4 0.0 collective-permute-done.7.flat_a
  16.5 0.4 %collective-permute-done.8.flat_b = f32[2,24,256]{2,1,0:T(8,128)S(1)} collective-permute-done((f32[2,24,256]{2,1,0:T(8,128)S(1)}, f32[2,24,256]{2,1,0:T(8,128)S(1)}, u32[]{:S(2)}, u32[]{:S(2)}) %collective-permute-start.8) | collective-permute-done | bytes 49184 | tf_op jit(solution)/shard_map/ppermute | solution.py:54
  16.8 0.4 %sides_1.1.partial = f32[4,6,16,256]{3,2,1,0:T(8,128)S(1)} custom-call(f32[4,24,128]{2,1,0:T(8,128)S(1)} %get-tuple-element.38.scale, f32[3,48,192]{2,1,0:T(8,128)S(1)} %get-tuple-element.39.select, f32[2,384,128]{2,1,0:T(8,128)S(1)} %inner_1.1.partial, f32[3,24,256]{2,1,0:T(8,128)S(1)} %get-tuple-element.65.low, f32[3,24,256]{2,1,0:T(8,128)S(1)} %get-tuple-element.66.high, ...), custom_call_target="tpu_custom_call" | custom-call | flops 1048576 | bytes 1048576 | tf_op jit(solution)/shard_map/sides_1/pallas_call | solution.py:477
  17.2 0.9 %collective-permute-done.9.deep_a = f32[24,256]{1,0:T(8,128)S(1)} collective-permute-done((f32[24,256]{1,0:T(8,128)S(1)}, f32[24,256]{1,0:T(8,128)S(1)}, u32[]{:S(2)}, u32[]{:S(2)}) %collective-permute-start.9) | collective-permute-done | bytes 24608 | tf_op jit(solution)/shard_map/ppermute | solution.py:54
  18.1 0.0 collective-permute-done.10.deep_b
  18.1 1.1 %finish_1.1 = f32[4,6,16,256]{3,2,1,0:T(8,128)} custom-call(f32[4,24,128]{2,1,0:T(8,128)S(1)} %get-tuple-element.38.scale, f32[3,48,192]{2,1,0:T(8,128)S(1)} %get-tuple-element.39.select, f32[4,6,16,256]{3,2,1,0:T(8,128)S(1)} %sides_1.1.partial, f32[3,24,256]{2,1,0:T(8,128)S(1)} %get-tuple-element.65.low, f32[3,24,256]{2,1,0:T(8,128)S(1)} %get-tuple-element.66.high, ...), custom_call_target="tpu_custom_call" | custom-call | tf_op jit(solution)/shard_map/finish_1/pallas_call | solution.py:564
  (3 shorter events, 0.0 us)
Async XLA Ops:
  1.4 5.1 %collective-permute-start.2 = (f32[40,256]{1,0:T(8,128)S(1)}, f32[40,256]{1,0:T(8,128)S(1)}, u32[]{:S(2)}, u32[]{:S(2)}) collective-permute-start(f32[40,256]{1,0:T(8,128)S(1)} %get-tuple-element.49), channel_id=1, source_target_pairs={{0,8},{1,9},{2,10},{3,11},{4,12},{5,13},{6,14},{7,15},{8,0},{9,1},... | collective-permute-start | bytes 122888 | tf_op jit(solution)/shard_map/ppermute | solution.py:54
  4.5 2.0 %collective-permute-start.3 = (f32[40,256]{1,0:T(8,128)S(1)}, f32[40,256]{1,0:T(8,128)S(1)}, u32[]{:S(2)}, u32[]{:S(2)}) collective-permute-start(f32[40,256]{1,0:T(8,128)S(1)} %get-tuple-element.50), channel_id=1, source_target_pairs={{0,1},{1,0},{2,3},{3,2},{4,5},{5,4},{6,7},{7,6},{8,9},{9,8},{10,11... | collective-permute-start | bytes 122888 | tf_op jit(solution)/shard_map/ppermute | solution.py:54
  5.2 5.8 %collective-permute-start.1 = (f32[120,256]{1,0:T(8,128)S(1)}, f32[120,256]{1,0:T(8,128)S(1)}, u32[]{:S(2)}, u32[]{:S(2)}) collective-permute-start(f32[120,256]{1,0:T(8,128)S(1)} %get-tuple-element.48), channel_id=1, source_target_pairs={{0,8},{1,9},{2,10},{3,11},{4,12},{5,13},{6,14},{7,15},{8,0},{9,1},... | collective-permute-start | bytes 368648 | tf_op jit(solution)/shard_map/ppermute | solution.py:54
  5.4 3.4 %collective-permute-start = (f32[96,256]{1,0:T(8,128)S(1)}, f32[96,256]{1,0:T(8,128)S(1)}, u32[]{:S(2)}, u32[]{:S(2)}) collective-permute-start(f32[96,256]{1,0:T(8,128)S(1)} %get-tuple-element.47), channel_id=1, source_target_pairs={{0,1},{1,0},{2,3},{3,2},{4,5},{5,4},{6,7},{7,6},{8,9},{9,8},{10,11... | collective-permute-start | bytes 294920 | tf_op jit(solution)/shard_map/ppermute | solution.py:54
  6.6 5.0 %collective-permute-start.4 = (f32[3,24,256]{2,1,0:T(8,128)S(1)}, f32[3,24,256]{2,1,0:T(8,128)S(1)}, u32[]{:S(2)}, u32[]{:S(2)}) collective-permute-start(f32[3,24,256]{2,1,0:T(8,128)S(1)} %get-tuple-element.54), channel_id=1, source_target_pairs={{0,1},{1,0},{2,3},{3,2},{4,5},{5,4},{6,7},{7,6},{8,9},{9,8},{10,11... | collective-permute-start | bytes 221192 | tf_op jit(solution)/shard_map/ppermute | solution.py:54
  6.7 4.9 %collective-permute-start.5 = (f32[2,24,256]{2,1,0:T(8,128)S(1)}, f32[2,24,256]{2,1,0:T(8,128)S(1)}, u32[]{:S(2)}, u32[]{:S(2)}) collective-permute-start(f32[2,24,256]{2,1,0:T(8,128)S(1)} %get-tuple-element.55), channel_id=1, source_target_pairs={{0,8},{1,2},{2,1},{3,4},{4,3},{5,6},{6,5},{7,15},{8,0},{9,10},{10,... | collective-permute-start | bytes 147464 | tf_op jit(solution)/shard_map/ppermute | solution.py:54
  8.7 3.4 %collective-permute-start.6 = (f32[24,256]{1,0:T(8,128)S(1)}, f32[24,256]{1,0:T(8,128)S(1)}, u32[]{:S(2)}, u32[]{:S(2)}) collective-permute-start(f32[24,256]{1,0:T(8,128)S(1)} %get-tuple-element.60), channel_id=1, source_target_pairs={{0,1},{1,0},{2,3},{3,2},{4,5},{5,4},{6,7},{7,6},{8,16},{9,17},{10,... | collective-permute-start | bytes 73736 | tf_op jit(solution)/shard_map/ppermute | solution.py:54
  12.6 3.8 %collective-permute-start.7 = (f32[2,24,256]{2,1,0:T(8,128)S(1)}, f32[2,24,256]{2,1,0:T(8,128)S(1)}, u32[]{:S(2)}, u32[]{:S(2)}) collective-permute-start(f32[2,24,256]{2,1,0:T(8,128)S(1)} %get-tuple-element.67), channel_id=1, source_target_pairs={{0,1},{1,0},{2,3},{3,2},{4,5},{5,4},{6,7},{7,6},{8,9},{9,8},{10,11... | collective-permute-start | bytes 147464 | tf_op jit(solution)/shard_map/ppermute | solution.py:54
  12.7 4.2 %collective-permute-start.8 = (f32[2,24,256]{2,1,0:T(8,128)S(1)}, f32[2,24,256]{2,1,0:T(8,128)S(1)}, u32[]{:S(2)}, u32[]{:S(2)}) collective-permute-start(f32[2,24,256]{2,1,0:T(8,128)S(1)} %get-tuple-element.68), channel_id=1, source_target_pairs={{0,8},{1,2},{2,1},{3,4},{4,3},{5,6},{6,5},{7,15},{8,0},{9,10},{10,... | collective-permute-start | bytes 147464 | tf_op jit(solution)/shard_map/ppermute | solution.py:54
  14.3 3.8 %collective-permute-start.9 = (f32[24,256]{1,0:T(8,128)S(1)}, f32[24,256]{1,0:T(8,128)S(1)}, u32[]{:S(2)}, u32[]{:S(2)}) collective-permute-start(f32[24,256]{1,0:T(8,128)S(1)} %get-tuple-element.69), channel_id=1, source_target_pairs={{0,8},{1,9},{2,10},{3,11},{4,12},{5,13},{6,14},{7,15},{8,0},{9,1},... | collective-permute-start | bytes 73736 | tf_op jit(solution)/shard_map/ppermute | solution.py:54
  14.8 3.4 %collective-permute-start.10 = (f32[24,256]{1,0:T(8,128)S(1)}, f32[24,256]{1,0:T(8,128)S(1)}, u32[]{:S(2)}, u32[]{:S(2)}) collective-permute-start(f32[24,256]{1,0:T(8,128)S(1)} %get-tuple-element.70), channel_id=1, source_target_pairs={{0,1},{1,0},{2,3},{3,2},{4,5},{5,4},{6,7},{7,6},{8,16},{9,17},{10,... | collective-permute-start | bytes 73736 | tf_op jit(solution)/shard_map/ppermute | solution.py:54

commit v3 on v2

--- a/solution.py
+++ b/solution.py
@@ -31,6 +31,10 @@
 SELECT = (3, 2 * ROWS, PARTS * SOURCES * ROWS)
 
 
+def swapped_order(dev):
+    return dev // 4 % 2 == 1
+
+
 def partners(axis, offset):
     sizes = (lax.axis_size("grp"), lax.axis_size("dev"))
     along = ("grp", "dev").index(axis)
@@ -38,9 +42,9 @@
     for grp in range(sizes[0]):
         for dev in range(sizes[1]):
             own = (grp, dev)
-            step = 1 if (own[along] - offset) % 2 == 0 else -1
+            start = offset(dev) if callable(offset) else offset
             partner = list(own)
-            partner[along] += step
+            partner[along] += 1 if (own[along] - start) % 2 == 0 else -1
             if not 0 <= partner[along] < sizes[along]:
                 partner = list(own)
                 partner[1 - along] ^= 1
@@ -112,14 +116,14 @@
 
 def emit_faces(own, sends):
     low, high = own
-    flat_a, flat_b, deep_a, deep_b = sends
+    flat_a, flat_b, deep_first, deep_second = sends
     even = even_place("dev")
     for face in range(2):
         flat_a[face] = jnp.where(even, high[face], low[face])
         flat_b[face] = jnp.where(even, low[face], high[face])
-    even = even_place("grp")
-    deep_a[...] = jnp.where(even, high[2], low[2])
-    deep_b[...] = jnp.where(even, low[2], high[2])
+    upper = even_place("grp") != swapped_order(lax.axis_index("dev"))
+    deep_first[...] = jnp.where(upper, high[2], low[2])
+    deep_second[...] = jnp.where(upper, low[2], high[2])
 
 
 def fill_slot(state, slot, block, first=0, count=EDGE):
@@ -430,8 +434,10 @@
     emit_faces((low, high), sends)
 
 
-def last_kernel(scale, select, partial, low, high, deep_a, deep_b, result, rows_of, blocks, sent):
-    for h, pair in enumerate(z_pairs(*ghosts_of(2, scale, select, [low[2], high[2], deep_a[...], deep_b[...]]))):
+def last_kernel(scale, select, partial, low, high, deep_first, deep_second, result, rows_of, blocks, sent):
+    first, second, swapped = deep_first[...], deep_second[...], swapped_order(lax.axis_index("dev"))
+    tables = [low[2], high[2], jnp.where(swapped, second, first), jnp.where(swapped, first, second)]
+    for h, pair in enumerate(z_pairs(*ghosts_of(2, scale, select, tables))):
         for odd in range(2):
             rows_of[h, odd] = pair[odd]
     shape = (EDGE, HALF)
@@ -551,8 +557,8 @@
     own, sends = tables[:2], tables[2:]
     flat_a = exchange(sends[0], "dev", 0)
     flat_b = exchange(sends[1], "dev", 1)
-    deep_a = exchange(sends[2], "grp", 0)
-    deep_b = exchange(sends[3], "grp", 1)
+    deep_first = exchange(sends[2], "grp", lambda dev: 1 if swapped_order(dev) else 0)
+    deep_second = exchange(sends[3], "grp", lambda dev: 0 if swapped_order(dev) else 1)
     (partial,) = call(inner_kernel, "inner_1", [STATE], [state, scale], 4 << 20)
     (blocks,) = call(
         sides_kernel,
@@ -573,7 +579,7 @@
             pltpu.VMEM(fields.shape, jnp.float32),
             pltpu.SemaphoreType.DMA((SLOTS,)),
         ],
-    )(scale, select, blocks, *own, deep_a, deep_b)
+    )(scale, select, blocks, *own, deep_first, deep_second)
 
 
 def solution(mesh):

time: 19.5 us -> 19.5 us (level)
  no operation moved by 1% of the time
where the time goes in v3:
time: 19.5 us; the launch traced here: 19.3 us
  starting transfers between devices  9.2 us (47%)
  Pallas kernels  5.09 us (26%)
  waiting for transfers between devices  3.58 us (18%)
  between operations  1.43 us (7%)
    ppermute x11, starting transfers between devices, exchange(): return lax.ppermute(block, ('grp', 'dev'), partners(axis, offset))  9.2 us
    ppermute x11, waiting for transfers between devices, exchange(): return lax.ppermute(block, ('grp', 'dev'), partners(axis, offset))  3.58 us
    pallas_call x7, Pallas kernels, call(): pl.pallas_call(kernel, name=name, compiler_params=SMALL, out_shape=[shape...  2.5 us
    pallas_call x1, Pallas kernels, start(): pl.pallas_call(start_kernel, name='start', compiler_params=SMALL, out_sha...  1.43 us
    pallas_call x1, Pallas kernels, body(): pl.pallas_call(last_kernel, name='finish_1', compiler_params=SMALL, out_s...  1.15 us
  transfers between devices with their start and end apart: 11, of which 3 were waited for; matrix products, arithmetic and copies ran while one was open for 0% of the time, Pallas kernels for 10%

profile of v3, /device:TPU:0, one launch (start us, length us, event | category | flops | bytes accessed | tf_op | source)
XLA Modules:
  0.0 19.3 jit_solution(7976779460632210064)
XLA Ops:
  0.0 1.4 %start.1 = (f32[4,6,16,256]{3,2,1,0:T(8,128)S(1)}, f32[3,24,256]{2,1,0:T(8,128)S(1)}, f32[3,24,256]{2,1,0:T(8,128)S(1)}, f32[40,256]{1,0:T(8,128)S(1)}, f32[40,2...) custom-call(f32[4,6,16,256]{3,2,1,0:T(8,128)} %fields.1, s32[4,6]{1,0:T(4,128)} %neighbors.1, ...), custom_call_target="tpu_custom_call" | custom-call | tf_op jit(solution)/shard_map/start/pallas_call | solution.py:497
  1.4 3.1 %collective-permute-start.2 = (f32[40,256]{1,0:T(8,128)S(1)}, f32[40,256]{1,0:T(8,128)S(1)}, u32[]{:S(2)}, u32[]{:S(2)}) collective-permute-start(f32[40,256]{1,0:T(8,128)S(1)} %get-tuple-element.49), channel_id=1, source_target_pairs={{0,8},{1,9},{2,10},{3,11},{4,12},{5,13},{6,14},{7,15},{8,0},{9,1},... | collective-permute-start | bytes 122888 | tf_op jit(solution)/shard_map/ppermute | solution.py:58
  4.5 0.0 collective-permute-start.3
  5.2 0.1 collective-permute-start.1
  5.4 0.5 %collective-permute-start = (f32[96,256]{1,0:T(8,128)S(1)}, f32[96,256]{1,0:T(8,128)S(1)}, u32[]{:S(2)}, u32[]{:S(2)}) collective-permute-start(f32[96,256]{1,0:T(8,128)S(1)} %get-tuple-element.47), channel_id=1, source_target_pairs={{0,1},{1,0},{2,3},{3,2},{4,5},{5,4},{6,7},{7,6},{8,9},{9,8},{10,11... | collective-permute-start | bytes 294920 | tf_op jit(solution)/shard_map/ppermute | solution.py:58
  6.5 0.0 collective-permute-done.2.faces
  6.5 0.0 collective-permute-done.3.faces_dev
  6.6 0.1 faces.1
  6.6 0.1 collective-permute-start.4
  6.7 2.0 %collective-permute-start.5 = (f32[2,24,256]{2,1,0:T(8,128)S(1)}, f32[2,24,256]{2,1,0:T(8,128)S(1)}, u32[]{:S(2)}, u32[]{:S(2)}) collective-permute-start(f32[2,24,256]{2,1,0:T(8,128)S(1)} %get-tuple-element.55), channel_id=1, source_target_pairs={{0,8},{1,2},{2,1},{3,4},{4,3},{5,6},{6,5},{7,15},{8,0},{9,10},{10,... | collective-permute-start | bytes 147464 | tf_op jit(solution)/shard_map/ppermute | solution.py:58
  8.7 0.0 collective-permute-start.6
  8.8 0.0 collective-permute-done.block_dev
  8.8 2.3 %collective-permute-done.1.block_grp = f32[120,256]{1,0:T(8,128)S(1)} collective-permute-done((f32[120,256]{1,0:T(8,128)S(1)}, f32[120,256]{1,0:T(8,128)S(1)}, u32[]{:S(2)}, u32[]{:S(2)}) %collective-permute-start.1) | collective-permute-done | bytes 122912 | tf_op jit(solution)/shard_map/ppermute | solution.py:58
  11.0 0.5 %inner_0.1 = (f32[2,384,128]{2,1,0:T(8,128)S(1)}, f32[24,256]{1,0:T(8,128)S(1)}, f32[24,256]{1,0:T(8,128)S(1)}, f32[24,256]{1,0:T(8,128)S(1)}, f32[24,256]{1,0:T(8,128)S(1)}) custom-call(f32[24,256]{1,0:T(8,128)S(1)} %broadcast_in_dim.21.mask_dev, f32[24,256]{1,0:T(8,128)S(1)} %broadcast_in_dim.23.mask_grp, f32[4,24,128]{2,1,0:T(8,128)S(1)} %get-tuple-element.38.scale, ...), custom_call_target="tpu_custom_call" | custom-call | flops 4194304 | bytes 2097152 | tf_op jit(solution)/shard_map/inner_0/pallas_call | solution.py:483
  11.6 0.0 collective-permute-done.5.flat_b
  11.6 0.0 collective-permute-done.4.flat_a
  11.6 0.5 %sides_0.1 = (f32[2,384,128]{2,1,0:T(8,128)S(1)}, f32[24,256]{1,0:T(8,128)S(1)}, f32[24,256]{1,0:T(8,128)S(1)}) custom-call(f32[4,24,128]{2,1,0:T(8,128)S(1)} %get-tuple-element.38.scale, f32[3,48,192]{2,1,0:T(8,128)S(1)} %get-tuple-element.39.select, f32[2,384,128]{2,1,0:T(8,128)S(1)} %get-tuple-element.53.partial, ...), custom_call_target="tpu_custom_call" | custom-call | flops 1048576 | bytes 1048576 | tf_op jit(solution)/shard_map/sides_0/pallas_call | solution.py:483
  12.1 0.0 collective-permute-done.6.deep_b
  12.1 0.5 %finish_0.1 = (f32[2,384,128]{2,1,0:T(8,128)S(1)}, f32[3,24,256]{2,1,0:T(8,128)S(1)}, f32[3,24,256]{2,1,0:T(8,128)S(1)}, f32[2,24,256]{2,1,0:T(8,128)S(1)}, f32[...) custom-call(f32[4,24,128]{2,1,0:T(8,128)S(1)} %get-tuple-element.38.scale, ...), custom_call_target="tpu_custom_call" | custom-call | flops 1048576 | bytes 1048576 | tf_op jit(solution)/shard_map/finish_0/pallas_call | solution.py:483
  12.6 0.0 collective-permute-start.7
  12.7 1.6 %collective-permute-start.8 = (f32[2,24,256]{2,1,0:T(8,128)S(1)}, f32[2,24,256]{2,1,0:T(8,128)S(1)}, u32[]{:S(2)}, u32[]{:S(2)}) collective-permute-start(f32[2,24,256]{2,1,0:T(8,128)S(1)} %get-tuple-element.68), channel_id=1, source_target_pairs={{0,8},{1,2},{2,1},{3,4},{4,3},{5,6},{6,5},{7,15},{8,0},{9,10},{10,... | collective-permute-start | bytes 147464 | tf_op jit(solution)/shard_map/ppermute | solution.py:58
  14.3 0.4 %collective-permute-start.9 = (f32[24,256]{1,0:T(8,128)S(1)}, f32[24,256]{1,0:T(8,128)S(1)}, u32[]{:S(2)}, u32[]{:S(2)}) collective-permute-start(f32[24,256]{1,0:T(8,128)S(1)} %get-tuple-element.69), channel_id=1, source_target_pairs={{0,8},{1,9},{2,10},{3,11},{4,5},{5,4},{6,7},{7,6},{8,0},{9,1},{10,... | collective-permute-start | bytes 73736 | tf_op jit(solution)/shard_map/ppermute | solution.py:58
  14.8 1.2 %collective-permute-start.10 = (f32[24,256]{1,0:T(8,128)S(1)}, f32[24,256]{1,0:T(8,128)S(1)}, u32[]{:S(2)}, u32[]{:S(2)}) collective-permute-start(f32[24,256]{1,0:T(8,128)S(1)} %get-tuple-element.70), channel_id=1, source_target_pairs={{0,1},{1,0},{2,3},{3,2},{4,12},{5,13},{6,14},{7,15},{8,16},{9,17},... | collective-permute-start | bytes 73736 | tf_op jit(solution)/shard_map/ppermute | solution.py:58
  16.0 0.5 %inner_1.1.partial = f32[2,384,128]{2,1,0:T(8,128)S(1)} custom-call(f32[2,384,128]{2,1,0:T(8,128)S(1)} %get-tuple-element.64.state, f32[4,24,128]{2,1,0:T(8,128)S(1)} %get-tuple-element.38.scale), custom_call_target="tpu_custom_call" | custom-call | flops 4194304 | bytes 2097152 | tf_op jit(solution)/shard_map/inner_1/pallas_call | solution.py:483
  16.4 0.0 collective-permute-done.7.flat_a
  16.5 0.4 %collective-permute-done.8.flat_b = f32[2,24,256]{2,1,0:T(8,128)S(1)} collective-permute-done((f32[2,24,256]{2,1,0:T(8,128)S(1)}, f32[2,24,256]{2,1,0:T(8,128)S(1)}, u32[]{:S(2)}, u32[]{:S(2)}) %collective-permute-start.8) | collective-permute-done | bytes 49184 | tf_op jit(solution)/shard_map/ppermute | solution.py:58
  16.8 0.4 %sides_1.1.partial = f32[4,6,16,256]{3,2,1,0:T(8,128)S(1)} custom-call(f32[4,24,128]{2,1,0:T(8,128)S(1)} %get-tuple-element.38.scale, f32[3,48,192]{2,1,0:T(8,128)S(1)} %get-tuple-element.39.select, f32[2,384,128]{2,1,0:T(8,128)S(1)} %inner_1.1.partial, f32[3,24,256]{2,1,0:T(8,128)S(1)} %get-tuple-element.65.low, f32[3,24,256]{2,1,0:T(8,128)S(1)} %get-tuple-element.66.high, ...), custom_call_target="tpu_custom_call" | custom-call | flops 1048576 | bytes 1048576 | tf_op jit(solution)/shard_map/sides_1/pallas_call | solution.py:483
  17.2 0.9 %collective-permute-done.9.deep_first = f32[24,256]{1,0:T(8,128)S(1)} collective-permute-done((f32[24,256]{1,0:T(8,128)S(1)}, f32[24,256]{1,0:T(8,128)S(1)}, u32[]{:S(2)}, u32[]{:S(2)}) %collective-permute-start.9) | collective-permute-done | bytes 24608 | tf_op jit(solution)/shard_map/ppermute | solution.py:58
  18.1 0.0 collective-permute-done.10.deep_second
  18.1 1.2 %finish_1.1 = f32[4,6,16,256]{3,2,1,0:T(8,128)} custom-call(f32[4,24,128]{2,1,0:T(8,128)S(1)} %get-tuple-element.38.scale, f32[3,48,192]{2,1,0:T(8,128)S(1)} %get-tuple-element.39.select, f32[4,6,16,256]{3,2,1,0:T(8,128)S(1)} %sides_1.1.partial, f32[3,24,256]{2,1,0:T(8,128)S(1)} %get-tuple-element.65.low, f32[3,24,256]{2,1,0:T(8,128)S(1)} %get-tuple-element.66.high, ...), custom_call_target="tpu_custom_call" | custom-call | tf_op jit(solution)/shard_map/finish_1/pallas_call | solution.py:570
  (3 shorter events, 0.0 us)
Async XLA Ops:
  1.4 5.1 %collective-permute-start.2 = (f32[40,256]{1,0:T(8,128)S(1)}, f32[40,256]{1,0:T(8,128)S(1)}, u32[]{:S(2)}, u32[]{:S(2)}) collective-permute-start(f32[40,256]{1,0:T(8,128)S(1)} %get-tuple-element.49), channel_id=1, source_target_pairs={{0,8},{1,9},{2,10},{3,11},{4,12},{5,13},{6,14},{7,15},{8,0},{9,1},... | collective-permute-start | bytes 122888 | tf_op jit(solution)/shard_map/ppermute | solution.py:58
  4.5 2.0 %collective-permute-start.3 = (f32[40,256]{1,0:T(8,128)S(1)}, f32[40,256]{1,0:T(8,128)S(1)}, u32[]{:S(2)}, u32[]{:S(2)}) collective-permute-start(f32[40,256]{1,0:T(8,128)S(1)} %get-tuple-element.50), channel_id=1, source_target_pairs={{0,1},{1,0},{2,3},{3,2},{4,5},{5,4},{6,7},{7,6},{8,9},{9,8},{10,11... | collective-permute-start | bytes 122888 | tf_op jit(solution)/shard_map/ppermute | solution.py:58
  5.2 5.8 %collective-permute-start.1 = (f32[120,256]{1,0:T(8,128)S(1)}, f32[120,256]{1,0:T(8,128)S(1)}, u32[]{:S(2)}, u32[]{:S(2)}) collective-permute-start(f32[120,256]{1,0:T(8,128)S(1)} %get-tuple-element.48), channel_id=1, source_target_pairs={{0,8},{1,9},{2,10},{3,11},{4,12},{5,13},{6,14},{7,15},{8,0},{9,1},... | collective-permute-start | bytes 368648 | tf_op jit(solution)/shard_map/ppermute | solution.py:58
  5.4 3.4 %collective-permute-start = (f32[96,256]{1,0:T(8,128)S(1)}, f32[96,256]{1,0:T(8,128)S(1)}, u32[]{:S(2)}, u32[]{:S(2)}) collective-permute-start(f32[96,256]{1,0:T(8,128)S(1)} %get-tuple-element.47), channel_id=1, source_target_pairs={{0,1},{1,0},{2,3},{3,2},{4,5},{5,4},{6,7},{7,6},{8,9},{9,8},{10,11... | collective-permute-start | bytes 294920 | tf_op jit(solution)/shard_map/ppermute | solution.py:58
  6.6 5.0 %collective-permute-start.4 = (f32[3,24,256]{2,1,0:T(8,128)S(1)}, f32[3,24,256]{2,1,0:T(8,128)S(1)}, u32[]{:S(2)}, u32[]{:S(2)}) collective-permute-start(f32[3,24,256]{2,1,0:T(8,128)S(1)} %get-tuple-element.54), channel_id=1, source_target_pairs={{0,1},{1,0},{2,3},{3,2},{4,5},{5,4},{6,7},{7,6},{8,9},{9,8},{10,11... | collective-permute-start | bytes 221192 | tf_op jit(solution)/shard_map/ppermute | solution.py:58
  6.7 4.9 %collective-permute-start.5 = (f32[2,24,256]{2,1,0:T(8,128)S(1)}, f32[2,24,256]{2,1,0:T(8,128)S(1)}, u32[]{:S(2)}, u32[]{:S(2)}) collective-permute-start(f32[2,24,256]{2,1,0:T(8,128)S(1)} %get-tuple-element.55), channel_id=1, source_target_pairs={{0,8},{1,2},{2,1},{3,4},{4,3},{5,6},{6,5},{7,15},{8,0},{9,10},{10,... | collective-permute-start | bytes 147464 | tf_op jit(solution)/shard_map/ppermute | solution.py:58
  8.7 3.4 %collective-permute-start.6 = (f32[24,256]{1,0:T(8,128)S(1)}, f32[24,256]{1,0:T(8,128)S(1)}, u32[]{:S(2)}, u32[]{:S(2)}) collective-permute-start(f32[24,256]{1,0:T(8,128)S(1)} %get-tuple-element.60), channel_id=1, source_target_pairs={{0,1},{1,0},{2,3},{3,2},{4,5},{5,4},{6,7},{7,6},{8,16},{9,17},{10,... | collective-permute-start | bytes 73736 | tf_op jit(solution)/shard_map/ppermute | solution.py:58
  12.6 3.8 %collective-permute-start.7 = (f32[2,24,256]{2,1,0:T(8,128)S(1)}, f32[2,24,256]{2,1,0:T(8,128)S(1)}, u32[]{:S(2)}, u32[]{:S(2)}) collective-permute-start(f32[2,24,256]{2,1,0:T(8,128)S(1)} %get-tuple-element.67), channel_id=1, source_target_pairs={{0,1},{1,0},{2,3},{3,2},{4,5},{5,4},{6,7},{7,6},{8,9},{9,8},{10,11... | collective-permute-start | bytes 147464 | tf_op jit(solution)/shard_map/ppermute | solution.py:58
  12.7 4.2 %collective-permute-start.8 = (f32[2,24,256]{2,1,0:T(8,128)S(1)}, f32[2,24,256]{2,1,0:T(8,128)S(1)}, u32[]{:S(2)}, u32[]{:S(2)}) collective-permute-start(f32[2,24,256]{2,1,0:T(8,128)S(1)} %get-tuple-element.68), channel_id=1, source_target_pairs={{0,8},{1,2},{2,1},{3,4},{4,3},{5,6},{6,5},{7,15},{8,0},{9,10},{10,... | collective-permute-start | bytes 147464 | tf_op jit(solution)/shard_map/ppermute | solution.py:58
  14.3 3.8 %collective-permute-start.9 = (f32[24,256]{1,0:T(8,128)S(1)}, f32[24,256]{1,0:T(8,128)S(1)}, u32[]{:S(2)}, u32[]{:S(2)}) collective-permute-start(f32[24,256]{1,0:T(8,128)S(1)} %get-tuple-element.69), channel_id=1, source_target_pairs={{0,8},{1,9},{2,10},{3,11},{4,5},{5,4},{6,7},{7,6},{8,0},{9,1},{10,... | collective-permute-start | bytes 73736 | tf_op jit(solution)/shard_map/ppermute | solution.py:58
  14.8 3.4 %collective-permute-start.10 = (f32[24,256]{1,0:T(8,128)S(1)}, f32[24,256]{1,0:T(8,128)S(1)}, u32[]{:S(2)}, u32[]{:S(2)}) collective-permute-start(f32[24,256]{1,0:T(8,128)S(1)} %get-tuple-element.70), channel_id=1, source_target_pairs={{0,1},{1,0},{2,3},{3,2},{4,12},{5,13},{6,14},{7,15},{8,16},{9,17},... | collective-permute-start | bytes 73736 | tf_op jit(solution)/shard_map/ppermute | solution.py:58

commit v4 on v3

--- a/solution.py
+++ b/solution.py
@@ -28,7 +28,8 @@
 SIDE = (3, ROWS, PLANE)
 SOURCES = 4
 PARTS = 2
-SELECT = (3, 2 * ROWS, PARTS * SOURCES * ROWS)
+SELECT = (2, 2 * ROWS, PARTS * SOURCES * ROWS)
+TURNS = (2, 2 * SLOTS, ROWS, HALF)
 
 
 def swapped_order(dev):
@@ -214,7 +215,7 @@
     return jnp.where((turn > 2) & (turn < 6), -size, size)
 
 
-def plan_kernel(neighbors, orient, scale, select):
+def plan_kernel(neighbors, orient, scale, select, turns):
     shape = (ROWS, HALF)
     slot, field, column = iota(shape, 0) % SLOTS, iota(shape, 0) // SLOTS, iota(shape, 1)
     grp, dev = lax.axis_index("grp"), lax.axis_index("dev")
@@ -236,9 +237,17 @@
     for axis in range(3):
         scale[axis] = weights[axis]
     scale[3] = 1.0 - 2.0 * (weights[0] + weights[1] + weights[2])
-    for face in range(6):
+    for face in range(4, 6):
+        where_from = []
+        for number in range(SLOTS):
+            target = neighbors[number, face]
+            where_from.append(jnp.where(target < 0, 2 * SLOTS - 1, number - (target & (SLOTS - 1)) + SLOTS - 1))
+        rows = by_slot(where_from)
+        for term in range(2 * SLOTS):
+            turns[face - 4, term] = jnp.where(rows == term, weights[2], 0.0)
+    for face in range(4):
         first = []
-        came = 2 + lax.rem(lax.rem(dev if face < 4 else grp, 2) + face % 2 + 1, 2)
+        came = 2 + lax.rem(lax.rem(dev, 2) + face % 2 + 1, 2)
         for number in range(SLOTS):
             target = neighbors[number, face]
             source = jnp.where(target < 0, face % 2, jnp.where(target // SLOTS == rank, 1 - face % 2, came))
@@ -250,8 +259,8 @@
 
 
 def start_kernel(fields, neighbors, orient, *refs):
-    fetched, low, high, faces_grp, faces_dev, scale, select = refs[:7]
-    state, near, turn, arrived = refs[7:]
+    fetched, low, high, faces_grp, faces_dev, scale, select, turns = refs[:8]
+    state, near, turn, arrived = refs[8:]
     scalars = ((neighbors, near), (orient, turn))
     parts = [pl.ds(first, EDGE // 2) for first in (0, EDGE // 2)]
     blocks = tuple((fields.at[:, :, part], fetched.at[:, :, part]) for part in parts)
@@ -260,7 +269,7 @@
         copy.start()
     for copy in copies[: len(scalars)]:
         copy.wait()
-    plan_kernel(near, turn, scale, select)
+    plan_kernel(near, turn, scale, select, turns)
     packer = Packer()
     for number, part in enumerate(parts):
         copies[len(scalars) + number].wait()
@@ -402,6 +411,25 @@
                     blocks[slot, f, :, h * HALF : (h + 1) * HALF] = done[h, rows, :]
 
 
+def z_ghosts(turns, own, deep_a, deep_b):
+    even = even_place("grp")
+    came = (jnp.where(even, deep_b, deep_a), jnp.where(even, deep_a, deep_b))
+    ghosts = []
+    for side in range(2):
+        halves = []
+        for h in range(2):
+            lanes = slice(h * HALF, (h + 1) * HALF)
+            table = came[side][:, lanes].reshape(NFIELD // 2, 2 * SLOTS, HALF)
+            total = turns[side, 2 * SLOTS - 1] * own[side][:, lanes]
+            for term in range(2 * SLOTS - 1):
+                shift = (term - SLOTS + 1) % (2 * SLOTS)
+                moved = pltpu.roll(table, shift, 1) if shift else table
+                total = total + turns[side, term] * moved.reshape(ROWS, HALF)
+            halves.append(total)
+        ghosts.append(jnp.concatenate(halves, axis=1))
+    return ghosts
+
+
 def z_pairs(z_low, z_high):
     even = iota((ROWS, HALF), 1) % 2 == 0
     halves = [slice(h * HALF, (h + 1) * HALF) for h in range(2)]
@@ -414,10 +442,10 @@
 
 
 def finish_kernel(
-    scale, select, partial, packed_low, packed_high, known, deep_b, flat_a, relayed, z_low, z_high, done, low, high, *sends
+    turns, partial, packed_low, packed_high, known, deep_b, flat_a, relayed, z_low, z_high, done, low, high, *sends
 ):
     deep_a = jnp.where(relayed[...] > 0.5, flat_a[2], known[...])
-    ghosts = ghosts_of(2, scale, select, [z_low[...], z_high[...], deep_a, deep_b[...]])
+    ghosts = z_ghosts(turns, (z_low[...], z_high[...]), deep_a, deep_b[...])
     pairs = z_pairs(*ghosts)
     ends = ends_of((ROWS, HALF))
     packer = Packer()
@@ -434,10 +462,10 @@
     emit_faces((low, high), sends)
 
 
-def last_kernel(scale, select, partial, low, high, deep_first, deep_second, result, rows_of, blocks, sent):
+def last_kernel(turns, partial, low, high, deep_first, deep_second, result, rows_of, blocks, sent):
     first, second, swapped = deep_first[...], deep_second[...], swapped_order(lax.axis_index("dev"))
-    tables = [low[2], high[2], jnp.where(swapped, second, first), jnp.where(swapped, first, second)]
-    for h, pair in enumerate(z_pairs(*ghosts_of(2, scale, select, tables))):
+    came = jnp.where(swapped, second, first), jnp.where(swapped, first, second)
+    for h, pair in enumerate(z_pairs(*z_ghosts(turns, (low[2], high[2]), *came))):
         for odd in range(2):
             rows_of[h, odd] = pair[odd]
     shape = (EDGE, HALF)
@@ -493,7 +521,7 @@
 
 
 def start(arguments):
-    shapes = (arguments[0].shape, SIDE, SIDE, EARLY, EARLY, (4, ROWS, HALF), SELECT)
+    shapes = (arguments[0].shape, SIDE, SIDE, EARLY, EARLY, (4, ROWS, HALF), SELECT, TURNS)
     return pl.pallas_call(
         start_kernel,
         name="start",
@@ -514,7 +542,7 @@
 
 
 def body(fields, swap_dev, swap_grp, neighbors, orient):
-    fields, low, high, faces, faces_dev, scale, select = start((fields, neighbors, orient))
+    fields, low, high, faces, faces_dev, scale, select, turns = start((fields, neighbors, orient))
     swap_dev, faces = lax.optimization_barrier((swap_dev, faces))
     faces = exchange(faces, "grp", 0)
     faces_dev = exchange(faces_dev, "dev", 0)
@@ -552,7 +580,7 @@
         finish_kernel,
         "finish_0",
         TABLES,
-        [scale, select, partial, packed_low, packed_high, deep_a, deep_b, flat_a, relayed, z_low, z_high],
+        [turns, partial, packed_low, packed_high, deep_a, deep_b, flat_a, relayed, z_low, z_high],
     )
     own, sends = tables[:2], tables[2:]
     flat_a = exchange(sends[0], "dev", 0)
@@ -572,14 +600,14 @@
         name="finish_1",
         compiler_params=SMALL,
         out_shape=shaped(fields.shape),
-        in_specs=[spec(VECTOR)] * 7,
+        in_specs=[spec(VECTOR)] * 6,
         out_specs=spec(pl.ANY),
         scratch_shapes=[
             pltpu.VMEM((2, 2, ROWS, HALF), jnp.float32),
             pltpu.VMEM(fields.shape, jnp.float32),
             pltpu.SemaphoreType.DMA((SLOTS,)),
         ],
-    )(scale, select, blocks, *own, deep_first, deep_second)
+    )(turns, blocks, *own, deep_first, deep_second)
 
 
 def solution(mesh):

time: 19.5 us -> 19.1 us (0.979)
  Pallas kernels: 5.09 us -> 4.72 us
where the time goes in v4:
time: 19.1 us; the launch traced here: 18.9 us
  starting transfers between devices  9.22 us (48%)
  Pallas kernels  4.72 us (25%)
  waiting for transfers between devices  3.58 us (19%)
  between operations  1.43 us (7%)
    ppermute x11, starting transfers between devices, exchange(): return lax.ppermute(block, ('grp', 'dev'), partners(axis, offset))  9.22 us
    ppermute x11, waiting for transfers between devices, exchange(): return lax.ppermute(block, ('grp', 'dev'), partners(axis, offset))  3.58 us
    pallas_call x7, Pallas kernels, call(): pl.pallas_call(kernel, name=name, compiler_params=SMALL, out_shape=[shape...  2.37 us
    pallas_call x1, Pallas kernels, start(): pl.pallas_call(start_kernel, name='start', compiler_params=SMALL, out_sha...  1.38 us
    pallas_call x1, Pallas kernels, body(): pl.pallas_call(last_kernel, name='finish_1', compiler_params=SMALL, out_s...  0.97 us
  transfers between devices with their start and end apart: 11, of which 3 were waited for; matrix products, arithmetic and copies ran while one was open for 0% of the time, Pallas kernels for 10%

profile of v4, /device:TPU:0, one launch (start us, length us, event | category | flops | bytes accessed | tf_op | source)
XLA Modules:
  0.0 18.9 jit_solution(7054118873017213641)
XLA Ops:
  0.0 1.4 %start.1 = (f32[4,6,16,256]{3,2,1,0:T(8,128)S(1)}, f32[3,24,256]{2,1,0:T(8,128)S(1)}, f32[3,24,256]{2,1,0:T(8,128)S(1)}, f32[40,256]{1,0:T(8,128)S(1)}, f32[40,2...) custom-call(f32[4,6,16,256]{3,2,1,0:T(8,128)} %fields.1, ...), custom_call_target="tpu_custom_call" | custom-call | tf_op jit(solution)/shard_map/start/pallas_call | solution.py:525
  1.4 3.1 %collective-permute-start.2 = (f32[40,256]{1,0:T(8,128)S(1)}, f32[40,256]{1,0:T(8,128)S(1)}, u32[]{:S(2)}, u32[]{:S(2)}) collective-permute-start(f32[40,256]{1,0:T(8,128)S(1)} %get-tuple-element.51), channel_id=1, source_target_pairs={{0,8},{1,9},{2,10},{3,11},{4,12},{5,13},{6,14},{7,15},{8,0},{9,1},... | collective-permute-start | bytes 122888 | tf_op jit(solution)/shard_map/ppermute | solution.py:59
  4.5 0.0 collective-permute-start.3
  5.2 0.1 collective-permute-start.1
  5.3 0.5 %collective-permute-start = (f32[96,256]{1,0:T(8,128)S(1)}, f32[96,256]{1,0:T(8,128)S(1)}, u32[]{:S(2)}, u32[]{:S(2)}) collective-permute-start(f32[96,256]{1,0:T(8,128)S(1)} %get-tuple-element.49), channel_id=1, source_target_pairs={{0,1},{1,0},{2,3},{3,2},{4,5},{5,4},{6,7},{7,6},{8,9},{9,8},{10,11... | collective-permute-start | bytes 294920 | tf_op jit(solution)/shard_map/ppermute | solution.py:59
  6.5 0.0 collective-permute-done.2.faces
  6.5 0.0 collective-permute-done.3.faces_dev
  6.5 0.1 faces.1
  6.6 0.1 collective-permute-start.4
  6.7 2.0 %collective-permute-start.5 = (f32[2,24,256]{2,1,0:T(8,128)S(1)}, f32[2,24,256]{2,1,0:T(8,128)S(1)}, u32[]{:S(2)}, u32[]{:S(2)}) collective-permute-start(f32[2,24,256]{2,1,0:T(8,128)S(1)} %get-tuple-element.57), channel_id=1, source_target_pairs={{0,8},{1,2},{2,1},{3,4},{4,3},{5,6},{6,5},{7,15},{8,0},{9,10},{10,... | collective-permute-start | bytes 147464 | tf_op jit(solution)/shard_map/ppermute | solution.py:59
  8.7 0.0 collective-permute-start.6
  8.7 0.0 collective-permute-done.block_dev
  8.7 2.3 %collective-permute-done.1.block_grp = f32[120,256]{1,0:T(8,128)S(1)} collective-permute-done((f32[120,256]{1,0:T(8,128)S(1)}, f32[120,256]{1,0:T(8,128)S(1)}, u32[]{:S(2)}, u32[]{:S(2)}) %collective-permute-start.1) | collective-permute-done | bytes 122912 | tf_op jit(solution)/shard_map/ppermute | solution.py:59
  11.0 0.5 %inner_0.1 = (f32[2,384,128]{2,1,0:T(8,128)S(1)}, f32[24,256]{1,0:T(8,128)S(1)}, f32[24,256]{1,0:T(8,128)S(1)}, f32[24,256]{1,0:T(8,128)S(1)}, f32[24,256]{1,0:T(8,128)S(1)}) custom-call(f32[24,256]{1,0:T(8,128)S(1)} %broadcast_in_dim.21.mask_dev, f32[24,256]{1,0:T(8,128)S(1)} %broadcast_in_dim.23.mask_grp, f32[4,24,128]{2,1,0:T(8,128)S(1)} %get-tuple-element.40.scale, ...), custom_call_target="tpu_custom_call" | custom-call | flops 4194304 | bytes 2097152 | tf_op jit(solution)/shard_map/inner_0/pallas_call | solution.py:511
  11.5 0.0 collective-permute-done.5.flat_b
  11.5 0.0 collective-permute-done.4.flat_a
  11.5 0.5 %sides_0.1 = (f32[2,384,128]{2,1,0:T(8,128)S(1)}, f32[24,256]{1,0:T(8,128)S(1)}, f32[24,256]{1,0:T(8,128)S(1)}) custom-call(f32[4,24,128]{2,1,0:T(8,128)S(1)} %get-tuple-element.40.scale, f32[2,48,192]{2,1,0:T(8,128)S(1)} %get-tuple-element.41.select, f32[2,384,128]{2,1,0:T(8,128)S(1)} %get-tuple-element.55.partial, ...), custom_call_target="tpu_custom_call" | custom-call | flops 1048576 | bytes 1048576 | tf_op jit(solution)/shard_map/sides_0/pallas_call | solution.py:511
  12.0 0.0 collective-permute-done.6.deep_b
  12.0 0.4 %finish_0.1 = (f32[2,384,128]{2,1,0:T(8,128)S(1)}, f32[3,24,256]{2,1,0:T(8,128)S(1)}, f32[3,24,256]{2,1,0:T(8,128)S(1)}, f32[2,24,256]{2,1,0:T(8,128)S(1)}, f32[...) custom-call(f32[2,8,24,128]{3,2,1,0:T(8,128)S(1)} %get-tuple-element.39.turns, ...), custom_call_target="tpu_custom_call" | custom-call | flops 1048576 | bytes 1048576 | tf_op jit(solution)/shard_map/finish_0/pallas_call | solution.py:511
  12.4 0.0 collective-permute-start.7
  12.5 1.6 %collective-permute-start.8 = (f32[2,24,256]{2,1,0:T(8,128)S(1)}, f32[2,24,256]{2,1,0:T(8,128)S(1)}, u32[]{:S(2)}, u32[]{:S(2)}) collective-permute-start(f32[2,24,256]{2,1,0:T(8,128)S(1)} %get-tuple-element.70), channel_id=1, source_target_pairs={{0,8},{1,2},{2,1},{3,4},{4,3},{5,6},{6,5},{7,15},{8,0},{9,10},{10,... | collective-permute-start | bytes 147464 | tf_op jit(solution)/shard_map/ppermute | solution.py:59
  14.1 0.4 %collective-permute-start.9 = (f32[24,256]{1,0:T(8,128)S(1)}, f32[24,256]{1,0:T(8,128)S(1)}, u32[]{:S(2)}, u32[]{:S(2)}) collective-permute-start(f32[24,256]{1,0:T(8,128)S(1)} %get-tuple-element.71), channel_id=1, source_target_pairs={{0,8},{1,9},{2,10},{3,11},{4,5},{5,4},{6,7},{7,6},{8,0},{9,1},{10,... | collective-permute-start | bytes 73736 | tf_op jit(solution)/shard_map/ppermute | solution.py:59
  14.6 1.2 %collective-permute-start.10 = (f32[24,256]{1,0:T(8,128)S(1)}, f32[24,256]{1,0:T(8,128)S(1)}, u32[]{:S(2)}, u32[]{:S(2)}) collective-permute-start(f32[24,256]{1,0:T(8,128)S(1)} %get-tuple-element.72), channel_id=1, source_target_pairs={{0,1},{1,0},{2,3},{3,2},{4,12},{5,13},{6,14},{7,15},{8,16},{9,17},... | collective-permute-start | bytes 73736 | tf_op jit(solution)/shard_map/ppermute | solution.py:59
  15.8 0.5 %inner_1.1.partial = f32[2,384,128]{2,1,0:T(8,128)S(1)} custom-call(f32[2,384,128]{2,1,0:T(8,128)S(1)} %get-tuple-element.66.state, f32[4,24,128]{2,1,0:T(8,128)S(1)} %get-tuple-element.40.scale), custom_call_target="tpu_custom_call" | custom-call | flops 4194304 | bytes 2097152 | tf_op jit(solution)/shard_map/inner_1/pallas_call | solution.py:511
  16.3 0.0 collective-permute-done.7.flat_a
  16.3 0.4 %collective-permute-done.8.flat_b = f32[2,24,256]{2,1,0:T(8,128)S(1)} collective-permute-done((f32[2,24,256]{2,1,0:T(8,128)S(1)}, f32[2,24,256]{2,1,0:T(8,128)S(1)}, u32[]{:S(2)}, u32[]{:S(2)}) %collective-permute-start.8) | collective-permute-done | bytes 49184 | tf_op jit(solution)/shard_map/ppermute | solution.py:59
  16.7 0.4 %sides_1.1.partial = f32[4,6,16,256]{3,2,1,0:T(8,128)S(1)} custom-call(f32[4,24,128]{2,1,0:T(8,128)S(1)} %get-tuple-element.40.scale, f32[2,48,192]{2,1,0:T(8,128)S(1)} %get-tuple-element.41.select, f32[2,384,128]{2,1,0:T(8,128)S(1)} %inner_1.1.partial, f32[3,24,256]{2,1,0:T(8,128)S(1)} %get-tuple-element.67.low, f32[3,24,256]{2,1,0:T(8,128)S(1)} %get-tuple-element.68.high, ...), custom_call_target="tpu_custom_call" | custom-call | flops 1048576 | bytes 1048576 | tf_op jit(solution)/shard_map/sides_1/pallas_call | solution.py:511
  17.0 0.9 %collective-permute-done.9.deep_first = f32[24,256]{1,0:T(8,128)S(1)} collective-permute-done((f32[24,256]{1,0:T(8,128)S(1)}, f32[24,256]{1,0:T(8,128)S(1)}, u32[]{:S(2)}, u32[]{:S(2)}) %collective-permute-start.9) | collective-permute-done | bytes 24608 | tf_op jit(solution)/shard_map/ppermute | solution.py:59
  18.0 0.0 collective-permute-done.10.deep_second
  18.0 1.0 %finish_1.1 = f32[4,6,16,256]{3,2,1,0:T(8,128)} custom-call(f32[2,8,24,128]{3,2,1,0:T(8,128)S(1)} %get-tuple-element.39.turns, f32[4,6,16,256]{3,2,1,0:T(8,128)S(1)} %sides_1.1.partial, f32[3,24,256]{2,1,0:T(8,128)S(1)} %get-tuple-element.67.low, f32[3,24,256]{2,1,0:T(8,128)S(1)} %get-tuple-element.68.high, f32[24,256]{1,0:T(8,128)S(1)} %collective-permute-done.9.deep_first, ...), custom_call_target="tpu_custom_call" | custom-call | tf_op jit(solution)/shard_map/finish_1/pallas_call | solution.py:598
  (3 shorter events, 0.0 us)
Async XLA Ops:
  1.4 5.1 %collective-permute-start.2 = (f32[40,256]{1,0:T(8,128)S(1)}, f32[40,256]{1,0:T(8,128)S(1)}, u32[]{:S(2)}, u32[]{:S(2)}) collective-permute-start(f32[40,256]{1,0:T(8,128)S(1)} %get-tuple-element.51), channel_id=1, source_target_pairs={{0,8},{1,9},{2,10},{3,11},{4,12},{5,13},{6,14},{7,15},{8,0},{9,1},... | collective-permute-start | bytes 122888 | tf_op jit(solution)/shard_map/ppermute | solution.py:59
  4.5 2.0 %collective-permute-start.3 = (f32[40,256]{1,0:T(8,128)S(1)}, f32[40,256]{1,0:T(8,128)S(1)}, u32[]{:S(2)}, u32[]{:S(2)}) collective-permute-start(f32[40,256]{1,0:T(8,128)S(1)} %get-tuple-element.52), channel_id=1, source_target_pairs={{0,1},{1,0},{2,3},{3,2},{4,5},{5,4},{6,7},{7,6},{8,9},{9,8},{10,11... | collective-permute-start | bytes 122888 | tf_op jit(solution)/shard_map/ppermute | solution.py:59
  5.2 5.8 %collective-permute-start.1 = (f32[120,256]{1,0:T(8,128)S(1)}, f32[120,256]{1,0:T(8,128)S(1)}, u32[]{:S(2)}, u32[]{:S(2)}) collective-permute-start(f32[120,256]{1,0:T(8,128)S(1)} %get-tuple-element.50), channel_id=1, source_target_pairs={{0,8},{1,9},{2,10},{3,11},{4,12},{5,13},{6,14},{7,15},{8,0},{9,1},... | collective-permute-start | bytes 368648 | tf_op jit(solution)/shard_map/ppermute | solution.py:59
  5.3 3.4 %collective-permute-start = (f32[96,256]{1,0:T(8,128)S(1)}, f32[96,256]{1,0:T(8,128)S(1)}, u32[]{:S(2)}, u32[]{:S(2)}) collective-permute-start(f32[96,256]{1,0:T(8,128)S(1)} %get-tuple-element.49), channel_id=1, source_target_pairs={{0,1},{1,0},{2,3},{3,2},{4,5},{5,4},{6,7},{7,6},{8,9},{9,8},{10,11... | collective-permute-start | bytes 294920 | tf_op jit(solution)/shard_map/ppermute | solution.py:59
  6.6 5.0 %collective-permute-start.4 = (f32[3,24,256]{2,1,0:T(8,128)S(1)}, f32[3,24,256]{2,1,0:T(8,128)S(1)}, u32[]{:S(2)}, u32[]{:S(2)}) collective-permute-start(f32[3,24,256]{2,1,0:T(8,128)S(1)} %get-tuple-element.56), channel_id=1, source_target_pairs={{0,1},{1,0},{2,3},{3,2},{4,5},{5,4},{6,7},{7,6},{8,9},{9,8},{10,11... | collective-permute-start | bytes 221192 | tf_op jit(solution)/shard_map/ppermute | solution.py:59
  6.7 4.9 %collective-permute-start.5 = (f32[2,24,256]{2,1,0:T(8,128)S(1)}, f32[2,24,256]{2,1,0:T(8,128)S(1)}, u32[]{:S(2)}, u32[]{:S(2)}) collective-permute-start(f32[2,24,256]{2,1,0:T(8,128)S(1)} %get-tuple-element.57), channel_id=1, source_target_pairs={{0,8},{1,2},{2,1},{3,4},{4,3},{5,6},{6,5},{7,15},{8,0},{9,10},{10,... | collective-permute-start | bytes 147464 | tf_op jit(solution)/shard_map/ppermute | solution.py:59
  8.7 3.4 %collective-permute-start.6 = (f32[24,256]{1,0:T(8,128)S(1)}, f32[24,256]{1,0:T(8,128)S(1)}, u32[]{:S(2)}, u32[]{:S(2)}) collective-permute-start(f32[24,256]{1,0:T(8,128)S(1)} %get-tuple-element.62), channel_id=1, source_target_pairs={{0,1},{1,0},{2,3},{3,2},{4,5},{5,4},{6,7},{7,6},{8,16},{9,17},{10,... | collective-permute-start | bytes 73736 | tf_op jit(solution)/shard_map/ppermute | solution.py:59
  12.4 3.8 %collective-permute-start.7 = (f32[2,24,256]{2,1,0:T(8,128)S(1)}, f32[2,24,256]{2,1,0:T(8,128)S(1)}, u32[]{:S(2)}, u32[]{:S(2)}) collective-permute-start(f32[2,24,256]{2,1,0:T(8,128)S(1)} %get-tuple-element.69), channel_id=1, source_target_pairs={{0,1},{1,0},{2,3},{3,2},{4,5},{5,4},{6,7},{7,6},{8,9},{9,8},{10,11... | collective-permute-start | bytes 147464 | tf_op jit(solution)/shard_map/ppermute | solution.py:59
  12.5 4.2 %collective-permute-start.8 = (f32[2,24,256]{2,1,0:T(8,128)S(1)}, f32[2,24,256]{2,1,0:T(8,128)S(1)}, u32[]{:S(2)}, u32[]{:S(2)}) collective-permute-start(f32[2,24,256]{2,1,0:T(8,128)S(1)} %get-tuple-element.70), channel_id=1, source_target_pairs={{0,8},{1,2},{2,1},{3,4},{4,3},{5,6},{6,5},{7,15},{8,0},{9,10},{10,... | collective-permute-start | bytes 147464 | tf_op jit(solution)/shard_map/ppermute | solution.py:59
  14.1 3.8 %collective-permute-start.9 = (f32[24,256]{1,0:T(8,128)S(1)}, f32[24,256]{1,0:T(8,128)S(1)}, u32[]{:S(2)}, u32[]{:S(2)}) collective-permute-start(f32[24,256]{1,0:T(8,128)S(1)} %get-tuple-element.71), channel_id=1, source_target_pairs={{0,8},{1,9},{2,10},{3,11},{4,5},{5,4},{6,7},{7,6},{8,0},{9,1},{10,... | collective-permute-start | bytes 73736 | tf_op jit(solution)/shard_map/ppermute | solution.py:59
  14.6 3.4 %collective-permute-start.10 = (f32[24,256]{1,0:T(8,128)S(1)}, f32[24,256]{1,0:T(8,128)S(1)}, u32[]{:S(2)}, u32[]{:S(2)}) collective-permute-start(f32[24,256]{1,0:T(8,128)S(1)} %get-tuple-element.72), channel_id=1, source_target_pairs={{0,1},{1,0},{2,3},{3,2},{4,12},{5,13},{6,14},{7,15},{8,16},{9,17},... | collective-permute-start | bytes 73736 | tf_op jit(solution)/shard_map/ppermute | solution.py:59

commit v5 on v4

--- a/solution.py
+++ b/solution.py
@@ -318,16 +318,28 @@
     inner_kernel(state, scale, partial)
 
 
-def inner_kernel(state, scale, partial):
+def later_inner_kernel(state, ghosts, scale, partial):
+    inner_kernel(state, scale, partial, z_pairs(ghosts[0], ghosts[1]))
+
+
+def inner_kernel(state, scale, partial, pairs=None):
+    ends = ends_of((ROWS, HALF))
+
+    def plane(x):
+        halves, at = plane_at(state, x), EDGE - 1 - x
+        if pairs is None:
+            return halves
+        return [half + jnp.where(ends, turned(pairs[h][at % 2], -at), 0.0) for h, half in enumerate(halves)]
+
     lane = iota((ROWS, HALF), 1)
     start_y, end_y = lane < EDGE, lane >= HALF - EDGE
     start_z, end_z = lane % EDGE == 0, lane % EDGE == EDGE - 1
     weight_x, weight_y, weight_z, weight = (scale[number] for number in range(4))
     tile = 2 * SLOTS
-    planes = {0: plane_at(state, 0)}
+    planes = {0: plane(0)}
     for x in range(EDGE):
         if x + 1 < EDGE:
-            planes[x + 1] = plane_at(state, x + 1)
+            planes[x + 1] = plane(x + 1)
         left, right = planes[x]
         up = [turned(half, EDGE) for half in (left, right)]
         down = [turned(half, -EDGE) for half in (left, right)]
@@ -372,7 +384,7 @@
 
 
 def sides_kernel(scale, select, partial, low, high, flat_a, flat_b, *refs):
-    first_step = len(refs) == 3
+    first_step = len(refs) == 5
     done = refs[0] if first_step else refs[1]
     packer = Packer()
     sources = (low, high, flat_a, flat_b)
@@ -398,9 +410,10 @@
             halves.append(value)
         if first_step:
             packer.add_z(x, *halves)
+            packer.add_y(x, *halves)
     if first_step:
         for h in range(2):
-            for ref, table in zip(refs[1:], packer.z_tables(h)):
+            for ref, table in zip(refs[1:], (*packer.z_tables(h), *packer.y_tables(h))):
                 ref[:, h * HALF : (h + 1) * HALF] = table
     else:
         blocks = refs[0]
@@ -441,25 +454,35 @@
     return (place == 0) | (place == EDGE - 1)
 
 
-def finish_kernel(
-    turns, partial, packed_low, packed_high, known, deep_b, flat_a, relayed, z_low, z_high, done, low, high, *sends
-):
+def finish_kernel(turns, partial, packed_z, packed_y, known, deep_b, flat_a, relayed, own_z, outs):
+    low, high, *sends, ghosts = outs
     deep_a = jnp.where(relayed[...] > 0.5, flat_a[2], known[...])
-    ghosts = z_ghosts(turns, (z_low[...], z_high[...]), deep_a, deep_b[...])
-    pairs = z_pairs(*ghosts)
-    ends = ends_of((ROWS, HALF))
-    packer = Packer()
-    for x in range(EDGE):
-        halves, at = [], EDGE - 1 - x
-        for h, value in enumerate(plane_at(partial, x)):
-            value = value + jnp.where(ends, turned(pairs[h][at % 2], -at), 0.0)
-            done[h, pl.ds(x * ROWS, ROWS), :] = value
-            halves.append(value)
-        packer.add_y(x, *halves)
-    write_tables(packer, done, (low, high))
-    low[2] = packed_low[...] + ghosts[0]
-    high[2] = packed_high[...] + ghosts[1]
+    both = z_ghosts(turns, [ref[...] for ref in own_z], deep_a, deep_b[...])
+    pairs = z_pairs(*both)
+    lane = iota((ROWS, HALF), 1)
+    ends, group = ends_of((ROWS, HALF)), lane // EDGE
+    for side, ref in enumerate((low, high)):
+        ghosts[side] = both[side]
+        x = side * (EDGE - 1)
+        at = EDGE - 1 - x
+        for h, half in enumerate(plane_at(partial, x)):
+            lanes = slice(h * HALF, (h + 1) * HALF)
+            ref[0, :, lanes] = half + jnp.where(ends, turned(pairs[h][at % 2], -at), 0.0)
+        ref[2] = packed_z[side][...] + both[side]
+        for h in range(2):
+            total = jnp.zeros((ROWS, HALF), jnp.float32)
+            for number in range(GROUPS):
+                at = EDGE - 1 - (h * GROUPS + number)
+                moved = turned(pairs[side][at % 2], EDGE * number - at - side * (HALF - EDGE))
+                total = jnp.where(ends & (group == number), moved, total)
+            lanes = slice(h * HALF, (h + 1) * HALF)
+            ref[1, :, lanes] = packed_y[side][:, lanes] + total
     emit_faces((low, high), sends)
+
+
+def finish_0_kernel(turns, partial, *refs):
+    packed, (known, deep_b, flat_a, relayed), own_z, outs = refs[:4], refs[4:8], refs[8:10], refs[10:]
+    finish_kernel(turns, partial, packed[:2], packed[2:], known, deep_b, flat_a, relayed, own_z, outs)
 
 
 def last_kernel(turns, partial, low, high, deep_first, deep_second, result, rows_of, blocks, sent):
@@ -493,7 +516,7 @@
 VECTOR = pltpu.VMEM
 SMALL = pltpu.CompilerParams(vmem_limit_bytes=8 << 20)
 FLAT = (2, ROWS, PLANE)
-TABLES = (STATE, SIDE, SIDE, FLAT, FLAT, FACE, FACE)
+TABLES = (SIDE, SIDE, FLAT, FLAT, FACE, FACE, (2, *FACE))
 EARLY = (ROWS + 4 * SLOTS, PLANE)
 TO_DEV = (NFIELD * EDGE, PLANE)
 TO_GRP = (NFIELD * EDGE + ROWS, PLANE)
@@ -570,24 +593,24 @@
         4 << 20,
         [pltpu.VMEM(SPARE, jnp.float32)],
     )
-    partial, packed_low, packed_high = call(
+    partial, *packed = call(
         sides_kernel,
         "sides_0",
-        [STATE, FACE, FACE],
+        [STATE, FACE, FACE, FACE, FACE],
         [scale, select, partial, new_low, new_high, flat_a, flat_b],
     )
-    state, *tables = call(
-        finish_kernel,
+    *tables, ghosts = call(
+        finish_0_kernel,
         "finish_0",
         TABLES,
-        [turns, partial, packed_low, packed_high, deep_a, deep_b, flat_a, relayed, z_low, z_high],
+        [turns, partial, *packed, deep_a, deep_b, flat_a, relayed, z_low, z_high],
     )
     own, sends = tables[:2], tables[2:]
     flat_a = exchange(sends[0], "dev", 0)
     flat_b = exchange(sends[1], "dev", 1)
     deep_first = exchange(sends[2], "grp", lambda dev: 1 if swapped_order(dev) else 0)
     deep_second = exchange(sends[3], "grp", lambda dev: 0 if swapped_order(dev) else 1)
-    (partial,) = call(inner_kernel, "inner_1", [STATE], [state, scale], 4 << 20)
+    (partial,) = call(later_inner_kernel, "inner_1", [STATE], [partial, ghosts, scale], 4 << 20)
     (blocks,) = call(
         sides_kernel,
         "sides_1",

time: 19.1 us -> 19.1 us (level)
  waiting for transfers between devices: 3.58 us -> 3.15 us
  Pallas kernels: 4.72 us -> 5.01 us
    ppermute x11, waiting for transfers between devices: 3.58 us -> 3.15 us  [exchange(): return lax.ppermute(block, ('grp', 'dev'), partners(axis, offset))]
    pallas_call x7, Pallas kernels: 2.37 us -> 2.66 us  [call(): pl.pallas_call(kernel, name=name, compiler_params=SMALL, out_shape=[shape...]
  transfers between devices with their start and end apart: 11 -> 11, of which waited for: 3 -> 2; matrix products, arithmetic and copies ran while one was open for 0% -> 0% of each run, Pallas kernels for 10% -> 13%
where the time goes in v5:
time: 19.1 us; the launch traced here: 18.9 us
  starting transfers between devices  9.24 us (48%)
  Pallas kernels  5.01 us (26%)
  waiting for transfers between devices  3.15 us (16%)
  between operations  1.44 us (8%)
    ppermute x11, starting transfers between devices, exchange(): return lax.ppermute(block, ('grp', 'dev'), partners(axis, offset))  9.24 us
    ppermute x11, waiting for transfers between devices, exchange(): return lax.ppermute(block, ('grp', 'dev'), partners(axis, offset))  3.15 us
    pallas_call x7, Pallas kernels, call(): pl.pallas_call(kernel, name=name, compiler_params=SMALL, out_shape=[shape...  2.66 us
    pallas_call x1, Pallas kernels, start(): pl.pallas_call(start_kernel, name='start', compiler_params=SMALL, out_sha...  1.38 us
    pallas_call x1, Pallas kernels, body(): pl.pallas_call(last_kernel, name='finish_1', compiler_params=SMALL, out_s...  0.97 us
  transfers between devices with their start and end apart: 11, of which 2 were waited for; matrix products, arithmetic and copies ran while one was open for 0% of the time, Pallas kernels for 13%

profile of v5, /device:TPU:0, one launch (start us, length us, event | category | flops | bytes accessed | tf_op | source)
XLA Modules:
  0.0 18.9 jit_solution(13217760502076433620)
XLA Ops:
  0.0 1.4 %start.1 = (f32[4,6,16,256]{3,2,1,0:T(8,128)S(1)}, f32[3,24,256]{2,1,0:T(8,128)S(1)}, f32[3,24,256]{2,1,0:T(8,128)S(1)}, f32[40,256]{1,0:T(8,128)S(1)}, f32[40,2...) custom-call(f32[4,6,16,256]{3,2,1,0:T(8,128)} %fields.1, ...), custom_call_target="tpu_custom_call" | custom-call | tf_op jit(solution)/shard_map/start/pallas_call | solution.py:548
  1.4 3.1 %collective-permute-start.2 = (f32[40,256]{1,0:T(8,128)S(1)}, f32[40,256]{1,0:T(8,128)S(1)}, u32[]{:S(2)}, u32[]{:S(2)}) collective-permute-start(f32[40,256]{1,0:T(8,128)S(1)} %get-tuple-element.53), channel_id=1, source_target_pairs={{0,8},{1,9},{2,10},{3,11},{4,12},{5,13},{6,14},{7,15},{8,0},{9,1},... | collective-permute-start | bytes 122888 | tf_op jit(solution)/shard_map/ppermute | solution.py:59
  4.5 0.0 collective-permute-start.3
  5.2 0.1 collective-permute-start.1
  5.3 0.5 %collective-permute-start = (f32[96,256]{1,0:T(8,128)S(1)}, f32[96,256]{1,0:T(8,128)S(1)}, u32[]{:S(2)}, u32[]{:S(2)}) collective-permute-start(f32[96,256]{1,0:T(8,128)S(1)} %get-tuple-element.51), channel_id=1, source_target_pairs={{0,1},{1,0},{2,3},{3,2},{4,5},{5,4},{6,7},{7,6},{8,9},{9,8},{10,11... | collective-permute-start | bytes 294920 | tf_op jit(solution)/shard_map/ppermute | solution.py:59
  6.5 0.0 collective-permute-done.2.faces
  6.5 0.0 collective-permute-done.3.faces_dev
  6.5 0.1 faces.1
  6.6 0.1 collective-permute-start.4
  6.7 2.0 %collective-permute-start.5 = (f32[2,24,256]{2,1,0:T(8,128)S(1)}, f32[2,24,256]{2,1,0:T(8,128)S(1)}, u32[]{:S(2)}, u32[]{:S(2)}) collective-permute-start(f32[2,24,256]{2,1,0:T(8,128)S(1)} %get-tuple-element.59), channel_id=1, source_target_pairs={{0,8},{1,2},{2,1},{3,4},{4,3},{5,6},{6,5},{7,15},{8,0},{9,10},{10,... | collective-permute-start | bytes 147464 | tf_op jit(solution)/shard_map/ppermute | solution.py:59
  8.7 0.0 collective-permute-start.6
  8.7 0.0 collective-permute-done.block_dev
  8.7 2.3 %collective-permute-done.1.block_grp = f32[120,256]{1,0:T(8,128)S(1)} collective-permute-done((f32[120,256]{1,0:T(8,128)S(1)}, f32[120,256]{1,0:T(8,128)S(1)}, u32[]{:S(2)}, u32[]{:S(2)}) %collective-permute-start.1) | collective-permute-done | bytes 122912 | tf_op jit(solution)/shard_map/ppermute | solution.py:59
  11.0 0.5 %inner_0.1 = (f32[2,384,128]{2,1,0:T(8,128)S(1)}, f32[24,256]{1,0:T(8,128)S(1)}, f32[24,256]{1,0:T(8,128)S(1)}, f32[24,256]{1,0:T(8,128)S(1)}, f32[24,256]{1,0:T(8,128)S(1)}) custom-call(f32[24,256]{1,0:T(8,128)S(1)} %broadcast_in_dim.21.mask_dev, f32[24,256]{1,0:T(8,128)S(1)} %broadcast_in_dim.23.mask_grp, f32[4,24,128]{2,1,0:T(8,128)S(1)} %get-tuple-element.42.scale, ...), custom_call_target="tpu_custom_call" | custom-call | flops 4194304 | bytes 2097152 | tf_op jit(solution)/shard_map/inner_0/pallas_call | solution.py:534
  11.5 0.0 collective-permute-done.5.flat_b
  11.5 0.0 collective-permute-done.4.flat_a.refs_6_
  11.5 0.6 %sides_0.1 = (f32[2,384,128]{2,1,0:T(8,128)S(1)}, f32[24,256]{1,0:T(8,128)S(1)}, f32[24,256]{1,0:T(8,128)S(1)}, f32[24,256]{1,0:T(8,128)S(1)}, f32[24,256]{1,0:T(8,128)S(1)}) custom-call(f32[4,24,128]{2,1,0:T(8,128)S(1)} %get-tuple-element.42.scale, f32[2,48,192]{2,1,0:T(8,128)S(1)} %get-tuple-element.43.select, ...), custom_call_target="tpu_custom_call" | custom-call | flops 1048576 | bytes 1048576 | tf_op jit(solution)/shard_map/sides_0/pallas_call | solution.py:534
  12.1 0.0 collective-permute-done.6.refs_5_
  12.1 0.3 %finish_0.1 = (f32[3,24,256]{2,1,0:T(8,128)S(1)}, f32[3,24,256]{2,1,0:T(8,128)S(1)}, f32[2,24,256]{2,1,0:T(8,128)S(1)}, f32[2,24,256]{2,1,0:T(8,128)S(1)}, f32[2...) custom-call(f32[2,8,24,128]{3,2,1,0:T(8,128)S(1)} %get-tuple-element.41.turns, ...), custom_call_target="tpu_custom_call" | custom-call | flops 1048576 | bytes 1048576 | tf_op jit(solution)/shard_map/finish_0/pallas_call | solution.py:534
  12.4 0.1 collective-permute-start.7
  12.5 1.6 %collective-permute-start.8 = (f32[2,24,256]{2,1,0:T(8,128)S(1)}, f32[2,24,256]{2,1,0:T(8,128)S(1)}, u32[]{:S(2)}, u32[]{:S(2)}) collective-permute-start(f32[2,24,256]{2,1,0:T(8,128)S(1)} %get-tuple-element.74), channel_id=1, source_target_pairs={{0,8},{1,2},{2,1},{3,4},{4,3},{5,6},{6,5},{7,15},{8,0},{9,10},{10,... | collective-permute-start | bytes 147464 | tf_op jit(solution)/shard_map/ppermute | solution.py:59
  14.1 0.5 %collective-permute-start.9 = (f32[24,256]{1,0:T(8,128)S(1)}, f32[24,256]{1,0:T(8,128)S(1)}, u32[]{:S(2)}, u32[]{:S(2)}) collective-permute-start(f32[24,256]{1,0:T(8,128)S(1)} %get-tuple-element.75), channel_id=1, source_target_pairs={{0,8},{1,9},{2,10},{3,11},{4,5},{5,4},{6,7},{7,6},{8,0},{9,1},{10,... | collective-permute-start | bytes 73736 | tf_op jit(solution)/shard_map/ppermute | solution.py:59
  14.6 1.2 %collective-permute-start.10 = (f32[24,256]{1,0:T(8,128)S(1)}, f32[24,256]{1,0:T(8,128)S(1)}, u32[]{:S(2)}, u32[]{:S(2)}) collective-permute-start(f32[24,256]{1,0:T(8,128)S(1)} %get-tuple-element.76), channel_id=1, source_target_pairs={{0,1},{1,0},{2,3},{3,2},{4,12},{5,13},{6,14},{7,15},{8,16},{9,17},... | collective-permute-start | bytes 73736 | tf_op jit(solution)/shard_map/ppermute | solution.py:59
  15.8 0.8 %inner_1.1.partial = f32[2,384,128]{2,1,0:T(8,128)S(1)} custom-call(f32[2,384,128]{2,1,0:T(8,128)S(1)} %get-tuple-element.60.partial.state, f32[2,24,256]{2,1,0:T(8,128)S(1)} %get-tuple-element.70.ghosts, f32[4,24,128]{2,1,0:T(8,128)S(1)} %get-tuple-element.42.scale), custom_call_target="tpu_custom_call" | custom-call | flops 4194304 | bytes 2097152 | tf_op jit(solution)/shard_map/inner_1/pallas_call | solution.py:534
  16.6 0.0 collective-permute-done.7.flat_a
  16.6 0.0 collective-permute-done.8.flat_b
  16.6 0.4 %sides_1.1.partial = f32[4,6,16,256]{3,2,1,0:T(8,128)S(1)} custom-call(f32[4,24,128]{2,1,0:T(8,128)S(1)} %get-tuple-element.42.scale, f32[2,48,192]{2,1,0:T(8,128)S(1)} %get-tuple-element.43.select, f32[2,384,128]{2,1,0:T(8,128)S(1)} %inner_1.1.partial, f32[3,24,256]{2,1,0:T(8,128)S(1)} %get-tuple-element.71.low, f32[3,24,256]{2,1,0:T(8,128)S(1)} %get-tuple-element.72.high, ...), custom_call_target="tpu_custom_call" | custom-call | flops 1048576 | bytes 1048576 | tf_op jit(solution)/shard_map/sides_1/pallas_call | solution.py:534
  17.0 0.9 %collective-permute-done.9.deep_first = f32[24,256]{1,0:T(8,128)S(1)} collective-permute-done((f32[24,256]{1,0:T(8,128)S(1)}, f32[24,256]{1,0:T(8,128)S(1)}, u32[]{:S(2)}, u32[]{:S(2)}) %collective-permute-start.9) | collective-permute-done | bytes 24608 | tf_op jit(solution)/shard_map/ppermute | solution.py:59
  17.9 0.0 collective-permute-done.10.deep_second
  17.9 1.0 %finish_1.1 = f32[4,6,16,256]{3,2,1,0:T(8,128)} custom-call(f32[2,8,24,128]{3,2,1,0:T(8,128)S(1)} %get-tuple-element.41.turns, f32[4,6,16,256]{3,2,1,0:T(8,128)S(1)} %sides_1.1.partial, f32[3,24,256]{2,1,0:T(8,128)S(1)} %get-tuple-element.71.low, f32[3,24,256]{2,1,0:T(8,128)S(1)} %get-tuple-element.72.high, f32[24,256]{1,0:T(8,128)S(1)} %collective-permute-done.9.deep_first, ...), custom_call_target="tpu_custom_call" | custom-call | tf_op jit(solution)/shard_map/finish_1/pallas_call | solution.py:621
  (3 shorter events, 0.0 us)
Async XLA Ops:
  1.4 5.1 %collective-permute-start.2 = (f32[40,256]{1,0:T(8,128)S(1)}, f32[40,256]{1,0:T(8,128)S(1)}, u32[]{:S(2)}, u32[]{:S(2)}) collective-permute-start(f32[40,256]{1,0:T(8,128)S(1)} %get-tuple-element.53), channel_id=1, source_target_pairs={{0,8},{1,9},{2,10},{3,11},{4,12},{5,13},{6,14},{7,15},{8,0},{9,1},... | collective-permute-start | bytes 122888 | tf_op jit(solution)/shard_map/ppermute | solution.py:59
  4.5 2.0 %collective-permute-start.3 = (f32[40,256]{1,0:T(8,128)S(1)}, f32[40,256]{1,0:T(8,128)S(1)}, u32[]{:S(2)}, u32[]{:S(2)}) collective-permute-start(f32[40,256]{1,0:T(8,128)S(1)} %get-tuple-element.54), channel_id=1, source_target_pairs={{0,1},{1,0},{2,3},{3,2},{4,5},{5,4},{6,7},{7,6},{8,9},{9,8},{10,11... | collective-permute-start | bytes 122888 | tf_op jit(solution)/shard_map/ppermute | solution.py:59
  5.2 5.8 %collective-permute-start.1 = (f32[120,256]{1,0:T(8,128)S(1)}, f32[120,256]{1,0:T(8,128)S(1)}, u32[]{:S(2)}, u32[]{:S(2)}) collective-permute-start(f32[120,256]{1,0:T(8,128)S(1)} %get-tuple-element.52), channel_id=1, source_target_pairs={{0,8},{1,9},{2,10},{3,11},{4,12},{5,13},{6,14},{7,15},{8,0},{9,1},... | collective-permute-start | bytes 368648 | tf_op jit(solution)/shard_map/ppermute | solution.py:59
  5.3 3.4 %collective-permute-start = (f32[96,256]{1,0:T(8,128)S(1)}, f32[96,256]{1,0:T(8,128)S(1)}, u32[]{:S(2)}, u32[]{:S(2)}) collective-permute-start(f32[96,256]{1,0:T(8,128)S(1)} %get-tuple-element.51), channel_id=1, source_target_pairs={{0,1},{1,0},{2,3},{3,2},{4,5},{5,4},{6,7},{7,6},{8,9},{9,8},{10,11... | collective-permute-start | bytes 294920 | tf_op jit(solution)/shard_map/ppermute | solution.py:59
  6.6 5.0 %collective-permute-start.4 = (f32[3,24,256]{2,1,0:T(8,128)S(1)}, f32[3,24,256]{2,1,0:T(8,128)S(1)}, u32[]{:S(2)}, u32[]{:S(2)}) collective-permute-start(f32[3,24,256]{2,1,0:T(8,128)S(1)} %get-tuple-element.58), channel_id=1, source_target_pairs={{0,1},{1,0},{2,3},{3,2},{4,5},{5,4},{6,7},{7,6},{8,9},{9,8},{10,11... | collective-permute-start | bytes 221192 | tf_op jit(solution)/shard_map/ppermute | solution.py:59
  6.7 4.9 %collective-permute-start.5 = (f32[2,24,256]{2,1,0:T(8,128)S(1)}, f32[2,24,256]{2,1,0:T(8,128)S(1)}, u32[]{:S(2)}, u32[]{:S(2)}) collective-permute-start(f32[2,24,256]{2,1,0:T(8,128)S(1)} %get-tuple-element.59), channel_id=1, source_target_pairs={{0,8},{1,2},{2,1},{3,4},{4,3},{5,6},{6,5},{7,15},{8,0},{9,10},{10,... | collective-permute-start | bytes 147464 | tf_op jit(solution)/shard_map/ppermute | solution.py:59
  8.7 3.4 %collective-permute-start.6 = (f32[24,256]{1,0:T(8,128)S(1)}, f32[24,256]{1,0:T(8,128)S(1)}, u32[]{:S(2)}, u32[]{:S(2)}) collective-permute-start(f32[24,256]{1,0:T(8,128)S(1)} %get-tuple-element.66), channel_id=1, source_target_pairs={{0,1},{1,0},{2,3},{3,2},{4,5},{5,4},{6,7},{7,6},{8,16},{9,17},{10,... | collective-permute-start | bytes 73736 | tf_op jit(solution)/shard_map/ppermute | solution.py:59
  12.4 4.2 %collective-permute-start.7 = (f32[2,24,256]{2,1,0:T(8,128)S(1)}, f32[2,24,256]{2,1,0:T(8,128)S(1)}, u32[]{:S(2)}, u32[]{:S(2)}) collective-permute-start(f32[2,24,256]{2,1,0:T(8,128)S(1)} %get-tuple-element.73), channel_id=1, source_target_pairs={{0,1},{1,0},{2,3},{3,2},{4,5},{5,4},{6,7},{7,6},{8,9},{9,8},{10,11... | collective-permute-start | bytes 147464 | tf_op jit(solution)/shard_map/ppermute | solution.py:59
  12.5 4.2 %collective-permute-start.8 = (f32[2,24,256]{2,1,0:T(8,128)S(1)}, f32[2,24,256]{2,1,0:T(8,128)S(1)}, u32[]{:S(2)}, u32[]{:S(2)}) collective-permute-start(f32[2,24,256]{2,1,0:T(8,128)S(1)} %get-tuple-element.74), channel_id=1, source_target_pairs={{0,8},{1,2},{2,1},{3,4},{4,3},{5,6},{6,5},{7,15},{8,0},{9,10},{10,... | collective-permute-start | bytes 147464 | tf_op jit(solution)/shard_map/ppermute | solution.py:59
  14.1 3.8 %collective-permute-start.9 = (f32[24,256]{1,0:T(8,128)S(1)}, f32[24,256]{1,0:T(8,128)S(1)}, u32[]{:S(2)}, u32[]{:S(2)}) collective-permute-start(f32[24,256]{1,0:T(8,128)S(1)} %get-tuple-element.75), channel_id=1, source_target_pairs={{0,8},{1,9},{2,10},{3,11},{4,5},{5,4},{6,7},{7,6},{8,0},{9,1},{10,... | collective-permute-start | bytes 73736 | tf_op jit(solution)/shard_map/ppermute | solution.py:59
  14.6 3.3 %collective-permute-start.10 = (f32[24,256]{1,0:T(8,128)S(1)}, f32[24,256]{1,0:T(8,128)S(1)}, u32[]{:S(2)}, u32[]{:S(2)}) collective-permute-start(f32[24,256]{1,0:T(8,128)S(1)} %get-tuple-element.76), channel_id=1, source_target_pairs={{0,1},{1,0},{2,3},{3,2},{4,12},{5,13},{6,14},{7,15},{8,16},{9,17},... | collective-permute-start | bytes 73736 | tf_op jit(solution)/shard_map/ppermute | solution.py:59

commit v6 on v5

--- a/solution.py
+++ b/solution.py
@@ -29,6 +29,7 @@
 SOURCES = 4
 PARTS = 2
 SELECT = (2, 2 * ROWS, PARTS * SOURCES * ROWS)
+PIECE = 3
 TURNS = (2, 2 * SLOTS, ROWS, HALF)
 
 
@@ -502,9 +503,11 @@
                 ghost = pltpu.roll(jnp.where(even, *both), HALF - EDGE + 1, 1, stride=1, stride_axis=0)
                 lanes = pl.ds(h * HALF, HALF)
                 blocks[slot, f, :, lanes] = partial[slot, f, :, lanes] + jnp.where(ends, ghost, 0.0)
-        copy = pltpu.make_async_copy(blocks.at[slot], result.at[slot], sent.at[slot])
-        copy.start()
-        copies.append(copy)
+            if f % PIECE == PIECE - 1:
+                part = (slot, pl.ds(f + 1 - PIECE, PIECE))
+                copy = pltpu.make_async_copy(blocks.at[part], result.at[part], sent.at[len(copies)])
+                copy.start()
+                copies.append(copy)
     for copy in copies:
         copy.wait()
 
@@ -628,7 +631,7 @@
         scratch_shapes=[
             pltpu.VMEM((2, 2, ROWS, HALF), jnp.float32),
             pltpu.VMEM(fields.shape, jnp.float32),
-            pltpu.SemaphoreType.DMA((SLOTS,)),
+            pltpu.SemaphoreType.DMA((SLOTS * NFIELD // PIECE,)),
         ],
     )(turns, blocks, *own, deep_first, deep_second)
 

time: 19.1 us -> 19.1 us (level)
  no operation moved by 1% of the time
where the time goes in v6:
time: 19.1 us; the launch traced here: 18.9 us
  starting transfers between devices  9.24 us (48%)
  Pallas kernels  5.02 us (26%)
  waiting for transfers between devices  3.15 us (16%)
  between operations  1.44 us (8%)
    ppermute x11, starting transfers between devices, exchange(): return lax.ppermute(block, ('grp', 'dev'), partners(axis, offset))  9.24 us
    ppermute x11, waiting for transfers between devices, exchange(): return lax.ppermute(block, ('grp', 'dev'), partners(axis, offset))  3.15 us
    pallas_call x7, Pallas kernels, call(): pl.pallas_call(kernel, name=name, compiler_params=SMALL, out_shape=[shape...  2.66 us
    pallas_call x1, Pallas kernels, start(): pl.pallas_call(start_kernel, name='start', compiler_params=SMALL, out_sha...  1.38 us
    pallas_call x1, Pallas kernels, body(): pl.pallas_call(last_kernel, name='finish_1', compiler_params=SMALL, out_s...  0.99 us
  transfers between devices with their start and end apart: 11, of which 2 were waited for; matrix products, arithmetic and copies ran while one was open for 0% of the time, Pallas kernels for 13%

profile of v6, /device:TPU:0, one launch (start us, length us, event | category | flops | bytes accessed | tf_op | source)
XLA Modules:
  0.0 18.9 jit_solution(2715287677492534329)
XLA Ops:
  0.0 1.4 %start.1 = (f32[4,6,16,256]{3,2,1,0:T(8,128)S(1)}, f32[3,24,256]{2,1,0:T(8,128)S(1)}, f32[3,24,256]{2,1,0:T(8,128)S(1)}, f32[40,256]{1,0:T(8,128)S(1)}, f32[40,2...) custom-call(f32[4,6,16,256]{3,2,1,0:T(8,128)} %fields.1, ...), custom_call_target="tpu_custom_call" | custom-call | tf_op jit(solution)/shard_map/start/pallas_call | solution.py:551
  1.4 3.1 %collective-permute-start.2 = (f32[40,256]{1,0:T(8,128)S(1)}, f32[40,256]{1,0:T(8,128)S(1)}, u32[]{:S(2)}, u32[]{:S(2)}) collective-permute-start(f32[40,256]{1,0:T(8,128)S(1)} %get-tuple-element.53), channel_id=1, source_target_pairs={{0,8},{1,9},{2,10},{3,11},{4,12},{5,13},{6,14},{7,15},{8,0},{9,1},... | collective-permute-start | bytes 122888 | tf_op jit(solution)/shard_map/ppermute | solution.py:60
  4.5 0.0 collective-permute-start.3
  5.2 0.1 collective-permute-start.1
  5.3 0.5 %collective-permute-start = (f32[96,256]{1,0:T(8,128)S(1)}, f32[96,256]{1,0:T(8,128)S(1)}, u32[]{:S(2)}, u32[]{:S(2)}) collective-permute-start(f32[96,256]{1,0:T(8,128)S(1)} %get-tuple-element.51), channel_id=1, source_target_pairs={{0,1},{1,0},{2,3},{3,2},{4,5},{5,4},{6,7},{7,6},{8,9},{9,8},{10,11... | collective-permute-start | bytes 294920 | tf_op jit(solution)/shard_map/ppermute | solution.py:60
  6.5 0.0 collective-permute-done.2.faces
  6.5 0.0 collective-permute-done.3.faces_dev
  6.5 0.1 faces.1
  6.6 0.1 collective-permute-start.4
  6.7 2.0 %collective-permute-start.5 = (f32[2,24,256]{2,1,0:T(8,128)S(1)}, f32[2,24,256]{2,1,0:T(8,128)S(1)}, u32[]{:S(2)}, u32[]{:S(2)}) collective-permute-start(f32[2,24,256]{2,1,0:T(8,128)S(1)} %get-tuple-element.59), channel_id=1, source_target_pairs={{0,8},{1,2},{2,1},{3,4},{4,3},{5,6},{6,5},{7,15},{8,0},{9,10},{10,... | collective-permute-start | bytes 147464 | tf_op jit(solution)/shard_map/ppermute | solution.py:60
  8.7 0.0 collective-permute-start.6
  8.7 0.0 collective-permute-done.block_dev
  8.7 2.3 %collective-permute-done.1.block_grp = f32[120,256]{1,0:T(8,128)S(1)} collective-permute-done((f32[120,256]{1,0:T(8,128)S(1)}, f32[120,256]{1,0:T(8,128)S(1)}, u32[]{:S(2)}, u32[]{:S(2)}) %collective-permute-start.1) | collective-permute-done | bytes 122912 | tf_op jit(solution)/shard_map/ppermute | solution.py:60
  11.0 0.5 %inner_0.1 = (f32[2,384,128]{2,1,0:T(8,128)S(1)}, f32[24,256]{1,0:T(8,128)S(1)}, f32[24,256]{1,0:T(8,128)S(1)}, f32[24,256]{1,0:T(8,128)S(1)}, f32[24,256]{1,0:T(8,128)S(1)}) custom-call(f32[24,256]{1,0:T(8,128)S(1)} %broadcast_in_dim.21.mask_dev, f32[24,256]{1,0:T(8,128)S(1)} %broadcast_in_dim.23.mask_grp, f32[4,24,128]{2,1,0:T(8,128)S(1)} %get-tuple-element.42.scale, ...), custom_call_target="tpu_custom_call" | custom-call | flops 4194304 | bytes 2097152 | tf_op jit(solution)/shard_map/inner_0/pallas_call | solution.py:537
  11.5 0.0 collective-permute-done.5.flat_b
  11.5 0.0 collective-permute-done.4.flat_a.refs_6_
  11.5 0.6 %sides_0.1 = (f32[2,384,128]{2,1,0:T(8,128)S(1)}, f32[24,256]{1,0:T(8,128)S(1)}, f32[24,256]{1,0:T(8,128)S(1)}, f32[24,256]{1,0:T(8,128)S(1)}, f32[24,256]{1,0:T(8,128)S(1)}) custom-call(f32[4,24,128]{2,1,0:T(8,128)S(1)} %get-tuple-element.42.scale, f32[2,48,192]{2,1,0:T(8,128)S(1)} %get-tuple-element.43.select, ...), custom_call_target="tpu_custom_call" | custom-call | flops 1048576 | bytes 1048576 | tf_op jit(solution)/shard_map/sides_0/pallas_call | solution.py:537
  12.1 0.0 collective-permute-done.6.refs_5_
  12.1 0.3 %finish_0.1 = (f32[3,24,256]{2,1,0:T(8,128)S(1)}, f32[3,24,256]{2,1,0:T(8,128)S(1)}, f32[2,24,256]{2,1,0:T(8,128)S(1)}, f32[2,24,256]{2,1,0:T(8,128)S(1)}, f32[2...) custom-call(f32[2,8,24,128]{3,2,1,0:T(8,128)S(1)} %get-tuple-element.41.turns, ...), custom_call_target="tpu_custom_call" | custom-call | flops 1048576 | bytes 1048576 | tf_op jit(solution)/shard_map/finish_0/pallas_call | solution.py:537
  12.4 0.1 collective-permute-start.7
  12.5 1.6 %collective-permute-start.8 = (f32[2,24,256]{2,1,0:T(8,128)S(1)}, f32[2,24,256]{2,1,0:T(8,128)S(1)}, u32[]{:S(2)}, u32[]{:S(2)}) collective-permute-start(f32[2,24,256]{2,1,0:T(8,128)S(1)} %get-tuple-element.74), channel_id=1, source_target_pairs={{0,8},{1,2},{2,1},{3,4},{4,3},{5,6},{6,5},{7,15},{8,0},{9,10},{10,... | collective-permute-start | bytes 147464 | tf_op jit(solution)/shard_map/ppermute | solution.py:60
  14.1 0.5 %collective-permute-start.9 = (f32[24,256]{1,0:T(8,128)S(1)}, f32[24,256]{1,0:T(8,128)S(1)}, u32[]{:S(2)}, u32[]{:S(2)}) collective-permute-start(f32[24,256]{1,0:T(8,128)S(1)} %get-tuple-element.75), channel_id=1, source_target_pairs={{0,8},{1,9},{2,10},{3,11},{4,5},{5,4},{6,7},{7,6},{8,0},{9,1},{10,... | collective-permute-start | bytes 73736 | tf_op jit(solution)/shard_map/ppermute | solution.py:60
  14.6 1.2 %collective-permute-start.10 = (f32[24,256]{1,0:T(8,128)S(1)}, f32[24,256]{1,0:T(8,128)S(1)}, u32[]{:S(2)}, u32[]{:S(2)}) collective-permute-start(f32[24,256]{1,0:T(8,128)S(1)} %get-tuple-element.76), channel_id=1, source_target_pairs={{0,1},{1,0},{2,3},{3,2},{4,12},{5,13},{6,14},{7,15},{8,16},{9,17},... | collective-permute-start | bytes 73736 | tf_op jit(solution)/shard_map/ppermute | solution.py:60
  15.8 0.8 %inner_1.1.partial = f32[2,384,128]{2,1,0:T(8,128)S(1)} custom-call(f32[2,384,128]{2,1,0:T(8,128)S(1)} %get-tuple-element.60.partial.state, f32[2,24,256]{2,1,0:T(8,128)S(1)} %get-tuple-element.70.ghosts, f32[4,24,128]{2,1,0:T(8,128)S(1)} %get-tuple-element.42.scale), custom_call_target="tpu_custom_call" | custom-call | flops 4194304 | bytes 2097152 | tf_op jit(solution)/shard_map/inner_1/pallas_call | solution.py:537
  16.6 0.0 collective-permute-done.7.flat_a
  16.6 0.0 collective-permute-done.8.flat_b
  16.6 0.4 %sides_1.1.partial = f32[4,6,16,256]{3,2,1,0:T(8,128)S(1)} custom-call(f32[4,24,128]{2,1,0:T(8,128)S(1)} %get-tuple-element.42.scale, f32[2,48,192]{2,1,0:T(8,128)S(1)} %get-tuple-element.43.select, f32[2,384,128]{2,1,0:T(8,128)S(1)} %inner_1.1.partial, f32[3,24,256]{2,1,0:T(8,128)S(1)} %get-tuple-element.71.low, f32[3,24,256]{2,1,0:T(8,128)S(1)} %get-tuple-element.72.high, ...), custom_call_target="tpu_custom_call" | custom-call | flops 1048576 | bytes 1048576 | tf_op jit(solution)/shard_map/sides_1/pallas_call | solution.py:537
  17.0 0.9 %collective-permute-done.9.deep_first = f32[24,256]{1,0:T(8,128)S(1)} collective-permute-done((f32[24,256]{1,0:T(8,128)S(1)}, f32[24,256]{1,0:T(8,128)S(1)}, u32[]{:S(2)}, u32[]{:S(2)}) %collective-permute-start.9) | collective-permute-done | bytes 24608 | tf_op jit(solution)/shard_map/ppermute | solution.py:60
  17.9 0.0 collective-permute-done.10.deep_second
  17.9 1.0 %finish_1.1 = f32[4,6,16,256]{3,2,1,0:T(8,128)} custom-call(f32[2,8,24,128]{3,2,1,0:T(8,128)S(1)} %get-tuple-element.41.turns, f32[4,6,16,256]{3,2,1,0:T(8,128)S(1)} %sides_1.1.partial, f32[3,24,256]{2,1,0:T(8,128)S(1)} %get-tuple-element.71.low, f32[3,24,256]{2,1,0:T(8,128)S(1)} %get-tuple-element.72.high, f32[24,256]{1,0:T(8,128)S(1)} %collective-permute-done.9.deep_first, ...), custom_call_target="tpu_custom_call" | custom-call | tf_op jit(solution)/shard_map/finish_1/pallas_call | solution.py:624
  (3 shorter events, 0.0 us)
Async XLA Ops:
  1.4 5.1 %collective-permute-start.2 = (f32[40,256]{1,0:T(8,128)S(1)}, f32[40,256]{1,0:T(8,128)S(1)}, u32[]{:S(2)}, u32[]{:S(2)}) collective-permute-start(f32[40,256]{1,0:T(8,128)S(1)} %get-tuple-element.53), channel_id=1, source_target_pairs={{0,8},{1,9},{2,10},{3,11},{4,12},{5,13},{6,14},{7,15},{8,0},{9,1},... | collective-permute-start | bytes 122888 | tf_op jit(solution)/shard_map/ppermute | solution.py:60
  4.5 2.0 %collective-permute-start.3 = (f32[40,256]{1,0:T(8,128)S(1)}, f32[40,256]{1,0:T(8,128)S(1)}, u32[]{:S(2)}, u32[]{:S(2)}) collective-permute-start(f32[40,256]{1,0:T(8,128)S(1)} %get-tuple-element.54), channel_id=1, source_target_pairs={{0,1},{1,0},{2,3},{3,2},{4,5},{5,4},{6,7},{7,6},{8,9},{9,8},{10,11... | collective-permute-start | bytes 122888 | tf_op jit(solution)/shard_map/ppermute | solution.py:60
  5.2 5.8 %collective-permute-start.1 = (f32[120,256]{1,0:T(8,128)S(1)}, f32[120,256]{1,0:T(8,128)S(1)}, u32[]{:S(2)}, u32[]{:S(2)}) collective-permute-start(f32[120,256]{1,0:T(8,128)S(1)} %get-tuple-element.52), channel_id=1, source_target_pairs={{0,8},{1,9},{2,10},{3,11},{4,12},{5,13},{6,14},{7,15},{8,0},{9,1},... | collective-permute-start | bytes 368648 | tf_op jit(solution)/shard_map/ppermute | solution.py:60
  5.3 3.4 %collective-permute-start = (f32[96,256]{1,0:T(8,128)S(1)}, f32[96,256]{1,0:T(8,128)S(1)}, u32[]{:S(2)}, u32[]{:S(2)}) collective-permute-start(f32[96,256]{1,0:T(8,128)S(1)} %get-tuple-element.51), channel_id=1, source_target_pairs={{0,1},{1,0},{2,3},{3,2},{4,5},{5,4},{6,7},{7,6},{8,9},{9,8},{10,11... | collective-permute-start | bytes 294920 | tf_op jit(solution)/shard_map/ppermute | solution.py:60
  6.6 5.0 %collective-permute-start.4 = (f32[3,24,256]{2,1,0:T(8,128)S(1)}, f32[3,24,256]{2,1,0:T(8,128)S(1)}, u32[]{:S(2)}, u32[]{:S(2)}) collective-permute-start(f32[3,24,256]{2,1,0:T(8,128)S(1)} %get-tuple-element.58), channel_id=1, source_target_pairs={{0,1},{1,0},{2,3},{3,2},{4,5},{5,4},{6,7},{7,6},{8,9},{9,8},{10,11... | collective-permute-start | bytes 221192 | tf_op jit(solution)/shard_map/ppermute | solution.py:60
  6.7 4.9 %collective-permute-start.5 = (f32[2,24,256]{2,1,0:T(8,128)S(1)}, f32[2,24,256]{2,1,0:T(8,128)S(1)}, u32[]{:S(2)}, u32[]{:S(2)}) collective-permute-start(f32[2,24,256]{2,1,0:T(8,128)S(1)} %get-tuple-element.59), channel_id=1, source_target_pairs={{0,8},{1,2},{2,1},{3,4},{4,3},{5,6},{6,5},{7,15},{8,0},{9,10},{10,... | collective-permute-start | bytes 147464 | tf_op jit(solution)/shard_map/ppermute | solution.py:60
  8.7 3.4 %collective-permute-start.6 = (f32[24,256]{1,0:T(8,128)S(1)}, f32[24,256]{1,0:T(8,128)S(1)}, u32[]{:S(2)}, u32[]{:S(2)}) collective-permute-start(f32[24,256]{1,0:T(8,128)S(1)} %get-tuple-element.66), channel_id=1, source_target_pairs={{0,1},{1,0},{2,3},{3,2},{4,5},{5,4},{6,7},{7,6},{8,16},{9,17},{10,... | collective-permute-start | bytes 73736 | tf_op jit(solution)/shard_map/ppermute | solution.py:60
  12.4 4.2 %collective-permute-start.7 = (f32[2,24,256]{2,1,0:T(8,128)S(1)}, f32[2,24,256]{2,1,0:T(8,128)S(1)}, u32[]{:S(2)}, u32[]{:S(2)}) collective-permute-start(f32[2,24,256]{2,1,0:T(8,128)S(1)} %get-tuple-element.73), channel_id=1, source_target_pairs={{0,1},{1,0},{2,3},{3,2},{4,5},{5,4},{6,7},{7,6},{8,9},{9,8},{10,11... | collective-permute-start | bytes 147464 | tf_op jit(solution)/shard_map/ppermute | solution.py:60
  12.5 4.2 %collective-permute-start.8 = (f32[2,24,256]{2,1,0:T(8,128)S(1)}, f32[2,24,256]{2,1,0:T(8,128)S(1)}, u32[]{:S(2)}, u32[]{:S(2)}) collective-permute-start(f32[2,24,256]{2,1,0:T(8,128)S(1)} %get-tuple-element.74), channel_id=1, source_target_pairs={{0,8},{1,2},{2,1},{3,4},{4,3},{5,6},{6,5},{7,15},{8,0},{9,10},{10,... | collective-permute-start | bytes 147464 | tf_op jit(solution)/shard_map/ppermute | solution.py:60
  14.1 3.8 %collective-permute-start.9 = (f32[24,256]{1,0:T(8,128)S(1)}, f32[24,256]{1,0:T(8,128)S(1)}, u32[]{:S(2)}, u32[]{:S(2)}) collective-permute-start(f32[24,256]{1,0:T(8,128)S(1)} %get-tuple-element.75), channel_id=1, source_target_pairs={{0,8},{1,9},{2,10},{3,11},{4,5},{5,4},{6,7},{7,6},{8,0},{9,1},{10,... | collective-permute-start | bytes 73736 | tf_op jit(solution)/shard_map/ppermute | solution.py:60
  14.6 3.3 %collective-permute-start.10 = (f32[24,256]{1,0:T(8,128)S(1)}, f32[24,256]{1,0:T(8,128)S(1)}, u32[]{:S(2)}, u32[]{:S(2)}) collective-permute-start(f32[24,256]{1,0:T(8,128)S(1)} %get-tuple-element.76), channel_id=1, source_target_pairs={{0,1},{1,0},{2,3},{3,2},{4,12},{5,13},{6,14},{7,15},{8,16},{9,17},... | collective-permute-start | bytes 73736 | tf_op jit(solution)/shard_map/ppermute | solution.py:60

commit v7 on v6

--- a/solution.py
+++ b/solution.py
@@ -216,7 +216,8 @@
     return jnp.where((turn > 2) & (turn < 6), -size, size)
 
 
-def plan_kernel(neighbors, orient, scale, select, turns):
+def plan_kernel(neighbors, orient, sent, scale, select, turns):
+    del sent
     shape = (ROWS, HALF)
     slot, field, column = iota(shape, 0) % SLOTS, iota(shape, 0) // SLOTS, iota(shape, 1)
     grp, dev = lax.axis_index("grp"), lax.axis_index("dev")
@@ -259,21 +260,17 @@
             select[face // 2, rows, pl.ds(part * SOURCES * ROWS, SOURCES * ROWS)] = chosen
 
 
-def start_kernel(fields, neighbors, orient, *refs):
-    fetched, low, high, faces_grp, faces_dev, scale, select, turns = refs[:8]
-    state, near, turn, arrived = refs[8:]
-    scalars = ((neighbors, near), (orient, turn))
+def start_kernel(fields, fetched, low, high, faces_grp, faces_dev, state, arrived):
     parts = [pl.ds(first, EDGE // 2) for first in (0, EDGE // 2)]
-    blocks = tuple((fields.at[:, :, part], fetched.at[:, :, part]) for part in parts)
-    copies = [pltpu.make_async_copy(*pair, arrived.at[number]) for number, pair in enumerate((*scalars, *blocks))]
+    copies = [
+        pltpu.make_async_copy(fields.at[:, :, part], fetched.at[:, :, part], arrived.at[number])
+        for number, part in enumerate(parts)
+    ]
     for copy in copies:
         copy.start()
-    for copy in copies[: len(scalars)]:
-        copy.wait()
-    plan_kernel(near, turn, scale, select, turns)
     packer = Packer()
     for number, part in enumerate(parts):
-        copies[len(scalars) + number].wait()
+        copies[number].wait()
         first = number * (EDGE // 2)
         for slot in range(SLOTS):
             fill_slot(state, slot, lambda f: fetched[slot, f, part], first, EDGE // 2)
@@ -546,21 +543,29 @@
     )(*vectors)
 
 
-def start(arguments):
-    shapes = (arguments[0].shape, SIDE, SIDE, EARLY, EARLY, (4, ROWS, HALF), SELECT, TURNS)
+def start(fields):
+    shapes = (fields.shape, SIDE, SIDE, EARLY, EARLY)
     return pl.pallas_call(
         start_kernel,
         name="start",
         compiler_params=SMALL,
         out_shape=[shaped(shape) for shape in shapes],
-        in_specs=[spec(pl.ANY)] * len(arguments),
+        in_specs=[spec(pl.ANY)],
         out_specs=[spec(VECTOR)] * len(shapes),
-        scratch_shapes=[
-            pltpu.VMEM(SPARE, jnp.float32),
-            *(pltpu.SMEM(array.shape, jnp.int32) for array in arguments[1:]),
-            pltpu.SemaphoreType.DMA((len(arguments) + 1,)),
-        ],
-    )(*(pltpu.with_memory_space_constraint(array, pltpu.HBM) for array in arguments))
+        scratch_shapes=[pltpu.VMEM(SPARE, jnp.float32), pltpu.SemaphoreType.DMA((2,))],
+    )(pltpu.with_memory_space_constraint(fields, pltpu.HBM))
+
+
+def plan(neighbors, orient, sent):
+    return pl.pallas_call(
+        plan_kernel,
+        name="plan",
+        compiler_params=SMALL,
+        out_shape=[shaped((4, ROWS, HALF)), shaped(SELECT), shaped(TURNS)],
+        in_specs=[spec(pltpu.SMEM)] * 2 + [spec(VECTOR)],
+        out_specs=[spec(VECTOR)] * 3,
+        cost_estimate=cost(1 << 20),
+    )(neighbors, orient, sent)
 
 
 def mask(flag):
@@ -568,7 +573,7 @@
 
 
 def body(fields, swap_dev, swap_grp, neighbors, orient):
-    fields, low, high, faces, faces_dev, scale, select, turns = start((fields, neighbors, orient))
+    fields, low, high, faces, faces_dev = start(fields)
     swap_dev, faces = lax.optimization_barrier((swap_dev, faces))
     faces = exchange(faces, "grp", 0)
     faces_dev = exchange(faces_dev, "dev", 0)
@@ -588,6 +593,7 @@
     flat_a = exchange(sends[0], "dev", 0)
     flat_b = exchange(sends[1], "dev", 1)
     deep_b = exchange(sends[2], "grp", 1)
+    scale, select, turns = plan(neighbors, orient, sends[2])
     partial, deep_a, relayed, z_low, z_high = call(
         first_inner_kernel,
         "inner_0",

time: 19.1 us -> 19.2 us (level)
  Pallas kernels: 5.02 us -> 5.77 us
  waiting for transfers between devices: 3.15 us -> 2.49 us
    pallas_call x0 -> x1, Pallas kernels: none -> 0.76 us  [plan(): pl.pallas_call(plan_kernel, name='plan', compiler_params=SMALL, out_shape...]
    ppermute x11, waiting for transfers between devices: 3.15 us -> 2.49 us  [exchange(): return lax.ppermute(block, ('grp', 'dev'), partners(axis, offset))]
  transfers between devices with their start and end apart: 11 -> 11, of which waited for: 2 -> 2; matrix products, arithmetic and copies ran while one was open for 0% -> 0% of each run, Pallas kernels for 13% -> 17%
where the time goes in v7:
time: 19.2 us; the launch traced here: 19 us
  starting transfers between devices  9.26 us (48%)
  Pallas kernels  5.77 us (30%)
  waiting for transfers between devices  2.49 us (13%)
  between operations  1.46 us (8%)
    ppermute x11, starting transfers between devices, exchange(): return lax.ppermute(block, ('grp', 'dev'), partners(axis, offset))  9.26 us
    pallas_call x7, Pallas kernels, call(): pl.pallas_call(kernel, name=name, compiler_params=SMALL, out_shape=[shape...  2.66 us
    ppermute x11, waiting for transfers between devices, exchange(): return lax.ppermute(block, ('grp', 'dev'), partners(axis, offset))  2.49 us
    pallas_call x1, Pallas kernels, start(): pl.pallas_call(start_kernel, name='start', compiler_params=SMALL, out_sha...  1.36 us
    pallas_call x1, Pallas kernels, body(): pl.pallas_call(last_kernel, name='finish_1', compiler_params=SMALL, out_s...  0.99 us
    pallas_call x1, Pallas kernels, plan(): pl.pallas_call(plan_kernel, name='plan', compiler_params=SMALL, out_shape...  0.76 us
  transfers between devices with their start and end apart: 11, of which 2 were waited for; matrix products, arithmetic and copies ran while one was open for 0% of the time, Pallas kernels for 17%

profile of v7, /device:TPU:0, one launch (start us, length us, event | category | flops | bytes accessed | tf_op | source)
XLA Modules:
  0.0 19.0 jit_solution(9626749240985236461)
XLA Ops:
  0.0 1.4 %start.1 = (f32[4,6,16,256]{3,2,1,0:T(8,128)S(1)}, f32[3,24,256]{2,1,0:T(8,128)S(1)}, f32[3,24,256]{2,1,0:T(8,128)S(1)}, f32[40,256]{1,0:T(8,128)S(1)}, f32[40,256]{1,0:T(8,128)S(1)}) custom-call(f32[4,6,16,256]{3,2,1,0:T(8,128)} %fields.1), custom_call_target="tpu_custom_call" | custom-call | tf_op jit(solution)/shard_map/start/pallas_call | solution.py:548
  1.4 3.1 %collective-permute-start = (f32[40,256]{1,0:T(8,128)S(1)}, f32[40,256]{1,0:T(8,128)S(1)}, u32[]{:S(2)}, u32[]{:S(2)}) collective-permute-start(f32[40,256]{1,0:T(8,128)S(1)} %get-tuple-element.48), channel_id=1, source_target_pairs={{0,8},{1,9},{2,10},{3,11},{4,12},{5,13},{6,14},{7,15},{8,0},{9,1},... | collective-permute-start | bytes 122888 | tf_op jit(solution)/shard_map/ppermute | solution.py:60
  4.5 0.0 collective-permute-start.1
  5.2 0.1 collective-permute-start.3
  5.3 0.5 %collective-permute-start.2 = (f32[96,256]{1,0:T(8,128)S(1)}, f32[96,256]{1,0:T(8,128)S(1)}, u32[]{:S(2)}, u32[]{:S(2)}) collective-permute-start(f32[96,256]{1,0:T(8,128)S(1)} %get-tuple-element.54), channel_id=1, source_target_pairs={{0,1},{1,0},{2,3},{3,2},{4,5},{5,4},{6,7},{7,6},{8,9},{9,8},{10,11... | collective-permute-start | bytes 294920 | tf_op jit(solution)/shard_map/ppermute | solution.py:60
  6.5 0.0 collective-permute-done.faces
  6.5 0.0 collective-permute-done.1.faces_dev
  6.5 0.1 faces.1
  6.6 0.0 copy-start
  6.6 0.1 collective-permute-start.4
  6.6 0.0 copy-start.1
  6.7 2.0 %collective-permute-start.5 = (f32[2,24,256]{2,1,0:T(8,128)S(1)}, f32[2,24,256]{2,1,0:T(8,128)S(1)}, u32[]{:S(2)}, u32[]{:S(2)}) collective-permute-start(f32[2,24,256]{2,1,0:T(8,128)S(1)} %get-tuple-element.60), channel_id=1, source_target_pairs={{0,8},{1,2},{2,1},{3,4},{4,3},{5,6},{6,5},{7,15},{8,0},{9,10},{10,... | collective-permute-start | bytes 147464 | tf_op jit(solution)/shard_map/ppermute | solution.py:60
  8.7 0.0 collective-permute-start.6
  8.7 0.0 copy-done
  8.7 0.0 copy-done.1
  8.7 0.8 %plan.1 = (f32[4,24,128]{2,1,0:T(8,128)S(1)}, f32[2,48,192]{2,1,0:T(8,128)S(1)}, f32[2,8,24,128]{3,2,1,0:T(8,128)S(1)}) custom-call(s32[4,6]{1,0:T(4,128)S(1)} %copy-done, s32[4]{0:T(128)S(1)} %copy-done.1, f32[24,256]{1,0:T(8,128)S(1)} %get-tuple-element.50.sent), custom_call_target="tpu_custom_call" | custom-call | flops 1048576 | bytes 1048576 | tf_op jit(solution)/shard_map/plan/pallas_call | solution.py:560
  9.5 0.0 collective-permute-done.2.block_dev
  9.5 1.5 %collective-permute-done.3.block_grp = f32[120,256]{1,0:T(8,128)S(1)} collective-permute-done((f32[120,256]{1,0:T(8,128)S(1)}, f32[120,256]{1,0:T(8,128)S(1)}, u32[]{:S(2)}, u32[]{:S(2)}) %collective-permute-start.3) | collective-permute-done | bytes 122912 | tf_op jit(solution)/shard_map/ppermute | solution.py:60
  11.0 0.5 %inner_0.1 = (f32[2,384,128]{2,1,0:T(8,128)S(1)}, f32[24,256]{1,0:T(8,128)S(1)}, f32[24,256]{1,0:T(8,128)S(1)}, f32[24,256]{1,0:T(8,128)S(1)}, f32[24,256]{1,0:T(8,128)S(1)}) custom-call(f32[24,256]{1,0:T(8,128)S(1)} %broadcast_in_dim.21.mask_dev, f32[24,256]{1,0:T(8,128)S(1)} %broadcast_in_dim.23.mask_grp, f32[4,24,128]{2,1,0:T(8,128)S(1)} %get-tuple-element.52.scale, ...), custom_call_target="tpu_custom_call" | custom-call | flops 4194304 | bytes 2097152 | tf_op jit(solution)/shard_map/inner_0/pallas_call | solution.py:534
  11.5 0.0 collective-permute-done.5.flat_b
  11.5 0.0 collective-permute-done.4.flat_a.refs_6_
  11.5 0.6 %sides_0.1 = (f32[2,384,128]{2,1,0:T(8,128)S(1)}, f32[24,256]{1,0:T(8,128)S(1)}, f32[24,256]{1,0:T(8,128)S(1)}, f32[24,256]{1,0:T(8,128)S(1)}, f32[24,256]{1,0:T(8,128)S(1)}) custom-call(f32[4,24,128]{2,1,0:T(8,128)S(1)} %get-tuple-element.52.scale, f32[2,48,192]{2,1,0:T(8,128)S(1)} %get-tuple-element.53.select, ...), custom_call_target="tpu_custom_call" | custom-call | flops 1048576 | bytes 1048576 | tf_op jit(solution)/shard_map/sides_0/pallas_call | solution.py:534
  12.1 0.0 collective-permute-done.6.refs_5_
  12.1 0.3 %finish_0.1 = (f32[3,24,256]{2,1,0:T(8,128)S(1)}, f32[3,24,256]{2,1,0:T(8,128)S(1)}, f32[2,24,256]{2,1,0:T(8,128)S(1)}, f32[2,24,256]{2,1,0:T(8,128)S(1)}, f32[2...) custom-call(f32[2,8,24,128]{3,2,1,0:T(8,128)S(1)} %get-tuple-element.51.turns, ...), custom_call_target="tpu_custom_call" | custom-call | flops 1048576 | bytes 1048576 | tf_op jit(solution)/shard_map/finish_0/pallas_call | solution.py:534
  12.4 0.1 collective-permute-start.7
  12.4 1.7 %collective-permute-start.8 = (f32[2,24,256]{2,1,0:T(8,128)S(1)}, f32[2,24,256]{2,1,0:T(8,128)S(1)}, u32[]{:S(2)}, u32[]{:S(2)}) collective-permute-start(f32[2,24,256]{2,1,0:T(8,128)S(1)} %get-tuple-element.74), channel_id=1, source_target_pairs={{0,8},{1,2},{2,1},{3,4},{4,3},{5,6},{6,5},{7,15},{8,0},{9,10},{10,... | collective-permute-start | bytes 147464 | tf_op jit(solution)/shard_map/ppermute | solution.py:60
  14.2 0.4 %collective-permute-start.9 = (f32[24,256]{1,0:T(8,128)S(1)}, f32[24,256]{1,0:T(8,128)S(1)}, u32[]{:S(2)}, u32[]{:S(2)}) collective-permute-start(f32[24,256]{1,0:T(8,128)S(1)} %get-tuple-element.75), channel_id=1, source_target_pairs={{0,8},{1,9},{2,10},{3,11},{4,5},{5,4},{6,7},{7,6},{8,0},{9,1},{10,... | collective-permute-start | bytes 73736 | tf_op jit(solution)/shard_map/ppermute | solution.py:60
  14.5 1.2 %collective-permute-start.10 = (f32[24,256]{1,0:T(8,128)S(1)}, f32[24,256]{1,0:T(8,128)S(1)}, u32[]{:S(2)}, u32[]{:S(2)}) collective-permute-start(f32[24,256]{1,0:T(8,128)S(1)} %get-tuple-element.76), channel_id=1, source_target_pairs={{0,1},{1,0},{2,3},{3,2},{4,12},{5,13},{6,14},{7,15},{8,16},{9,17},... | collective-permute-start | bytes 73736 | tf_op jit(solution)/shard_map/ppermute | solution.py:60
  15.8 0.8 %inner_1.1.partial = f32[2,384,128]{2,1,0:T(8,128)S(1)} custom-call(f32[2,384,128]{2,1,0:T(8,128)S(1)} %get-tuple-element.61.partial.state, f32[2,24,256]{2,1,0:T(8,128)S(1)} %get-tuple-element.70.ghosts, f32[4,24,128]{2,1,0:T(8,128)S(1)} %get-tuple-element.52.scale), custom_call_target="tpu_custom_call" | custom-call | flops 4194304 | bytes 2097152 | tf_op jit(solution)/shard_map/inner_1/pallas_call | solution.py:534
  16.6 0.0 collective-permute-done.7.flat_a
  16.6 0.0 collective-permute-done.8.flat_b
  16.6 0.4 %sides_1.1.partial = f32[4,6,16,256]{3,2,1,0:T(8,128)S(1)} custom-call(f32[4,24,128]{2,1,0:T(8,128)S(1)} %get-tuple-element.52.scale, f32[2,48,192]{2,1,0:T(8,128)S(1)} %get-tuple-element.53.select, f32[2,384,128]{2,1,0:T(8,128)S(1)} %inner_1.1.partial, f32[3,24,256]{2,1,0:T(8,128)S(1)} %get-tuple-element.71.low, f32[3,24,256]{2,1,0:T(8,128)S(1)} %get-tuple-element.72.high, ...), custom_call_target="tpu_custom_call" | custom-call | flops 1048576 | bytes 1048576 | tf_op jit(solution)/shard_map/sides_1/pallas_call | solution.py:534
  17.0 1.0 %collective-permute-done.9.deep_first = f32[24,256]{1,0:T(8,128)S(1)} collective-permute-done((f32[24,256]{1,0:T(8,128)S(1)}, f32[24,256]{1,0:T(8,128)S(1)}, u32[]{:S(2)}, u32[]{:S(2)}) %collective-permute-start.9) | collective-permute-done | bytes 24608 | tf_op jit(solution)/shard_map/ppermute | solution.py:60
  18.0 0.0 collective-permute-done.10.deep_second
  18.0 1.0 %finish_1.1 = f32[4,6,16,256]{3,2,1,0:T(8,128)} custom-call(f32[2,8,24,128]{3,2,1,0:T(8,128)S(1)} %get-tuple-element.51.turns, f32[4,6,16,256]{3,2,1,0:T(8,128)S(1)} %sides_1.1.partial, f32[3,24,256]{2,1,0:T(8,128)S(1)} %get-tuple-element.71.low, f32[3,24,256]{2,1,0:T(8,128)S(1)} %get-tuple-element.72.high, f32[24,256]{1,0:T(8,128)S(1)} %collective-permute-done.9.deep_first, ...), custom_call_target="tpu_custom_call" | custom-call | tf_op jit(solution)/shard_map/finish_1/pallas_call | solution.py:630
  (3 shorter events, 0.0 us)
Async XLA Ops:
  1.4 5.1 %collective-permute-start = (f32[40,256]{1,0:T(8,128)S(1)}, f32[40,256]{1,0:T(8,128)S(1)}, u32[]{:S(2)}, u32[]{:S(2)}) collective-permute-start(f32[40,256]{1,0:T(8,128)S(1)} %get-tuple-element.48), channel_id=1, source_target_pairs={{0,8},{1,9},{2,10},{3,11},{4,12},{5,13},{6,14},{7,15},{8,0},{9,1},... | collective-permute-start | bytes 122888 | tf_op jit(solution)/shard_map/ppermute | solution.py:60
  4.5 2.0 %collective-permute-start.1 = (f32[40,256]{1,0:T(8,128)S(1)}, f32[40,256]{1,0:T(8,128)S(1)}, u32[]{:S(2)}, u32[]{:S(2)}) collective-permute-start(f32[40,256]{1,0:T(8,128)S(1)} %get-tuple-element.49), channel_id=1, source_target_pairs={{0,1},{1,0},{2,3},{3,2},{4,5},{5,4},{6,7},{7,6},{8,9},{9,8},{10,11... | collective-permute-start | bytes 122888 | tf_op jit(solution)/shard_map/ppermute | solution.py:60
  5.2 5.8 %collective-permute-start.3 = (f32[120,256]{1,0:T(8,128)S(1)}, f32[120,256]{1,0:T(8,128)S(1)}, u32[]{:S(2)}, u32[]{:S(2)}) collective-permute-start(f32[120,256]{1,0:T(8,128)S(1)} %get-tuple-element.55), channel_id=1, source_target_pairs={{0,8},{1,9},{2,10},{3,11},{4,12},{5,13},{6,14},{7,15},{8,0},{9,1},... | collective-permute-start | bytes 368648 | tf_op jit(solution)/shard_map/ppermute | solution.py:60
  5.3 4.2 %collective-permute-start.2 = (f32[96,256]{1,0:T(8,128)S(1)}, f32[96,256]{1,0:T(8,128)S(1)}, u32[]{:S(2)}, u32[]{:S(2)}) collective-permute-start(f32[96,256]{1,0:T(8,128)S(1)} %get-tuple-element.54), channel_id=1, source_target_pairs={{0,1},{1,0},{2,3},{3,2},{4,5},{5,4},{6,7},{7,6},{8,9},{9,8},{10,11... | collective-permute-start | bytes 294920 | tf_op jit(solution)/shard_map/ppermute | solution.py:60
  6.6 2.2 %copy-start = (s32[4,6]{1,0:T(4,128)S(1)}, s32[4,6]{1,0:T(4,128)}, u32[]{:S(2)}) copy-start(s32[4,6]{1,0:T(4,128)} %neighbors.1) | copy-start | bytes 292
  6.6 5.0 %collective-permute-start.4 = (f32[3,24,256]{2,1,0:T(8,128)S(1)}, f32[3,24,256]{2,1,0:T(8,128)S(1)}, u32[]{:S(2)}, u32[]{:S(2)}) collective-permute-start(f32[3,24,256]{2,1,0:T(8,128)S(1)} %get-tuple-element.59), channel_id=1, source_target_pairs={{0,1},{1,0},{2,3},{3,2},{4,5},{5,4},{6,7},{7,6},{8,9},{9,8},{10,11... | collective-permute-start | bytes 221192 | tf_op jit(solution)/shard_map/ppermute | solution.py:60
  6.6 2.1 %copy-start.1 = (s32[4]{0:T(128)S(1)}, s32[4]{0:T(128)}, u32[]{:S(2)}) copy-start(s32[4]{0:T(128)} %orient.1) | copy-start | bytes 52
  6.7 4.9 %collective-permute-start.5 = (f32[2,24,256]{2,1,0:T(8,128)S(1)}, f32[2,24,256]{2,1,0:T(8,128)S(1)}, u32[]{:S(2)}, u32[]{:S(2)}) collective-permute-start(f32[2,24,256]{2,1,0:T(8,128)S(1)} %get-tuple-element.60), channel_id=1, source_target_pairs={{0,8},{1,2},{2,1},{3,4},{4,3},{5,6},{6,5},{7,15},{8,0},{9,10},{10,... | collective-permute-start | bytes 147464 | tf_op jit(solution)/shard_map/ppermute | solution.py:60
  8.7 3.4 %collective-permute-start.6 = (f32[24,256]{1,0:T(8,128)S(1)}, f32[24,256]{1,0:T(8,128)S(1)}, u32[]{:S(2)}, u32[]{:S(2)}) collective-permute-start(f32[24,256]{1,0:T(8,128)S(1)} %get-tuple-element.50.sent), channel_id=1, source_target_pairs={{0,1},{1,0},{2,3},{3,2},{4,5},{5,4},{6,7},{7,6},{8,16},{9,17},{10,... | collective-permute-start | bytes 73736 | tf_op jit(solution)/shard_map/ppermute | solution.py:60
  12.4 4.2 %collective-permute-start.7 = (f32[2,24,256]{2,1,0:T(8,128)S(1)}, f32[2,24,256]{2,1,0:T(8,128)S(1)}, u32[]{:S(2)}, u32[]{:S(2)}) collective-permute-start(f32[2,24,256]{2,1,0:T(8,128)S(1)} %get-tuple-element.73), channel_id=1, source_target_pairs={{0,1},{1,0},{2,3},{3,2},{4,5},{5,4},{6,7},{7,6},{8,9},{9,8},{10,11... | collective-permute-start | bytes 147464 | tf_op jit(solution)/shard_map/ppermute | solution.py:60
  12.4 4.2 %collective-permute-start.8 = (f32[2,24,256]{2,1,0:T(8,128)S(1)}, f32[2,24,256]{2,1,0:T(8,128)S(1)}, u32[]{:S(2)}, u32[]{:S(2)}) collective-permute-start(f32[2,24,256]{2,1,0:T(8,128)S(1)} %get-tuple-element.74), channel_id=1, source_target_pairs={{0,8},{1,2},{2,1},{3,4},{4,3},{5,6},{6,5},{7,15},{8,0},{9,10},{10,... | collective-permute-start | bytes 147464 | tf_op jit(solution)/shard_map/ppermute | solution.py:60
  14.2 3.8 %collective-permute-start.9 = (f32[24,256]{1,0:T(8,128)S(1)}, f32[24,256]{1,0:T(8,128)S(1)}, u32[]{:S(2)}, u32[]{:S(2)}) collective-permute-start(f32[24,256]{1,0:T(8,128)S(1)} %get-tuple-element.75), channel_id=1, source_target_pairs={{0,8},{1,9},{2,10},{3,11},{4,5},{5,4},{6,7},{7,6},{8,0},{9,1},{10,... | collective-permute-start | bytes 73736 | tf_op jit(solution)/shard_map/ppermute | solution.py:60
  14.5 3.5 %collective-permute-start.10 = (f32[24,256]{1,0:T(8,128)S(1)}, f32[24,256]{1,0:T(8,128)S(1)}, u32[]{:S(2)}, u32[]{:S(2)}) collective-permute-start(f32[24,256]{1,0:T(8,128)S(1)} %get-tuple-element.76), channel_id=1, source_target_pairs={{0,1},{1,0},{2,3},{3,2},{4,12},{5,13},{6,14},{7,15},{8,16},{9,17},... | collective-permute-start | bytes 73736 | tf_op jit(solution)/shard_map/ppermute | solution.py:60

commit v8 on v6

--- a/solution.py
+++ b/solution.py
@@ -462,14 +462,14 @@
     pairs = z_pairs(*both)
     lane = iota((ROWS, HALF), 1)
     ends, group = ends_of((ROWS, HALF)), lane // EDGE
+    made = [[], []]
     for side, ref in enumerate((low, high)):
         ghosts[side] = both[side]
+        x_halves, y_halves = [], []
         x = side * (EDGE - 1)
         at = EDGE - 1 - x
         for h, half in enumerate(plane_at(partial, x)):
-            lanes = slice(h * HALF, (h + 1) * HALF)
-            ref[0, :, lanes] = half + jnp.where(ends, turned(pairs[h][at % 2], -at), 0.0)
-        ref[2] = packed_z[side][...] + both[side]
+            x_halves.append(half + jnp.where(ends, turned(pairs[h][at % 2], -at), 0.0))
         for h in range(2):
             total = jnp.zeros((ROWS, HALF), jnp.float32)
             for number in range(GROUPS):
@@ -477,8 +477,12 @@
                 moved = turned(pairs[side][at % 2], EDGE * number - at - side * (HALF - EDGE))
                 total = jnp.where(ends & (group == number), moved, total)
             lanes = slice(h * HALF, (h + 1) * HALF)
-            ref[1, :, lanes] = packed_y[side][:, lanes] + total
-    emit_faces((low, high), sends)
+            y_halves.append(packed_y[side][:, lanes] + total)
+        z_face = packed_z[side][...] + both[side]
+        made[side] = [jnp.concatenate(x_halves, axis=1), jnp.concatenate(y_halves, axis=1), z_face]
+        for axis in range(3):
+            ref[axis] = made[side][axis]
+    emit_faces(made, sends)
 
 
 def finish_0_kernel(turns, partial, *refs):

time: 19.1 us -> 19.1 us (level)
  no operation moved by 1% of the time
where the time goes in v8:
time: 19.1 us; the launch traced here: 18.9 us
  starting transfers between devices  9.24 us (48%)
  Pallas kernels  5.02 us (26%)
  waiting for transfers between devices  3.15 us (16%)
  between operations  1.44 us (8%)
    ppermute x11, starting transfers between devices, exchange(): return lax.ppermute(block, ('grp', 'dev'), partners(axis, offset))  9.24 us
    ppermute x11, waiting for transfers between devices, exchange(): return lax.ppermute(block, ('grp', 'dev'), partners(axis, offset))  3.15 us
    pallas_call x7, Pallas kernels, call(): pl.pallas_call(kernel, name=name, compiler_params=SMALL, out_shape=[shape...  2.66 us
    pallas_call x1, Pallas kernels, start(): pl.pallas_call(start_kernel, name='start', compiler_params=SMALL, out_sha...  1.38 us
    pallas_call x1, Pallas kernels, body(): pl.pallas_call(last_kernel, name='finish_1', compiler_params=SMALL, out_s...  0.99 us
  transfers between devices with their start and end apart: 11, of which 2 were waited for; matrix products, arithmetic and copies ran while one was open for 0% of the time, Pallas kernels for 13%

profile of v8, /device:TPU:0, one launch (start us, length us, event | category | flops | bytes accessed | tf_op | source)
XLA Modules:
  0.0 18.9 jit_solution(8570436255062168096)
XLA Ops:
  0.0 1.4 %start.1 = (f32[4,6,16,256]{3,2,1,0:T(8,128)S(1)}, f32[3,24,256]{2,1,0:T(8,128)S(1)}, f32[3,24,256]{2,1,0:T(8,128)S(1)}, f32[40,256]{1,0:T(8,128)S(1)}, f32[40,2...) custom-call(f32[4,6,16,256]{3,2,1,0:T(8,128)} %fields.1, ...), custom_call_target="tpu_custom_call" | custom-call | tf_op jit(solution)/shard_map/start/pallas_call | solution.py:555
  1.4 3.1 %collective-permute-start.2 = (f32[40,256]{1,0:T(8,128)S(1)}, f32[40,256]{1,0:T(8,128)S(1)}, u32[]{:S(2)}, u32[]{:S(2)}) collective-permute-start(f32[40,256]{1,0:T(8,128)S(1)} %get-tuple-element.53), channel_id=1, source_target_pairs={{0,8},{1,9},{2,10},{3,11},{4,12},{5,13},{6,14},{7,15},{8,0},{9,1},... | collective-permute-start | bytes 122888 | tf_op jit(solution)/shard_map/ppermute | solution.py:60
  4.5 0.0 collective-permute-start.3
  5.2 0.1 collective-permute-start.1
  5.3 0.5 %collective-permute-start = (f32[96,256]{1,0:T(8,128)S(1)}, f32[96,256]{1,0:T(8,128)S(1)}, u32[]{:S(2)}, u32[]{:S(2)}) collective-permute-start(f32[96,256]{1,0:T(8,128)S(1)} %get-tuple-element.51), channel_id=1, source_target_pairs={{0,1},{1,0},{2,3},{3,2},{4,5},{5,4},{6,7},{7,6},{8,9},{9,8},{10,11... | collective-permute-start | bytes 294920 | tf_op jit(solution)/shard_map/ppermute | solution.py:60
  6.5 0.0 collective-permute-done.2.faces
  6.5 0.0 collective-permute-done.3.faces_dev
  6.5 0.1 faces.1
  6.6 0.1 collective-permute-start.4
  6.7 2.0 %collective-permute-start.5 = (f32[2,24,256]{2,1,0:T(8,128)S(1)}, f32[2,24,256]{2,1,0:T(8,128)S(1)}, u32[]{:S(2)}, u32[]{:S(2)}) collective-permute-start(f32[2,24,256]{2,1,0:T(8,128)S(1)} %get-tuple-element.59), channel_id=1, source_target_pairs={{0,8},{1,2},{2,1},{3,4},{4,3},{5,6},{6,5},{7,15},{8,0},{9,10},{10,... | collective-permute-start | bytes 147464 | tf_op jit(solution)/shard_map/ppermute | solution.py:60
  8.7 0.0 collective-permute-start.6
  8.7 0.0 collective-permute-done.block_dev
  8.7 2.3 %collective-permute-done.1.block_grp = f32[120,256]{1,0:T(8,128)S(1)} collective-permute-done((f32[120,256]{1,0:T(8,128)S(1)}, f32[120,256]{1,0:T(8,128)S(1)}, u32[]{:S(2)}, u32[]{:S(2)}) %collective-permute-start.1) | collective-permute-done | bytes 122912 | tf_op jit(solution)/shard_map/ppermute | solution.py:60
  11.0 0.5 %inner_0.1 = (f32[2,384,128]{2,1,0:T(8,128)S(1)}, f32[24,256]{1,0:T(8,128)S(1)}, f32[24,256]{1,0:T(8,128)S(1)}, f32[24,256]{1,0:T(8,128)S(1)}, f32[24,256]{1,0:T(8,128)S(1)}) custom-call(f32[24,256]{1,0:T(8,128)S(1)} %broadcast_in_dim.21.mask_dev, f32[24,256]{1,0:T(8,128)S(1)} %broadcast_in_dim.23.mask_grp, f32[4,24,128]{2,1,0:T(8,128)S(1)} %get-tuple-element.42.scale, ...), custom_call_target="tpu_custom_call" | custom-call | flops 4194304 | bytes 2097152 | tf_op jit(solution)/shard_map/inner_0/pallas_call | solution.py:541
  11.5 0.0 collective-permute-done.5.flat_b
  11.5 0.0 collective-permute-done.4.flat_a.refs_6_
  11.5 0.6 %sides_0.1 = (f32[2,384,128]{2,1,0:T(8,128)S(1)}, f32[24,256]{1,0:T(8,128)S(1)}, f32[24,256]{1,0:T(8,128)S(1)}, f32[24,256]{1,0:T(8,128)S(1)}, f32[24,256]{1,0:T(8,128)S(1)}) custom-call(f32[4,24,128]{2,1,0:T(8,128)S(1)} %get-tuple-element.42.scale, f32[2,48,192]{2,1,0:T(8,128)S(1)} %get-tuple-element.43.select, ...), custom_call_target="tpu_custom_call" | custom-call | flops 1048576 | bytes 1048576 | tf_op jit(solution)/shard_map/sides_0/pallas_call | solution.py:541
  12.1 0.0 collective-permute-done.6.refs_5_
  12.1 0.3 %finish_0.1 = (f32[3,24,256]{2,1,0:T(8,128)S(1)}, f32[3,24,256]{2,1,0:T(8,128)S(1)}, f32[2,24,256]{2,1,0:T(8,128)S(1)}, f32[2,24,256]{2,1,0:T(8,128)S(1)}, f32[2...) custom-call(f32[2,8,24,128]{3,2,1,0:T(8,128)S(1)} %get-tuple-element.41.turns, ...), custom_call_target="tpu_custom_call" | custom-call | flops 1048576 | bytes 1048576 | tf_op jit(solution)/shard_map/finish_0/pallas_call | solution.py:541
  12.4 0.1 collective-permute-start.7
  12.5 1.6 %collective-permute-start.8 = (f32[2,24,256]{2,1,0:T(8,128)S(1)}, f32[2,24,256]{2,1,0:T(8,128)S(1)}, u32[]{:S(2)}, u32[]{:S(2)}) collective-permute-start(f32[2,24,256]{2,1,0:T(8,128)S(1)} %get-tuple-element.74), channel_id=1, source_target_pairs={{0,8},{1,2},{2,1},{3,4},{4,3},{5,6},{6,5},{7,15},{8,0},{9,10},{10,... | collective-permute-start | bytes 147464 | tf_op jit(solution)/shard_map/ppermute | solution.py:60
  14.1 0.5 %collective-permute-start.9 = (f32[24,256]{1,0:T(8,128)S(1)}, f32[24,256]{1,0:T(8,128)S(1)}, u32[]{:S(2)}, u32[]{:S(2)}) collective-permute-start(f32[24,256]{1,0:T(8,128)S(1)} %get-tuple-element.75), channel_id=1, source_target_pairs={{0,8},{1,9},{2,10},{3,11},{4,5},{5,4},{6,7},{7,6},{8,0},{9,1},{10,... | collective-permute-start | bytes 73736 | tf_op jit(solution)/shard_map/ppermute | solution.py:60
  14.5 1.2 %collective-permute-start.10 = (f32[24,256]{1,0:T(8,128)S(1)}, f32[24,256]{1,0:T(8,128)S(1)}, u32[]{:S(2)}, u32[]{:S(2)}) collective-permute-start(f32[24,256]{1,0:T(8,128)S(1)} %get-tuple-element.76), channel_id=1, source_target_pairs={{0,1},{1,0},{2,3},{3,2},{4,12},{5,13},{6,14},{7,15},{8,16},{9,17},... | collective-permute-start | bytes 73736 | tf_op jit(solution)/shard_map/ppermute | solution.py:60
  15.8 0.8 %inner_1.1.partial = f32[2,384,128]{2,1,0:T(8,128)S(1)} custom-call(f32[2,384,128]{2,1,0:T(8,128)S(1)} %get-tuple-element.60.partial.state, f32[2,24,256]{2,1,0:T(8,128)S(1)} %get-tuple-element.70.ghosts, f32[4,24,128]{2,1,0:T(8,128)S(1)} %get-tuple-element.42.scale), custom_call_target="tpu_custom_call" | custom-call | flops 4194304 | bytes 2097152 | tf_op jit(solution)/shard_map/inner_1/pallas_call | solution.py:541
  16.6 0.0 collective-permute-done.7.flat_a
  16.6 0.0 collective-permute-done.8.flat_b
  16.6 0.4 %sides_1.1.partial = f32[4,6,16,256]{3,2,1,0:T(8,128)S(1)} custom-call(f32[4,24,128]{2,1,0:T(8,128)S(1)} %get-tuple-element.42.scale, f32[2,48,192]{2,1,0:T(8,128)S(1)} %get-tuple-element.43.select, f32[2,384,128]{2,1,0:T(8,128)S(1)} %inner_1.1.partial, f32[3,24,256]{2,1,0:T(8,128)S(1)} %get-tuple-element.71.low, f32[3,24,256]{2,1,0:T(8,128)S(1)} %get-tuple-element.72.high, ...), custom_call_target="tpu_custom_call" | custom-call | flops 1048576 | bytes 1048576 | tf_op jit(solution)/shard_map/sides_1/pallas_call | solution.py:541
  17.0 0.9 %collective-permute-done.9.deep_first = f32[24,256]{1,0:T(8,128)S(1)} collective-permute-done((f32[24,256]{1,0:T(8,128)S(1)}, f32[24,256]{1,0:T(8,128)S(1)}, u32[]{:S(2)}, u32[]{:S(2)}) %collective-permute-start.9) | collective-permute-done | bytes 24608 | tf_op jit(solution)/shard_map/ppermute | solution.py:60
  17.9 0.0 collective-permute-done.10.deep_second
  17.9 1.0 %finish_1.1 = f32[4,6,16,256]{3,2,1,0:T(8,128)} custom-call(f32[2,8,24,128]{3,2,1,0:T(8,128)S(1)} %get-tuple-element.41.turns, f32[4,6,16,256]{3,2,1,0:T(8,128)S(1)} %sides_1.1.partial, f32[3,24,256]{2,1,0:T(8,128)S(1)} %get-tuple-element.71.low, f32[3,24,256]{2,1,0:T(8,128)S(1)} %get-tuple-element.72.high, f32[24,256]{1,0:T(8,128)S(1)} %collective-permute-done.9.deep_first, ...), custom_call_target="tpu_custom_call" | custom-call | tf_op jit(solution)/shard_map/finish_1/pallas_call | solution.py:628
  (3 shorter events, 0.0 us)
Async XLA Ops:
  1.4 5.1 %collective-permute-start.2 = (f32[40,256]{1,0:T(8,128)S(1)}, f32[40,256]{1,0:T(8,128)S(1)}, u32[]{:S(2)}, u32[]{:S(2)}) collective-permute-start(f32[40,256]{1,0:T(8,128)S(1)} %get-tuple-element.53), channel_id=1, source_target_pairs={{0,8},{1,9},{2,10},{3,11},{4,12},{5,13},{6,14},{7,15},{8,0},{9,1},... | collective-permute-start | bytes 122888 | tf_op jit(solution)/shard_map/ppermute | solution.py:60
  4.5 2.0 %collective-permute-start.3 = (f32[40,256]{1,0:T(8,128)S(1)}, f32[40,256]{1,0:T(8,128)S(1)}, u32[]{:S(2)}, u32[]{:S(2)}) collective-permute-start(f32[40,256]{1,0:T(8,128)S(1)} %get-tuple-element.54), channel_id=1, source_target_pairs={{0,1},{1,0},{2,3},{3,2},{4,5},{5,4},{6,7},{7,6},{8,9},{9,8},{10,11... | collective-permute-start | bytes 122888 | tf_op jit(solution)/shard_map/ppermute | solution.py:60
  5.2 5.8 %collective-permute-start.1 = (f32[120,256]{1,0:T(8,128)S(1)}, f32[120,256]{1,0:T(8,128)S(1)}, u32[]{:S(2)}, u32[]{:S(2)}) collective-permute-start(f32[120,256]{1,0:T(8,128)S(1)} %get-tuple-element.52), channel_id=1, source_target_pairs={{0,8},{1,9},{2,10},{3,11},{4,12},{5,13},{6,14},{7,15},{8,0},{9,1},... | collective-permute-start | bytes 368648 | tf_op jit(solution)/shard_map/ppermute | solution.py:60
  5.3 3.4 %collective-permute-start = (f32[96,256]{1,0:T(8,128)S(1)}, f32[96,256]{1,0:T(8,128)S(1)}, u32[]{:S(2)}, u32[]{:S(2)}) collective-permute-start(f32[96,256]{1,0:T(8,128)S(1)} %get-tuple-element.51), channel_id=1, source_target_pairs={{0,1},{1,0},{2,3},{3,2},{4,5},{5,4},{6,7},{7,6},{8,9},{9,8},{10,11... | collective-permute-start | bytes 294920 | tf_op jit(solution)/shard_map/ppermute | solution.py:60
  6.6 5.0 %collective-permute-start.4 = (f32[3,24,256]{2,1,0:T(8,128)S(1)}, f32[3,24,256]{2,1,0:T(8,128)S(1)}, u32[]{:S(2)}, u32[]{:S(2)}) collective-permute-start(f32[3,24,256]{2,1,0:T(8,128)S(1)} %get-tuple-element.58), channel_id=1, source_target_pairs={{0,1},{1,0},{2,3},{3,2},{4,5},{5,4},{6,7},{7,6},{8,9},{9,8},{10,11... | collective-permute-start | bytes 221192 | tf_op jit(solution)/shard_map/ppermute | solution.py:60
  6.7 4.9 %collective-permute-start.5 = (f32[2,24,256]{2,1,0:T(8,128)S(1)}, f32[2,24,256]{2,1,0:T(8,128)S(1)}, u32[]{:S(2)}, u32[]{:S(2)}) collective-permute-start(f32[2,24,256]{2,1,0:T(8,128)S(1)} %get-tuple-element.59), channel_id=1, source_target_pairs={{0,8},{1,2},{2,1},{3,4},{4,3},{5,6},{6,5},{7,15},{8,0},{9,10},{10,... | collective-permute-start | bytes 147464 | tf_op jit(solution)/shard_map/ppermute | solution.py:60
  8.7 3.4 %collective-permute-start.6 = (f32[24,256]{1,0:T(8,128)S(1)}, f32[24,256]{1,0:T(8,128)S(1)}, u32[]{:S(2)}, u32[]{:S(2)}) collective-permute-start(f32[24,256]{1,0:T(8,128)S(1)} %get-tuple-element.66), channel_id=1, source_target_pairs={{0,1},{1,0},{2,3},{3,2},{4,5},{5,4},{6,7},{7,6},{8,16},{9,17},{10,... | collective-permute-start | bytes 73736 | tf_op jit(solution)/shard_map/ppermute | solution.py:60
  12.4 4.2 %collective-permute-start.7 = (f32[2,24,256]{2,1,0:T(8,128)S(1)}, f32[2,24,256]{2,1,0:T(8,128)S(1)}, u32[]{:S(2)}, u32[]{:S(2)}) collective-permute-start(f32[2,24,256]{2,1,0:T(8,128)S(1)} %get-tuple-element.73), channel_id=1, source_target_pairs={{0,1},{1,0},{2,3},{3,2},{4,5},{5,4},{6,7},{7,6},{8,9},{9,8},{10,11... | collective-permute-start | bytes 147464 | tf_op jit(solution)/shard_map/ppermute | solution.py:60
  12.5 4.2 %collective-permute-start.8 = (f32[2,24,256]{2,1,0:T(8,128)S(1)}, f32[2,24,256]{2,1,0:T(8,128)S(1)}, u32[]{:S(2)}, u32[]{:S(2)}) collective-permute-start(f32[2,24,256]{2,1,0:T(8,128)S(1)} %get-tuple-element.74), channel_id=1, source_target_pairs={{0,8},{1,2},{2,1},{3,4},{4,3},{5,6},{6,5},{7,15},{8,0},{9,10},{10,... | collective-permute-start | bytes 147464 | tf_op jit(solution)/shard_map/ppermute | solution.py:60
  14.1 3.8 %collective-permute-start.9 = (f32[24,256]{1,0:T(8,128)S(1)}, f32[24,256]{1,0:T(8,128)S(1)}, u32[]{:S(2)}, u32[]{:S(2)}) collective-permute-start(f32[24,256]{1,0:T(8,128)S(1)} %get-tuple-element.75), channel_id=1, source_target_pairs={{0,8},{1,9},{2,10},{3,11},{4,5},{5,4},{6,7},{7,6},{8,0},{9,1},{10,... | collective-permute-start | bytes 73736 | tf_op jit(solution)/shard_map/ppermute | solution.py:60
  14.5 3.3 %collective-permute-start.10 = (f32[24,256]{1,0:T(8,128)S(1)}, f32[24,256]{1,0:T(8,128)S(1)}, u32[]{:S(2)}, u32[]{:S(2)}) collective-permute-start(f32[24,256]{1,0:T(8,128)S(1)} %get-tuple-element.76), channel_id=1, source_target_pairs={{0,1},{1,0},{2,3},{3,2},{4,12},{5,13},{6,14},{7,15},{8,16},{9,17},... | collective-permute-start | bytes 73736 | tf_op jit(solution)/shard_map/ppermute | solution.py:60

commit v9 on v6

--- a/solution.py
+++ b/solution.py
@@ -29,7 +29,7 @@
 SOURCES = 4
 PARTS = 2
 SELECT = (2, 2 * ROWS, PARTS * SOURCES * ROWS)
-PIECE = 3
+PIECE = 2
 TURNS = (2, 2 * SLOTS, ROWS, HALF)
 
 

time: 19.1 us -> 19.2 us (level)
  no operation moved by 1% of the time
where the time goes in v9:
time: 19.2 us; the launch traced here: 18.9 us
  starting transfers between devices  9.24 us (48%)
  Pallas kernels  5.06 us (26%)
  waiting for transfers between devices  3.15 us (16%)
  between operations  1.44 us (8%)
    ppermute x11, starting transfers between devices, exchange(): return lax.ppermute(block, ('grp', 'dev'), partners(axis, offset))  9.24 us
    ppermute x11, waiting for transfers between devices, exchange(): return lax.ppermute(block, ('grp', 'dev'), partners(axis, offset))  3.15 us
    pallas_call x7, Pallas kernels, call(): pl.pallas_call(kernel, name=name, compiler_params=SMALL, out_shape=[shape...  2.66 us
    pallas_call x1, Pallas kernels, start(): pl.pallas_call(start_kernel, name='start', compiler_params=SMALL, out_sha...  1.38 us
    pallas_call x1, Pallas kernels, body(): pl.pallas_call(last_kernel, name='finish_1', compiler_params=SMALL, out_s...  1.02 us
  transfers between devices with their start and end apart: 11, of which 2 were waited for; matrix products, arithmetic and copies ran while one was open for 0% of the time, Pallas kernels for 13%

profile of v9, /device:TPU:0, one launch (start us, length us, event | category | flops | bytes accessed | tf_op | source)
XLA Modules:
  0.0 18.9 jit_solution(17451501487286409571)
XLA Ops:
  0.0 1.4 %start.1 = (f32[4,6,16,256]{3,2,1,0:T(8,128)S(1)}, f32[3,24,256]{2,1,0:T(8,128)S(1)}, f32[3,24,256]{2,1,0:T(8,128)S(1)}, f32[40,256]{1,0:T(8,128)S(1)}, f32[40,2...) custom-call(f32[4,6,16,256]{3,2,1,0:T(8,128)} %fields.1, ...), custom_call_target="tpu_custom_call" | custom-call | tf_op jit(solution)/shard_map/start/pallas_call | solution.py:551
  1.4 3.1 %collective-permute-start.2 = (f32[40,256]{1,0:T(8,128)S(1)}, f32[40,256]{1,0:T(8,128)S(1)}, u32[]{:S(2)}, u32[]{:S(2)}) collective-permute-start(f32[40,256]{1,0:T(8,128)S(1)} %get-tuple-element.53), channel_id=1, source_target_pairs={{0,8},{1,9},{2,10},{3,11},{4,12},{5,13},{6,14},{7,15},{8,0},{9,1},... | collective-permute-start | bytes 122888 | tf_op jit(solution)/shard_map/ppermute | solution.py:60
  4.5 0.0 collective-permute-start.3
  5.2 0.1 collective-permute-start.1
  5.3 0.5 %collective-permute-start = (f32[96,256]{1,0:T(8,128)S(1)}, f32[96,256]{1,0:T(8,128)S(1)}, u32[]{:S(2)}, u32[]{:S(2)}) collective-permute-start(f32[96,256]{1,0:T(8,128)S(1)} %get-tuple-element.51), channel_id=1, source_target_pairs={{0,1},{1,0},{2,3},{3,2},{4,5},{5,4},{6,7},{7,6},{8,9},{9,8},{10,11... | collective-permute-start | bytes 294920 | tf_op jit(solution)/shard_map/ppermute | solution.py:60
  6.5 0.0 collective-permute-done.2.faces
  6.5 0.0 collective-permute-done.3.faces_dev
  6.5 0.1 faces.1
  6.6 0.1 collective-permute-start.4
  6.7 2.0 %collective-permute-start.5 = (f32[2,24,256]{2,1,0:T(8,128)S(1)}, f32[2,24,256]{2,1,0:T(8,128)S(1)}, u32[]{:S(2)}, u32[]{:S(2)}) collective-permute-start(f32[2,24,256]{2,1,0:T(8,128)S(1)} %get-tuple-element.59), channel_id=1, source_target_pairs={{0,8},{1,2},{2,1},{3,4},{4,3},{5,6},{6,5},{7,15},{8,0},{9,10},{10,... | collective-permute-start | bytes 147464 | tf_op jit(solution)/shard_map/ppermute | solution.py:60
  8.7 0.0 collective-permute-start.6
  8.7 0.0 collective-permute-done.block_dev
  8.7 2.3 %collective-permute-done.1.block_grp = f32[120,256]{1,0:T(8,128)S(1)} collective-permute-done((f32[120,256]{1,0:T(8,128)S(1)}, f32[120,256]{1,0:T(8,128)S(1)}, u32[]{:S(2)}, u32[]{:S(2)}) %collective-permute-start.1) | collective-permute-done | bytes 122912 | tf_op jit(solution)/shard_map/ppermute | solution.py:60
  11.0 0.5 %inner_0.1 = (f32[2,384,128]{2,1,0:T(8,128)S(1)}, f32[24,256]{1,0:T(8,128)S(1)}, f32[24,256]{1,0:T(8,128)S(1)}, f32[24,256]{1,0:T(8,128)S(1)}, f32[24,256]{1,0:T(8,128)S(1)}) custom-call(f32[24,256]{1,0:T(8,128)S(1)} %broadcast_in_dim.21.mask_dev, f32[24,256]{1,0:T(8,128)S(1)} %broadcast_in_dim.23.mask_grp, f32[4,24,128]{2,1,0:T(8,128)S(1)} %get-tuple-element.42.scale, ...), custom_call_target="tpu_custom_call" | custom-call | flops 4194304 | bytes 2097152 | tf_op jit(solution)/shard_map/inner_0/pallas_call | solution.py:537
  11.5 0.0 collective-permute-done.5.flat_b
  11.5 0.0 collective-permute-done.4.flat_a.refs_6_
  11.5 0.6 %sides_0.1 = (f32[2,384,128]{2,1,0:T(8,128)S(1)}, f32[24,256]{1,0:T(8,128)S(1)}, f32[24,256]{1,0:T(8,128)S(1)}, f32[24,256]{1,0:T(8,128)S(1)}, f32[24,256]{1,0:T(8,128)S(1)}) custom-call(f32[4,24,128]{2,1,0:T(8,128)S(1)} %get-tuple-element.42.scale, f32[2,48,192]{2,1,0:T(8,128)S(1)} %get-tuple-element.43.select, ...), custom_call_target="tpu_custom_call" | custom-call | flops 1048576 | bytes 1048576 | tf_op jit(solution)/shard_map/sides_0/pallas_call | solution.py:537
  12.1 0.0 collective-permute-done.6.refs_5_
  12.1 0.3 %finish_0.1 = (f32[3,24,256]{2,1,0:T(8,128)S(1)}, f32[3,24,256]{2,1,0:T(8,128)S(1)}, f32[2,24,256]{2,1,0:T(8,128)S(1)}, f32[2,24,256]{2,1,0:T(8,128)S(1)}, f32[2...) custom-call(f32[2,8,24,128]{3,2,1,0:T(8,128)S(1)} %get-tuple-element.41.turns, ...), custom_call_target="tpu_custom_call" | custom-call | flops 1048576 | bytes 1048576 | tf_op jit(solution)/shard_map/finish_0/pallas_call | solution.py:537
  12.4 0.1 collective-permute-start.7
  12.5 1.6 %collective-permute-start.8 = (f32[2,24,256]{2,1,0:T(8,128)S(1)}, f32[2,24,256]{2,1,0:T(8,128)S(1)}, u32[]{:S(2)}, u32[]{:S(2)}) collective-permute-start(f32[2,24,256]{2,1,0:T(8,128)S(1)} %get-tuple-element.74), channel_id=1, source_target_pairs={{0,8},{1,2},{2,1},{3,4},{4,3},{5,6},{6,5},{7,15},{8,0},{9,10},{10,... | collective-permute-start | bytes 147464 | tf_op jit(solution)/shard_map/ppermute | solution.py:60
  14.1 0.5 %collective-permute-start.9 = (f32[24,256]{1,0:T(8,128)S(1)}, f32[24,256]{1,0:T(8,128)S(1)}, u32[]{:S(2)}, u32[]{:S(2)}) collective-permute-start(f32[24,256]{1,0:T(8,128)S(1)} %get-tuple-element.75), channel_id=1, source_target_pairs={{0,8},{1,9},{2,10},{3,11},{4,5},{5,4},{6,7},{7,6},{8,0},{9,1},{10,... | collective-permute-start | bytes 73736 | tf_op jit(solution)/shard_map/ppermute | solution.py:60
  14.6 1.2 %collective-permute-start.10 = (f32[24,256]{1,0:T(8,128)S(1)}, f32[24,256]{1,0:T(8,128)S(1)}, u32[]{:S(2)}, u32[]{:S(2)}) collective-permute-start(f32[24,256]{1,0:T(8,128)S(1)} %get-tuple-element.76), channel_id=1, source_target_pairs={{0,1},{1,0},{2,3},{3,2},{4,12},{5,13},{6,14},{7,15},{8,16},{9,17},... | collective-permute-start | bytes 73736 | tf_op jit(solution)/shard_map/ppermute | solution.py:60
  15.8 0.8 %inner_1.1.partial = f32[2,384,128]{2,1,0:T(8,128)S(1)} custom-call(f32[2,384,128]{2,1,0:T(8,128)S(1)} %get-tuple-element.60.partial.state, f32[2,24,256]{2,1,0:T(8,128)S(1)} %get-tuple-element.70.ghosts, f32[4,24,128]{2,1,0:T(8,128)S(1)} %get-tuple-element.42.scale), custom_call_target="tpu_custom_call" | custom-call | flops 4194304 | bytes 2097152 | tf_op jit(solution)/shard_map/inner_1/pallas_call | solution.py:537
  16.6 0.0 collective-permute-done.7.flat_a
  16.6 0.0 collective-permute-done.8.flat_b
  16.6 0.4 %sides_1.1.partial = f32[4,6,16,256]{3,2,1,0:T(8,128)S(1)} custom-call(f32[4,24,128]{2,1,0:T(8,128)S(1)} %get-tuple-element.42.scale, f32[2,48,192]{2,1,0:T(8,128)S(1)} %get-tuple-element.43.select, f32[2,384,128]{2,1,0:T(8,128)S(1)} %inner_1.1.partial, f32[3,24,256]{2,1,0:T(8,128)S(1)} %get-tuple-element.71.low, f32[3,24,256]{2,1,0:T(8,128)S(1)} %get-tuple-element.72.high, ...), custom_call_target="tpu_custom_call" | custom-call | flops 1048576 | bytes 1048576 | tf_op jit(solution)/shard_map/sides_1/pallas_call | solution.py:537
  17.0 0.9 %collective-permute-done.9.deep_first = f32[24,256]{1,0:T(8,128)S(1)} collective-permute-done((f32[24,256]{1,0:T(8,128)S(1)}, f32[24,256]{1,0:T(8,128)S(1)}, u32[]{:S(2)}, u32[]{:S(2)}) %collective-permute-start.9) | collective-permute-done | bytes 24608 | tf_op jit(solution)/shard_map/ppermute | solution.py:60
  17.9 0.0 collective-permute-done.10.deep_second
  17.9 1.0 %finish_1.1 = f32[4,6,16,256]{3,2,1,0:T(8,128)} custom-call(f32[2,8,24,128]{3,2,1,0:T(8,128)S(1)} %get-tuple-element.41.turns, f32[4,6,16,256]{3,2,1,0:T(8,128)S(1)} %sides_1.1.partial, f32[3,24,256]{2,1,0:T(8,128)S(1)} %get-tuple-element.71.low, f32[3,24,256]{2,1,0:T(8,128)S(1)} %get-tuple-element.72.high, f32[24,256]{1,0:T(8,128)S(1)} %collective-permute-done.9.deep_first, ...), custom_call_target="tpu_custom_call" | custom-call | tf_op jit(solution)/shard_map/finish_1/pallas_call | solution.py:624
  (3 shorter events, 0.0 us)
Async XLA Ops:
  1.4 5.1 %collective-permute-start.2 = (f32[40,256]{1,0:T(8,128)S(1)}, f32[40,256]{1,0:T(8,128)S(1)}, u32[]{:S(2)}, u32[]{:S(2)}) collective-permute-start(f32[40,256]{1,0:T(8,128)S(1)} %get-tuple-element.53), channel_id=1, source_target_pairs={{0,8},{1,9},{2,10},{3,11},{4,12},{5,13},{6,14},{7,15},{8,0},{9,1},... | collective-permute-start | bytes 122888 | tf_op jit(solution)/shard_map/ppermute | solution.py:60
  4.5 2.0 %collective-permute-start.3 = (f32[40,256]{1,0:T(8,128)S(1)}, f32[40,256]{1,0:T(8,128)S(1)}, u32[]{:S(2)}, u32[]{:S(2)}) collective-permute-start(f32[40,256]{1,0:T(8,128)S(1)} %get-tuple-element.54), channel_id=1, source_target_pairs={{0,1},{1,0},{2,3},{3,2},{4,5},{5,4},{6,7},{7,6},{8,9},{9,8},{10,11... | collective-permute-start | bytes 122888 | tf_op jit(solution)/shard_map/ppermute | solution.py:60
  5.2 5.8 %collective-permute-start.1 = (f32[120,256]{1,0:T(8,128)S(1)}, f32[120,256]{1,0:T(8,128)S(1)}, u32[]{:S(2)}, u32[]{:S(2)}) collective-permute-start(f32[120,256]{1,0:T(8,128)S(1)} %get-tuple-element.52), channel_id=1, source_target_pairs={{0,8},{1,9},{2,10},{3,11},{4,12},{5,13},{6,14},{7,15},{8,0},{9,1},... | collective-permute-start | bytes 368648 | tf_op jit(solution)/shard_map/ppermute | solution.py:60
  5.3 3.4 %collective-permute-start = (f32[96,256]{1,0:T(8,128)S(1)}, f32[96,256]{1,0:T(8,128)S(1)}, u32[]{:S(2)}, u32[]{:S(2)}) collective-permute-start(f32[96,256]{1,0:T(8,128)S(1)} %get-tuple-element.51), channel_id=1, source_target_pairs={{0,1},{1,0},{2,3},{3,2},{4,5},{5,4},{6,7},{7,6},{8,9},{9,8},{10,11... | collective-permute-start | bytes 294920 | tf_op jit(solution)/shard_map/ppermute | solution.py:60
  6.6 5.0 %collective-permute-start.4 = (f32[3,24,256]{2,1,0:T(8,128)S(1)}, f32[3,24,256]{2,1,0:T(8,128)S(1)}, u32[]{:S(2)}, u32[]{:S(2)}) collective-permute-start(f32[3,24,256]{2,1,0:T(8,128)S(1)} %get-tuple-element.58), channel_id=1, source_target_pairs={{0,1},{1,0},{2,3},{3,2},{4,5},{5,4},{6,7},{7,6},{8,9},{9,8},{10,11... | collective-permute-start | bytes 221192 | tf_op jit(solution)/shard_map/ppermute | solution.py:60
  6.7 4.9 %collective-permute-start.5 = (f32[2,24,256]{2,1,0:T(8,128)S(1)}, f32[2,24,256]{2,1,0:T(8,128)S(1)}, u32[]{:S(2)}, u32[]{:S(2)}) collective-permute-start(f32[2,24,256]{2,1,0:T(8,128)S(1)} %get-tuple-element.59), channel_id=1, source_target_pairs={{0,8},{1,2},{2,1},{3,4},{4,3},{5,6},{6,5},{7,15},{8,0},{9,10},{10,... | collective-permute-start | bytes 147464 | tf_op jit(solution)/shard_map/ppermute | solution.py:60
  8.7 3.4 %collective-permute-start.6 = (f32[24,256]{1,0:T(8,128)S(1)}, f32[24,256]{1,0:T(8,128)S(1)}, u32[]{:S(2)}, u32[]{:S(2)}) collective-permute-start(f32[24,256]{1,0:T(8,128)S(1)} %get-tuple-element.66), channel_id=1, source_target_pairs={{0,1},{1,0},{2,3},{3,2},{4,5},{5,4},{6,7},{7,6},{8,16},{9,17},{10,... | collective-permute-start | bytes 73736 | tf_op jit(solution)/shard_map/ppermute | solution.py:60
  12.4 4.2 %collective-permute-start.7 = (f32[2,24,256]{2,1,0:T(8,128)S(1)}, f32[2,24,256]{2,1,0:T(8,128)S(1)}, u32[]{:S(2)}, u32[]{:S(2)}) collective-permute-start(f32[2,24,256]{2,1,0:T(8,128)S(1)} %get-tuple-element.73), channel_id=1, source_target_pairs={{0,1},{1,0},{2,3},{3,2},{4,5},{5,4},{6,7},{7,6},{8,9},{9,8},{10,11... | collective-permute-start | bytes 147464 | tf_op jit(solution)/shard_map/ppermute | solution.py:60
  12.5 4.2 %collective-permute-start.8 = (f32[2,24,256]{2,1,0:T(8,128)S(1)}, f32[2,24,256]{2,1,0:T(8,128)S(1)}, u32[]{:S(2)}, u32[]{:S(2)}) collective-permute-start(f32[2,24,256]{2,1,0:T(8,128)S(1)} %get-tuple-element.74), channel_id=1, source_target_pairs={{0,8},{1,2},{2,1},{3,4},{4,3},{5,6},{6,5},{7,15},{8,0},{9,10},{10,... | collective-permute-start | bytes 147464 | tf_op jit(solution)/shard_map/ppermute | solution.py:60
  14.1 3.8 %collective-permute-start.9 = (f32[24,256]{1,0:T(8,128)S(1)}, f32[24,256]{1,0:T(8,128)S(1)}, u32[]{:S(2)}, u32[]{:S(2)}) collective-permute-start(f32[24,256]{1,0:T(8,128)S(1)} %get-tuple-element.75), channel_id=1, source_target_pairs={{0,8},{1,9},{2,10},{3,11},{4,5},{5,4},{6,7},{7,6},{8,0},{9,1},{10,... | collective-permute-start | bytes 73736 | tf_op jit(solution)/shard_map/ppermute | solution.py:60
  14.6 3.3 %collective-permute-start.10 = (f32[24,256]{1,0:T(8,128)S(1)}, f32[24,256]{1,0:T(8,128)S(1)}, u32[]{:S(2)}, u32[]{:S(2)}) collective-permute-start(f32[24,256]{1,0:T(8,128)S(1)} %get-tuple-element.76), channel_id=1, source_target_pairs={{0,1},{1,0},{2,3},{3,2},{4,12},{5,13},{6,14},{7,15},{8,16},{9,17},... | collective-permute-start | bytes 73736 | tf_op jit(solution)/shard_map/ppermute | solution.py:60
